TPU v7x, 32 devices: a whole 2x2x4 slice. The times are simulated.
32 devices in a mesh: groups: 2 (over y), gx: 4 (over z), gy: 2 (over x), gz: 2 (over core).
Axes of the slice: x: 2, y: 2, z: 4, core: 2. Of those that a mesh axis runs over, the one named last changes fastest.
Arguments:
- tokens: bfloat16 [128, 18432], P(('groups', 'gy', 'gz'), 'gx'), parts along dimension 0, may hold values from -6 to 6
- q_weight: bfloat16 [18432, 6144], P('gx', ('gy', 'gz')), may hold values from -0.046875 to 0.046875
- o_weight: bfloat16 [6144, 18432], P(('gy', 'gz'), 'gx'), may hold values from -0.078125 to 0.078125
- key_cache: bfloat16 [128, 512, 256], P(('groups', 'gx', 'gy', 'gz')), parts along dimension 0, may hold values from -410 to 410
- value_cache: bfloat16 [128, 512, 256], P(('groups', 'gx', 'gy', 'gz')), parts along dimension 0, may hold values from -8 to 8
- lengths: int32 [128], P(('groups', 'gx', 'gy', 'gz')), parts along dimension 0, may hold values from 2 to 512, as said below
Outputs:
- output: bfloat16 [128, 18432], P(('groups', 'gy', 'gz'), 'gx'), parts along dimension 0
There are 2 independent parts, one for each index of `groups`. A program takes and returns all parts, laid end to end along the dimension named above; an argument that names none is the same for every part. Nothing has to cross between parts.
Inputs may be any that keep to these rules, and one draw needn't show every extreme that they name: `lengths`: one row uses all 512 positions.
All inputs are finite; a program needn't handle non-finite values.
Results may differ from a plain program's by a relative error of at most 0.025.
Values may be sent and summed in bfloat16 or wider, within the bound.
No kernel may reach another device: no remote copies, remote signals or barrier semaphores. Data moves between devices by JAX's collectives and lax.ppermute only.
A program may use at most 128 MiB of HBM per device.

v0:
```python
import jax
import jax.numpy as jnp
from jax import lax
from jax.sharding import PartitionSpec as P

HDIM = 256


def attend(queries, key_block, value_block, lengths_here):
    row_count = queries.shape[0]
    head_count = queries.shape[1] // HDIM
    cache_len = key_block.shape[1]
    query = queries.reshape(row_count, head_count, HDIM)
    scores = jnp.einsum(
        "rhd,rld->rhl", query, key_block, preferred_element_type=jnp.float32
    ) * HDIM ** (-0.5)
    positions = lax.broadcasted_iota(jnp.int32, (row_count, cache_len), 1)
    usable = positions < lengths_here[:, None]
    scores = jnp.where(usable[:, None, :], scores, -jnp.inf)
    largest = jnp.max(scores, axis=2, keepdims=True)
    raised = jnp.exp(scores - largest)
    totals = jnp.sum(raised, axis=2, keepdims=True)
    weights = (raised / totals).astype(jnp.bfloat16)
    mixed = jnp.einsum("rhl,rld->rhd", weights, value_block, preferred_element_type=jnp.float32)
    return mixed.astype(jnp.bfloat16).reshape(row_count, head_count * HDIM)


def shards(tokens, q_weight, o_weight, key_cache, value_cache, lengths):
    rows_here = lax.all_gather(tokens, ("gy", "gz"), axis=0, tiled=True)
    queries = lax.psum_scatter(
        jnp.dot(rows_here, q_weight, preferred_element_type=jnp.float32).astype(jnp.bfloat16),
        "gx",
        scatter_dimension=0,
        tiled=True,
    )
    spread = lax.all_to_all(queries, ("gy", "gz"), split_axis=0, concat_axis=1, tiled=True)
    attended = attend(spread, key_cache, value_cache, lengths)
    collected = lax.all_gather(attended, "gx", axis=0, tiled=True)
    swapped = lax.all_to_all(collected, ("gy", "gz"), split_axis=1, concat_axis=0, tiled=True)
    outer_count = lax.axis_size(("gy", "gz"))
    inner_count = lax.axis_size("gx")
    per_device = attended.shape[0]
    ordered = swapped.reshape(outer_count, inner_count, per_device, swapped.shape[1])
    ordered = ordered.transpose(1, 0, 2, 3).reshape(swapped.shape[0], swapped.shape[1])
    partial_out = jnp.dot(ordered, o_weight, preferred_element_type=jnp.float32)
    summed = lax.psum_scatter(
        partial_out.astype(jnp.bfloat16), ("gy", "gz"), scatter_dimension=0, tiled=True
    )
    return summed


def solution(mesh):
    return jax.shard_map(
        shards,
        mesh=mesh,
        in_specs=(
            P(("groups", "gy", "gz"), "gx"),
            P("gx", ("gy", "gz")),
            P(("gy", "gz"), "gx"),
            P(("groups", "gx", "gy", "gz"), None, None),
            P(("groups", "gx", "gy", "gz"), None, None),
            P(("groups", "gx", "gy", "gz")),
        ),
        out_specs=P(("groups", "gy", "gz"), "gx"),
        check_vma=False,
    )
```

profile of v0, /device:TPU:0, one launch (start us, length us, event | category | flops | bytes accessed | tf_op | source)
XLA Modules:
  0.0 111.1 jit_solution(3777390741052663656)
XLA Ops:
  6.5 0.0 copy-start
  6.5 0.0 copy-start.1
  6.5 0.0 copy-start.2
  6.5 0.0 reduce-scatter.3.cloned.1.call-start
  6.5 9.3 %all_gather.6 = bf16[64,4608]{1,0:T(8,128)(2,1)S(1)} all-gather(bf16[16,4608]{1,0:T(8,128)(2,1)} %param.6), channel_id=1, replica_groups=mesh['groups'=2,'gx'=4,'gy'=2,'gz'=2] {'gy','gz'}, dimensions={0}, use_global_device_ids=true | all-gather | bytes 737280 | tf_op jit(solution)/shard_map/all_gather | solution.py:29
  15.9 8.2 %convolution_convert_fusion.1 = bf16[64,1536]{1,0:T(8,128)(2,1)} fusion(bf16[64,4608]{1,0:T(8,128)(2,1)S(1)} %all_gather.6, bf16[4608,1536]{1,0:T(8,128)(2,1)} %param.7), kind=kOutput, calls=%fused_computation.2 | convolution fusion | flops 906067968 | bytes 14942208 | tf_op jit(solution)/shard_map/dot_general | solution.py:31
  24.1 0.0 reduce-scatter.3.cloned.1.call-update
  24.1 20.4 %reduce-scatter.3.cloned.1.call-done = bf16[16,1536]{1,0:T(8,128)(2,1)} async-done(((bf16[64,1536]{1,0:T(8,128)(2,1)}), bf16[16,1536]{1,0:T(8,128)(2,1)}) %reduce-scatter.3.cloned.1.call-update) | async-done | bytes 49168 | tf_op jit(solution)/shard_map/reduce_scatter | solution.py:30
  44.6 1.4 %all_to_all.24 = bf16[4,4,1536]{2,1,0:T(4,128)(2,1)} reshape(bf16[16,1536]{1,0:T(8,128)(2,1)} %reduce-scatter.3.cloned.1.call-done) | data formatting | bytes 98304 | tf_op jit(solution)/shard_map/all_to_all | solution.py:36
  46.0 3.3 %all-to-all-start = ((bf16[4,4,1536]{2,1,0:T(4,128)(2,1)}), bf16[4,4,1536]{2,1,0:T(4,128)(2,1)S(1)}, u32[]{:S(2)}, u32[]{:S(2)}) async-start(bf16[4,4,1536]{2,1,0:T(4,128)(2,1)} %all_to_all.24), calls=%async_computation.1 | async-start | bytes 98304 | tf_op jit(solution)/shard_map/all_to_all | solution.py:36
  49.3 0.0 reduce-scatter.5.cloned.1.call-start
  49.3 0.0 copy-done.1
  49.3 0.1 iota_compare_fusion
  49.4 3.9 %all-to-all-done = bf16[4,4,1536]{2,1,0:T(4,128)(2,1)S(1)} async-done(((bf16[4,4,1536]{2,1,0:T(4,128)(2,1)}), bf16[4,4,1536]{2,1,0:T(4,128)(2,1)S(1)}, u32[]{:S(2)}, u32[]{:S(2)}) %all-to-all-start) | async-done | bytes 49184 | tf_op jit(solution)/shard_map/all_to_all | solution.py:36
  53.3 0.0 copy-done
  53.3 0.4 fusion.3
  53.7 0.2 fusion.6
  53.9 0.0 copy-done.2
  53.9 0.3 convolution_convert_fusion.2
  54.3 14.0 %all-gather = bf16[4,4,6144]{2,1,0:T(4,128)(2,1)S(1)} all-gather(bf16[1,4,6144]{2,1,0:T(4,128)(2,1)S(1)} %reshape.41), channel_id=1, replica_groups=mesh['groups'=2,'gx'=4,'gy'=2,'gz'=2] {'gx'}, dimensions={0}, use_global_device_ids=true | all-gather | bytes 245760 | tf_op jit(solution)/shard_map/all_gather | solution.py:38
  68.3 0.1 all_to_all.27
  68.5 7.7 %all_to_all.32 = bf16[16,4,1536]{2,0,1:T(8,128)(2,1)S(1)} all-to-all(bf16[16,4,1536]{2,0,1:T(8,128)(2,1)S(1)} %copy.12), channel_id=1, replica_groups=mesh['groups'=2,'gx'=4,'gy'=2,'gz'=2] {'gy','gz'}, dimensions={1} | all-to-all | bytes 393216 | tf_op jit(solution)/shard_map/all_to_all | solution.py:39
  76.2 0.2 copy.13
  76.4 0.1 copy.14
  76.5 0.1 reshape.40
  76.5 8.4 %convolution_convert_fusion = bf16[64,4608]{1,0:T(8,128)(2,1)} fusion(bf16[64,1536]{1,0:T(8,128)(2,1)S(1)} %reshape.40, bf16[1536,4608]{1,0:T(8,128)(2,1)} %param.8), kind=kOutput, calls=%fused_computation.1 | convolution fusion | flops 906264576 | bytes 14942208 | tf_op jit(solution)/shard_map/dot_general | solution.py:45
  84.9 0.0 reduce-scatter.5.cloned.1.call-update
  84.9 19.4 %reduce-scatter.5.cloned.1.call-done = bf16[16,4608]{1,0:T(8,128)(2,1)} async-done(((bf16[64,4608]{1,0:T(8,128)(2,1)}), bf16[16,4608]{1,0:T(8,128)(2,1)}) %reduce-scatter.5.cloned.1.call-update) | async-done | bytes 147472 | tf_op jit(solution)/shard_map/reduce_scatter | solution.py:46
  (4 shorter events, 0.1 us)
Async XLA Ops:
  6.5 46.8 %copy-start = (bf16[4,512,256]{2,1,0:T(8,128)(2,1)S(1)}, bf16[4,512,256]{2,1,0:T(8,128)(2,1)}, u32[]{:S(2)}) copy-start(bf16[4,512,256]{2,1,0:T(8,128)(2,1)} %param.9) | copy-start | bytes 3145732
  6.5 42.8 %copy-start.1 = (s32[4]{0:T(128)S(1)}, s32[4]{0:T(128)}, u32[]{:S(2)}) copy-start(s32[4]{0:T(128)} %param.11) | copy-start | bytes 52
  6.5 47.4 %copy-start.2 = (bf16[4,512,256]{2,1,0:T(8,128)(2,1)S(1)}, bf16[4,512,256]{2,1,0:T(8,128)(2,1)}, u32[]{:S(2)}) copy-start(bf16[4,512,256]{2,1,0:T(8,128)(2,1)} %param.10) | copy-start | bytes 3145732
  6.5 38.0 %reduce-scatter.3.cloned.1.call-start = ((), (), s32[]{:S(2)}) async-start(), calls=%async_computation.4 | async-start | bytes 245760 | tf_op jit(solution)/shard_map/reduce_scatter | solution.py:30
  46.0 7.3 %all-to-all-start = ((bf16[4,4,1536]{2,1,0:T(4,128)(2,1)}), bf16[4,4,1536]{2,1,0:T(4,128)(2,1)S(1)}, u32[]{:S(2)}, u32[]{:S(2)}) async-start(bf16[4,4,1536]{2,1,0:T(4,128)(2,1)} %all_to_all.24), calls=%async_computation.1 | async-start | bytes 98304 | tf_op jit(solution)/shard_map/all_to_all | solution.py:36
  49.3 55.0 %reduce-scatter.5.cloned.1.call-start = ((), (), s32[]{:S(2)}) async-start(), calls=%async_computation.5 | async-start | bytes 737280 | tf_op jit(solution)/shard_map/reduce_scatter | solution.py:46
Sparse Core Ops, SparseCore 0:
  24.3 20.2 reduce-scatter.2
  85.0 19.2 reduce-scatter.4
where the time goes:
time: 112 us; the launch traced here: 111 us
  waiting for transfers between devices  43.7 us (39%)
  blocking collectives  31 us (28%)
  matrix products  17.3 us (15%)
  between operations  13.5 us (12%)
  starting transfers between devices  3.32 us (3%)
  local copies, waits for them, and re-layouts  1.98 us (2%)
    reduce_scatter x1, waiting for transfers between devices, shards(): lax.psum_scatter(jnp.dot(rows_here, q_weight, preferred_element_type=jnp....  20.4 us
    reduce_scatter x1, waiting for transfers between devices, shards(): lax.psum_scatter(partial_out.astype(jnp.bfloat16), ('gy', 'gz'), scatter_...  19.4 us
    all_gather x1, blocking collectives, shards(): collected = lax.all_gather(attended, 'gx', axis=0, tiled=True)  14 us
    all_gather x1, blocking collectives, shards(): rows_here = lax.all_gather(tokens, ('gy', 'gz'), axis=0, tiled=True)  9.32 us
    dot_general x1, matrix products, shards(): partial_out = jnp.dot(ordered, o_weight, preferred_element_type=jnp.float32)  8.38 us
    dot_general x1, matrix products, shards(): jnp.dot(rows_here, q_weight, preferred_element_type=jnp.float32)  8.24 us
    all_to_all x1, blocking collectives, shards(): lax.all_to_all(collected, ('gy', 'gz'), split_axis=1, concat_axis=0, tile...  7.7 us
    all_to_all x1, waiting for transfers between devices, shards(): lax.all_to_all(queries, ('gy', 'gz'), split_axis=0, concat_axis=1, tiled=...  3.86 us
  transfers between devices with their start and end apart: 3, of which 3 were waited for; matrix products, arithmetic and copies ran while one was open for 0% of the time, Pallas kernels for 0%

commit v1 on v0

v1 whole, which is shorter than its diff:
```python
import functools

import jax
import jax.numpy as jnp
from jax import lax
from jax.experimental import pallas as pl
from jax.experimental.pallas import tpu as pltpu
from jax.sharding import PartitionSpec as P

HDIM = 256
BF16 = jnp.bfloat16
F32 = jnp.float32
VMEM = pl.BlockSpec(memory_space=pltpu.VMEM)
ANY = pl.BlockSpec(memory_space=pl.ANY)
SMEM = pl.BlockSpec(memory_space=pltpu.SMEM)


def shift(array, axis, by):
    size = lax.axis_size(axis)
    return lax.ppermute(array, axis, [(s, (s + by) % size) for s in range(size)])


def largest_divisor(extent, limit, unit):
    best = extent
    for size in range(unit, limit + 1, unit):
        if extent % size == 0:
            best = size
    return best


def call(body, outs, operands, in_specs, scratch=(), mib=8, flops=0, name=None):
    moved = sum(a.size * a.dtype.itemsize for a in operands)
    moved += sum(o.size * o.dtype.itemsize for o in outs)
    return pl.pallas_call(
        body,
        out_shape=list(outs),
        in_specs=in_specs,
        out_specs=[VMEM] * len(outs),
        scratch_shapes=list(scratch),
        compiler_params=pltpu.CompilerParams(vmem_limit_bytes=mib * 2**20),
        cost_estimate=pl.CostEstimate(flops=flops, bytes_accessed=moved, transcendentals=0),
        name=name,
    )(*operands)


def query_body(n_gx, n_gy, n_gz, chunk, where, *refs):
    count = n_gy * n_gz
    pieces, weight = refs[:count], refs[count]
    outs = refs[count + 1 : count + 1 + n_gx]
    rows, total, held, sems = refs[count + 1 + n_gx :]
    chunks = weight.shape[0] // chunk

    def copy(c):
        span = pl.ds(c * chunk, chunk)
        return pltpu.make_async_copy(weight.at[span, :], held.at[span, :], sems.at[c])

    for c in range(chunks):
        copy(c).start()
    block = pieces[0].shape[0]
    for k in range(n_gy):
        for j in range(n_gz):
            at = lax.rem(where[1] + n_gy - k, n_gy) * n_gz + lax.rem(where[2] + n_gz - j, n_gz)
            rows[pl.ds(pl.multiple_of(at * block, block), block), :] = pieces[k * n_gz + j][...]
    for c in range(chunks):
        copy(c).wait()
        span = slice(c * chunk, (c + 1) * chunk)
        term = jnp.dot(rows[:, span], held[span, :], preferred_element_type=F32)
        if c == 0:
            total[...] = term
        else:
            total[...] += term
    part = outs[0].shape[0]
    for k in range(n_gx):
        at = pl.multiple_of(lax.rem(where[0] + k, n_gx) * part, part)
        outs[k][...] = total[pl.ds(at, part), :].astype(BF16)


def sum_split_body(n_gx, n_gy, n_gz, where, *refs):
    pieces, outs, total = refs[:n_gx], refs[n_gx : n_gx + n_gy], refs[-1]
    value = pieces[0][...].astype(F32)
    for piece in pieces[1:]:
        value = value + piece[...].astype(F32)
    each = outs[0].shape[1]
    for at in range(n_gy * n_gz):
        total[at] = value[at * each : (at + 1) * each]
    for k in range(n_gy):
        for j in range(n_gz):
            outs[k][j] = total[lax.rem(where[1] + k, n_gy) * n_gz + j].astype(BF16)


def attend_body(n_gy, n_gz, where, lengths, *refs):
    count = n_gy * n_gz
    pieces, key, value, outs = refs[:count], refs[count], refs[count + 1], refs[count + 2 :]
    each, width = pieces[0].shape[1:]
    heads = width // HDIM
    stacked = []
    for piece in pieces:
        mine = piece[where[2]].astype(F32)
        stacked += [mine[:, h * HDIM : (h + 1) * HDIM] for h in range(heads)]
    query = jnp.concatenate(stacked, axis=0).astype(BF16)
    cache = key.shape[1]
    keys = key[...].reshape(each * cache, HDIM)
    values = value[...].reshape(each * cache, HDIM)
    scores = lax.dot_general(query, keys, (((1,), (1,)), ((), ())), preferred_element_type=F32)
    scores = scores * HDIM ** (-0.5)
    row = lax.rem(lax.broadcasted_iota(jnp.int32, scores.shape, 0), each)
    place = lax.broadcasted_iota(jnp.int32, scores.shape, 1) - row * cache
    used = jnp.zeros((scores.shape[0], 1), jnp.int32)
    row_of = lax.rem(lax.broadcasted_iota(jnp.int32, (scores.shape[0], 1), 0), each)
    for r in range(each):
        used = jnp.where(row_of == r, lengths[r], used)
    scores = jnp.where((place >= 0) & (place < used), scores, -jnp.inf)
    raised = jnp.exp(scores - jnp.max(scores, axis=1, keepdims=True))
    totals = jnp.sum(raised, axis=1, keepdims=True)
    mixed = jnp.dot(raised.astype(BF16), values, preferred_element_type=F32) / totals
    for k in range(n_gy):
        for j in range(n_gz):
            source = ((n_gy - k) % n_gy) * n_gz + (n_gz - j) % n_gz
            for h in range(heads):
                at = (source * heads + h) * each
                outs[k][j, :, h * HDIM : (h + 1) * HDIM] = mixed[at : at + each].astype(BF16)


def gather_rows_body(n_gy, n_gz, where, *refs):
    pieces, out, total = refs[:-2], refs[-2], refs[-1]
    each = pieces[0].shape[1]
    for k in range(n_gy):
        for j in range(n_gz):
            at = lax.rem(where[1] + n_gy - k, n_gy) * n_gz + lax.rem(where[2] + n_gz - j, n_gz)
            total[at] = pieces[k * n_gz + j][j].astype(F32)
    out[...] = jnp.concatenate([total[i] for i in range(n_gy * n_gz)], axis=0).astype(BF16)


def output_body(n_gx, n_gy, n_gz, chunk, where, *refs):
    pieces, weight = refs[:n_gx], refs[n_gx]
    count = n_gy * n_gz
    outs = refs[n_gx + 1 : n_gx + 1 + count]
    rows, total, held, sems = refs[n_gx + 1 + count :]
    chunks = weight.shape[1] // chunk

    def copy(c):
        span = pl.ds(c * chunk, chunk)
        return pltpu.make_async_copy(weight.at[:, span], held.at[:, span], sems.at[c])

    for c in range(chunks):
        copy(c).start()
    block = pieces[0].shape[0]
    for k in range(n_gx):
        at = pl.multiple_of(lax.rem(where[0] + n_gx - k, n_gx) * block, block)
        rows[pl.ds(at, block), :] = pieces[k][...]
    part = outs[0].shape[0]
    for c in range(chunks):
        copy(c).wait()
        span = slice(c * chunk, (c + 1) * chunk)
        total[...] = jnp.dot(rows[...], held[:, span], preferred_element_type=F32)
        for k in range(n_gy):
            for j in range(n_gz):
                at = lax.rem(where[1] + k, n_gy) * n_gz + lax.rem(where[2] + j, n_gz)
                at = pl.multiple_of(at * part, part)
                outs[k * n_gz + j][:, span] = total[pl.ds(at, part), :].astype(BF16)


def sum_body(*refs):
    value = refs[0][...].astype(F32)
    for ref in refs[1:-1]:
        value = value + ref[...].astype(F32)
    refs[-1][...] = value.astype(BF16)


def added(arrays, name):
    out = jax.ShapeDtypeStruct(arrays[0].shape, BF16)
    return call(sum_body, [out], arrays, [VMEM] * len(arrays), name=name)[0]


def mib_for(*sizes):
    return max(8, -(-int(sum(sizes) * 1.25) // 2**20) + 2)


def shards(tokens, q_weight, o_weight, key_cache, value_cache, lengths):
    n_gx, n_gy, n_gz = (lax.axis_size(a) for a in ("gx", "gy", "gz"))
    where = jnp.stack([lax.axis_index(a) for a in ("gx", "gy", "gz")]).astype(jnp.int32)
    own_rows, depth = tokens.shape
    row_count = own_rows * n_gy * n_gz
    width = q_weight.shape[1]
    each = key_cache.shape[0]
    part = row_count // n_gx
    struct = jax.ShapeDtypeStruct

    pieces = []
    for k in range(n_gy):
        over = shift(tokens, "gy", k) if k else tokens
        pieces += [shift(over, "gz", j) if j else over for j in range(n_gz)]
    chunk = largest_divisor(depth, 512, 128)
    terms = call(
        functools.partial(query_body, n_gx, n_gy, n_gz, chunk),
        [struct((part, width), BF16)] * n_gx,
        [where, *pieces, q_weight],
        [SMEM] + [VMEM] * len(pieces) + [ANY],
        scratch=[
            pltpu.VMEM((row_count, depth), BF16),
            pltpu.VMEM((row_count, width), F32),
            pltpu.VMEM(q_weight.shape, BF16),
            pltpu.SemaphoreType.DMA((depth // chunk,)),
        ],
        mib=mib_for(row_count * depth * 4, row_count * width * 8, depth * width * 2),
        flops=2 * row_count * depth * width,
        name="query_terms",
    )

    terms = [terms[0]] + [shift(terms[k], "gx", k) for k in range(1, n_gx)]
    queries = call(
        functools.partial(sum_split_body, n_gx, n_gy, n_gz),
        [struct((n_gz, each, width), BF16)] * n_gy,
        [where, *terms],
        [SMEM] + [VMEM] * n_gx,
        scratch=[pltpu.VMEM((n_gy * n_gz, each, width), F32)],
        name="query_sum",
    )
    pieces = []
    for k in range(n_gy):
        over = shift(queries[k], "gy", k) if k else queries[k]
        pieces += [shift(over, "gz", j) if j else over for j in range(n_gz)]
    mixed = call(
        functools.partial(attend_body, n_gy, n_gz),
        [struct((n_gz, each, width), BF16)] * n_gy,
        [where, lengths, *pieces, key_cache, value_cache],
        [SMEM, SMEM] + [VMEM] * (len(pieces) + 2),
        mib=24,
        name="attention",
    )

    pieces = []
    for k in range(n_gy):
        over = shift(mixed[k], "gy", k) if k else mixed[k]
        pieces += [shift(over, "gz", j) if j else over for j in range(n_gz)]
    block = call(
        functools.partial(gather_rows_body, n_gy, n_gz),
        [struct((part, width), BF16)],
        [where, *pieces],
        [SMEM] + [VMEM] * len(pieces),
        scratch=[pltpu.VMEM((n_gy * n_gz, each, width), F32)],
        name="mixed_rows",
    )[0]
    blocks = [block] + [shift(block, "gx", k) for k in range(1, n_gx)]
    columns = o_weight.shape[1]
    chunk = largest_divisor(columns, 512, 128)
    terms = call(
        functools.partial(output_body, n_gx, n_gy, n_gz, chunk),
        [struct((own_rows, columns), BF16)] * (n_gy * n_gz),
        [where, *blocks, o_weight],
        [SMEM] + [VMEM] * n_gx + [ANY],
        scratch=[
            pltpu.VMEM((row_count, width), BF16),
            pltpu.VMEM((row_count, chunk), F32),
            pltpu.VMEM(o_weight.shape, BF16),
            pltpu.SemaphoreType.DMA((columns // chunk,)),
        ],
        mib=mib_for(row_count * width * 4, row_count * (chunk * 4 + columns * 2), columns * width * 2),
        flops=2 * row_count * columns * width,
        name="output_terms",
    )

    arrived = []
    for k in range(1, n_gy):
        mine = terms[k * n_gz : (k + 1) * n_gz]
        mine = [mine[0]] + [shift(mine[j], "gz", j) for j in range(1, n_gz)]
        arrived.append(shift(added(mine, "pair_sum") if n_gz > 1 else mine[0], "gy", k))
    mine = [terms[0]] + [shift(terms[j], "gz", j) for j in range(1, n_gz)]
    return added(mine + arrived, "output_sum")


def solution(mesh):
    return jax.shard_map(
        shards,
        mesh=mesh,
        in_specs=(
            P(("groups", "gy", "gz"), "gx"),
            P("gx", ("gy", "gz")),
            P(("gy", "gz"), "gx"),
            P(("groups", "gx", "gy", "gz"), None, None),
            P(("groups", "gx", "gy", "gz"), None, None),
            P(("groups", "gx", "gy", "gz")),
        ),
        out_specs=P(("groups", "gy", "gz"), "gx"),
        check_vma=False,
    )
```

time: 112 us -> 65.3 us (0.58)
  blocking collectives: 31 us -> 0 us
  waiting for transfers between devices: 43.7 us -> 25.8 us
  matrix products: 17.3 us -> 0 us
  starting transfers between devices: 3.32 us -> 17.7 us
  between operations: 13.5 us -> 0.07 us
  Pallas kernels: 0 us -> 13 us
  local copies, waits for them, and re-layouts: 1.98 us -> 8.39 us
    reduce_scatter x2 -> x0, waiting for transfers between devices: 39.8 us -> none  [the longest x1 20.4 us: shards(): lax.psum_scatter(jnp.dot(rows_here, q_weight, preferred_element_type=jnp....]
    ppermute x0 -> x18, waiting for transfers between devices: none -> 25.8 us  [shift(): lax.ppermute(array, axis, [(s, (s + by) % size) for s in range(size)])]
    all_gather x2 -> x0, blocking collectives: 23.3 us -> none  [the longest x1 14 us: shards(): collected = lax.all_gather(attended, 'gx', axis=0, tiled=True)]
    ppermute x0 -> x18, starting transfers between devices: none -> 17.7 us  [shift(): lax.ppermute(array, axis, [(s, (s + by) % size) for s in range(size)])]
    dot_general x4 -> x0, matrix products: 17.3 us -> none  [the longest x1 8.38 us: shards(): partial_out = jnp.dot(ordered, o_weight, preferred_element_type=jnp.float32)]
    pallas_call x0 -> x7, Pallas kernels: none -> 13 us  [call(): pl.pallas_call(body, out_shape=list(outs), in_specs=in_specs, out_specs=[...]
    unnamed x7 -> x12, local copies, waits for them, and re-layouts: 0.05 us -> 8.39 us
    all_to_all x1 -> x0, blocking collectives: 7.7 us -> none  [shards(): lax.all_to_all(collected, ('gy', 'gz'), split_axis=1, concat_axis=0, tile...]
  transfers between devices with their start and end apart: 3 -> 18, of which waited for: 3 -> 14; matrix products, arithmetic and copies ran while one was open for 0% -> 0% of each run, Pallas kernels for 0% -> 0%
where the time goes in v1:
time: 65.3 us; the launch traced here: 65.1 us
  waiting for transfers between devices  25.8 us (40%)
  starting transfers between devices  17.7 us (27%)
  Pallas kernels  13 us (20%)
  local copies, waits for them, and re-layouts  8.39 us (13%)
    ppermute x18, waiting for transfers between devices, shift(): lax.ppermute(array, axis, [(s, (s + by) % size) for s in range(size)])  25.8 us
    ppermute x18, starting transfers between devices, shift(): lax.ppermute(array, axis, [(s, (s + by) % size) for s in range(size)])  17.7 us
    pallas_call x7, Pallas kernels, call(): pl.pallas_call(body, out_shape=list(outs), in_specs=in_specs, out_specs=[...  13 us
    unnamed x12, local copies, waits for them, and re-layouts  8.39 us
  transfers between devices with their start and end apart: 18, of which 14 were waited for; matrix products, arithmetic and copies ran while one was open for 0% of the time, Pallas kernels for 0%

profile of v1, /device:TPU:0, one launch (start us, length us, event | category | flops | bytes accessed | tf_op | source)
XLA Modules:
  0.0 65.1 jit_solution(16275771384812931307)
XLA Ops:
  0.0 2.9 %collective-permute-start.1 = (bf16[16,4608]{1,0:T(8,128)(2,1)}, bf16[16,4608]{1,0:T(8,128)(2,1)S(1)}, u32[]{:S(2)}, u32[]{:S(2)}) collective-permute-start(bf16[16,4608]{1,0:T(8,128)(2,1)} %refs_0_.1), channel_id=1, source_target_pairs={{0,2},{2,0},{1,3},{3,1},{4,6},{6,4},{5,7},{7,5},{8,10},{10,8},{9,1... | collective-permute-start | bytes 442376 | tf_op jit(solution)/shard_map/ppermute | solution.py:20
  2.9 4.1 %collective-permute-done.1.refs_2_ = bf16[16,4608]{1,0:T(8,128)(2,1)S(1)} collective-permute-done((bf16[16,4608]{1,0:T(8,128)(2,1)}, bf16[16,4608]{1,0:T(8,128)(2,1)S(1)}, u32[]{:S(2)}, u32[]{:S(2)}) %collective-permute-start.1) | collective-permute-done | bytes 147488 | tf_op jit(solution)/shard_map/ppermute | solution.py:20
  7.1 1.3 %collective-permute-done.2.refs_3_ = bf16[16,4608]{1,0:T(8,128)(2,1)S(1)} collective-permute-done((bf16[16,4608]{1,0:T(8,128)(2,1)S(1)}, bf16[16,4608]{1,0:T(8,128)(2,1)S(1)}, u32[]{:S(2)}, u32[]{:S(2)}) %collective-permute-start.2) | collective-permute-done | bytes 147488 | tf_op jit(solution)/shard_map/ppermute | solution.py:20
  8.4 5.0 %copy-done = bf16[4608,1536]{1,0:T(8,128)(2,1)S(1)} copy-done((bf16[4608,1536]{1,0:T(8,128)(2,1)S(1)}, bf16[4608,1536]{1,0:T(8,128)(2,1)}, u32[]{:S(2)}) %copy-start) | copy-done | bytes 14155800
  13.4 0.9 %copy-done.4 = bf16[16,4608]{1,0:T(8,128)(2,1)S(1)} copy-done((bf16[16,4608]{1,0:T(8,128)(2,1)S(1)}, bf16[16,4608]{1,0:T(8,128)(2,1)}, u32[]{:S(2)}) %copy-start.4) | copy-done | bytes 147480
  14.3 4.3 %query_terms.1 = (bf16[16,1536]{1,0:T(8,128)(2,1)S(1)}, bf16[16,1536]{1,0:T(8,128)(2,1)S(1)}, bf16[16,1536]{1,0:T(8,128)(2,1)S(1)}, bf16[16,1536]{1,0:T(8,128)(2,1)S(1)}) custom-call(s32[3]{0:T(128)S(1)} %pad_add_fusion.where, bf16[16,4608]{1,0:T(8,128)(2,1)S(1)} %copy-done.4, bf16[16,4608]{1,0:T(8,128)(2,1)S(1)} %collective-permute-done.refs_1_, ...), custom_call_target="tpu_custom_call" | custom-call | flops 905969664 | bytes 14942220 | tf_op jit(solution)/shard_map/query_terms/pallas_call | solution.py:34
  18.6 1.9 %collective-permute-start.3 = (bf16[16,1536]{1,0:T(8,128)(2,1)S(1)}, bf16[16,1536]{1,0:T(8,128)(2,1)S(1)}, u32[]{:S(2)}, u32[]{:S(2)}) collective-permute-start(bf16[16,1536]{1,0:T(8,128)(2,1)S(1)} %get-tuple-element.18), channel_id=1, source_target_pairs={{0,4},{4,8},{8,12},{12,0},{1,5},{5,9},{9,13},{13,1},{2,6},{6,10},{... | collective-permute-start | bytes 147464 | tf_op jit(solution)/shard_map/ppermute | solution.py:20
  20.5 2.6 %collective-permute-start.4 = (bf16[16,1536]{1,0:T(8,128)(2,1)S(1)}, bf16[16,1536]{1,0:T(8,128)(2,1)S(1)}, u32[]{:S(2)}, u32[]{:S(2)}) collective-permute-start(bf16[16,1536]{1,0:T(8,128)(2,1)S(1)} %get-tuple-element.19), channel_id=1, source_target_pairs={{0,8},{4,12},{8,0},{12,4},{1,9},{5,13},{9,1},{13,5},{2,10},{6,14},... | collective-permute-start | bytes 147464 | tf_op jit(solution)/shard_map/ppermute | solution.py:20
  23.1 1.3 %collective-permute-start.5 = (bf16[16,1536]{1,0:T(8,128)(2,1)S(1)}, bf16[16,1536]{1,0:T(8,128)(2,1)S(1)}, u32[]{:S(2)}, u32[]{:S(2)}) collective-permute-start(bf16[16,1536]{1,0:T(8,128)(2,1)S(1)} %get-tuple-element.20), channel_id=1, source_target_pairs={{0,12},{4,0},{8,4},{12,8},{1,13},{5,1},{9,5},{13,9},{2,14},{6,2},{... | collective-permute-start | bytes 147464 | tf_op jit(solution)/shard_map/ppermute | solution.py:20
  24.6 2.3 %collective-permute-done.4.refs_2_ = bf16[16,1536]{1,0:T(8,128)(2,1)S(1)} collective-permute-done((bf16[16,1536]{1,0:T(8,128)(2,1)S(1)}, bf16[16,1536]{1,0:T(8,128)(2,1)S(1)}, u32[]{:S(2)}, u32[]{:S(2)}) %collective-permute-start.4) | collective-permute-done | bytes 49184 | tf_op jit(solution)/shard_map/ppermute | solution.py:20
  27.3 0.6 query_sum.1
  27.9 1.6 %collective-permute-start.7 = (bf16[2,4,1536]{2,1,0:T(4,128)(2,1)S(1)}, bf16[2,4,1536]{2,1,0:T(4,128)(2,1)S(1)}, u32[]{:S(2)}, u32[]{:S(2)}) collective-permute-start(bf16[2,4,1536]{2,1,0:T(4,128)(2,1)S(1)} %get-tuple-element.22), channel_id=1, source_target_pairs={{0,2},{2,0},{1,3},{3,1},{4,6},{6,4},{5,7},{7,5},{8,10},{10,8},{9,1... | collective-permute-start | bytes 73736 | tf_op jit(solution)/shard_map/ppermute | solution.py:20
  29.5 2.3 %collective-permute-done.7.refs_2_ = bf16[2,4,1536]{2,1,0:T(4,128)(2,1)S(1)} collective-permute-done((bf16[2,4,1536]{2,1,0:T(4,128)(2,1)S(1)}, bf16[2,4,1536]{2,1,0:T(4,128)(2,1)S(1)}, u32[]{:S(2)}, u32[]{:S(2)}) %collective-permute-start.7) | collective-permute-done | bytes 24608 | tf_op jit(solution)/shard_map/ppermute | solution.py:20
  31.8 1.2 %collective-permute-done.8.refs_3_ = bf16[2,4,1536]{2,1,0:T(4,128)(2,1)S(1)} collective-permute-done((bf16[2,4,1536]{2,1,0:T(4,128)(2,1)S(1)}, bf16[2,4,1536]{2,1,0:T(4,128)(2,1)S(1)}, u32[]{:S(2)}, u32[]{:S(2)}) %collective-permute-start.8) | collective-permute-done | bytes 24608 | tf_op jit(solution)/shard_map/ppermute | solution.py:20
  33.0 1.2 %copy-done.2 = bf16[4,512,256]{2,1,0:T(8,128)(2,1)S(1)} copy-done((bf16[4,512,256]{2,1,0:T(8,128)(2,1)S(1)}, bf16[4,512,256]{2,1,0:T(8,128)(2,1)}, u32[]{:S(2)}) %copy-start.2) | copy-done | bytes 1048600
  34.2 1.2 %copy-done.3 = bf16[4,512,256]{2,1,0:T(8,128)(2,1)S(1)} copy-done((bf16[4,512,256]{2,1,0:T(8,128)(2,1)S(1)}, bf16[4,512,256]{2,1,0:T(8,128)(2,1)}, u32[]{:S(2)}) %copy-start.3) | copy-done | bytes 1048600
  35.5 1.7 %attention.1 = (bf16[2,4,1536]{2,1,0:T(4,128)(2,1)S(1)}, bf16[2,4,1536]{2,1,0:T(4,128)(2,1)S(1)}) custom-call(s32[3]{0:T(128)S(1)} %pad_add_fusion.where, s32[4]{0:T(128)S(1)} %copy-done.5, bf16[2,4,1536]{2,1,0:T(4,128)(2,1)S(1)} %get-tuple-element.21.refs_0_, bf16[2,4,1536]{2,1,0:T(4,128)(2,1)S(1)} %collective-permute-done.6.refs_1_, ...), custom_call_target="tpu_custom_call" | custom-call | bytes 2244636 | tf_op jit(solution)/shard_map/attention/pallas_call | solution.py:34
  37.1 1.6 %collective-permute-start.10 = (bf16[2,4,1536]{2,1,0:T(4,128)(2,1)S(1)}, bf16[2,4,1536]{2,1,0:T(4,128)(2,1)S(1)}, u32[]{:S(2)}, u32[]{:S(2)}) collective-permute-start(bf16[2,4,1536]{2,1,0:T(4,128)(2,1)S(1)} %get-tuple-element.24), channel_id=1, source_target_pairs={{0,2},{2,0},{1,3},{3,1},{4,6},{6,4},{5,7},{7,5},{8,10},{10,8},{9,1... | collective-permute-start | bytes 73736 | tf_op jit(solution)/shard_map/ppermute | solution.py:20
  38.7 2.3 %collective-permute-done.10.refs_2_ = bf16[2,4,1536]{2,1,0:T(4,128)(2,1)S(1)} collective-permute-done((bf16[2,4,1536]{2,1,0:T(4,128)(2,1)S(1)}, bf16[2,4,1536]{2,1,0:T(4,128)(2,1)S(1)}, u32[]{:S(2)}, u32[]{:S(2)}) %collective-permute-start.10) | collective-permute-done | bytes 24608 | tf_op jit(solution)/shard_map/ppermute | solution.py:20
  41.0 1.2 %collective-permute-done.11.refs_3_ = bf16[2,4,1536]{2,1,0:T(4,128)(2,1)S(1)} collective-permute-done((bf16[2,4,1536]{2,1,0:T(4,128)(2,1)S(1)}, bf16[2,4,1536]{2,1,0:T(4,128)(2,1)S(1)}, u32[]{:S(2)}, u32[]{:S(2)}) %collective-permute-start.11) | collective-permute-done | bytes 24608 | tf_op jit(solution)/shard_map/ppermute | solution.py:20
  42.2 0.6 mixed_rows.1.refs_0_
  42.8 3.0 %collective-permute-start.14 = (bf16[16,1536]{1,0:T(8,128)(2,1)S(1)}, bf16[16,1536]{1,0:T(8,128)(2,1)S(1)}, u32[]{:S(2)}, u32[]{:S(2)}) collective-permute-start(bf16[16,1536]{1,0:T(8,128)(2,1)S(1)} %mixed_rows.1.refs_0_), channel_id=1, source_target_pairs={{0,12},{4,0},{8,4},{12,8},{1,13},{5,1},{9,5},{13,9},{2,14},{6,2},{... | collective-permute-start | bytes 147464 | tf_op jit(solution)/shard_map/ppermute | solution.py:20
  45.9 0.6 collective-permute-start.12
  46.5 1.5 %collective-permute-done.14.refs_3_ = bf16[16,1536]{1,0:T(8,128)(2,1)S(1)} collective-permute-done((bf16[16,1536]{1,0:T(8,128)(2,1)S(1)}, bf16[16,1536]{1,0:T(8,128)(2,1)S(1)}, u32[]{:S(2)}, u32[]{:S(2)}) %collective-permute-start.14) | collective-permute-done | bytes 49184 | tf_op jit(solution)/shard_map/ppermute | solution.py:20
  48.0 3.2 %collective-permute-done.13.refs_2_ = bf16[16,1536]{1,0:T(8,128)(2,1)S(1)} collective-permute-done((bf16[16,1536]{1,0:T(8,128)(2,1)S(1)}, bf16[16,1536]{1,0:T(8,128)(2,1)S(1)}, u32[]{:S(2)}, u32[]{:S(2)}) %collective-permute-start.13) | collective-permute-done | bytes 49184 | tf_op jit(solution)/shard_map/ppermute | solution.py:20
  51.2 0.6 collective-permute-done.12.refs_1_
  51.7 5.2 %output_terms.1 = (bf16[16,4608]{1,0:T(8,128)(2,1)S(1)}, bf16[16,4608]{1,0:T(8,128)(2,1)S(1)}, bf16[16,4608]{1,0:T(8,128)(2,1)S(1)}, bf16[16,4608]{1,0:T(8,128)(2,1)S(1)}) custom-call(s32[3]{0:T(128)S(1)} %pad_add_fusion.where, bf16[16,1536]{1,0:T(8,128)(2,1)S(1)} %mixed_rows.1.refs_0_, bf16[16,1536]{1,0:T(8,128)(2,1)S(1)} %collective-permute-done.12.refs_1_, ...), custom_call_target="tpu_custom_call" | custom-call | flops 905969664 | bytes 14942220 | tf_op jit(solution)/shard_map/output_terms/pallas_call | solution.py:34
  57.0 0.5 collective-permute-start.15
  57.5 0.9 %collective-permute-done.16.refs_1_ = bf16[16,4608]{1,0:T(8,128)(2,1)S(1)} collective-permute-done((bf16[16,4608]{1,0:T(8,128)(2,1)S(1)}, bf16[16,4608]{1,0:T(8,128)(2,1)S(1)}, u32[]{:S(2)}, u32[]{:S(2)}) %collective-permute-start.16) | collective-permute-done | bytes 147488 | tf_op jit(solution)/shard_map/ppermute | solution.py:20
  58.4 1.6 %collective-permute-start.17 = (bf16[16,4608]{1,0:T(8,128)(2,1)S(1)}, bf16[16,4608]{1,0:T(8,128)(2,1)S(1)}, u32[]{:S(2)}, u32[]{:S(2)}) collective-permute-start(bf16[16,4608]{1,0:T(8,128)(2,1)S(1)} %pair_sum.1), channel_id=1, source_target_pairs={{0,2},{2,0},{1,3},{3,1},{4,6},{6,4},{5,7},{7,5},{8,10},{10,8},{9,1... | collective-permute-start | bytes 442376 | tf_op jit(solution)/shard_map/ppermute | solution.py:20
  60.0 4.4 %collective-permute-done.17.refs_2_ = bf16[16,4608]{1,0:T(8,128)(2,1)S(1)} collective-permute-done((bf16[16,4608]{1,0:T(8,128)(2,1)S(1)}, bf16[16,4608]{1,0:T(8,128)(2,1)S(1)}, u32[]{:S(2)}, u32[]{:S(2)}) %collective-permute-start.17) | collective-permute-done | bytes 147488 | tf_op jit(solution)/shard_map/ppermute | solution.py:20
  64.3 0.7 %output_sum.1 = bf16[16,4608]{1,0:T(8,128)(2,1)} custom-call(bf16[16,4608]{1,0:T(8,128)(2,1)S(1)} %get-tuple-element.25.refs_0_, bf16[16,4608]{1,0:T(8,128)(2,1)S(1)} %collective-permute-done.15.refs_1_, bf16[16,4608]{1,0:T(8,128)(2,1)S(1)} %collective-permute-done.17.refs_2_), custom_call_target="tpu_custom_call" | custom-call | bytes 589824 | tf_op jit(solution)/shard_map/output_sum/pallas_call | solution.py:34
  (24 shorter events, 0.8 us)
Async XLA Ops:
  0.0 33.0 %copy-start.5 = (s32[4]{0:T(128)S(1)}, s32[4]{0:T(128)}, u32[]{:S(2)}) copy-start(s32[4]{0:T(128)} %lengths.1) | copy-start | bytes 52
  0.0 7.0 %collective-permute-start.1 = (bf16[16,4608]{1,0:T(8,128)(2,1)}, bf16[16,4608]{1,0:T(8,128)(2,1)S(1)}, u32[]{:S(2)}, u32[]{:S(2)}) collective-permute-start(bf16[16,4608]{1,0:T(8,128)(2,1)} %refs_0_.1), channel_id=1, source_target_pairs={{0,2},{2,0},{1,3},{3,1},{4,6},{6,4},{5,7},{7,5},{8,10},{10,8},{9,1... | collective-permute-start | bytes 442376 | tf_op jit(solution)/shard_map/ppermute | solution.py:20
  2.9 4.1 %collective-permute-start = (bf16[16,4608]{1,0:T(8,128)(2,1)}, bf16[16,4608]{1,0:T(8,128)(2,1)S(1)}, u32[]{:S(2)}, u32[]{:S(2)}) collective-permute-start(bf16[16,4608]{1,0:T(8,128)(2,1)} %refs_0_.1), channel_id=1, source_target_pairs={{0,1},{1,0},{2,3},{3,2},{4,5},{5,4},{6,7},{7,6},{8,9},{9,8},{10,11... | collective-permute-start | bytes 442376 | tf_op jit(solution)/shard_map/ppermute | solution.py:20
  7.0 1.4 %collective-permute-start.2 = (bf16[16,4608]{1,0:T(8,128)(2,1)S(1)}, bf16[16,4608]{1,0:T(8,128)(2,1)S(1)}, u32[]{:S(2)}, u32[]{:S(2)}) collective-permute-start(bf16[16,4608]{1,0:T(8,128)(2,1)S(1)} %collective-permute-done.1.refs_2_), channel_id=1, source_target_pairs={{0,1},{1,0},{2,3},{3,2},{4,5},{5,4},{6,7},{7,6},{8,9},{9,8},{10,11... | collective-permute-start | bytes 442376 | tf_op jit(solution)/shard_map/ppermute | solution.py:20
  8.4 5.0 %copy-start = (bf16[4608,1536]{1,0:T(8,128)(2,1)S(1)}, bf16[4608,1536]{1,0:T(8,128)(2,1)}, u32[]{:S(2)}) copy-start(bf16[4608,1536]{1,0:T(8,128)(2,1)} %refs_4_.3) | copy-start | bytes 42467332
  13.4 0.9 %copy-start.4 = (bf16[16,4608]{1,0:T(8,128)(2,1)S(1)}, bf16[16,4608]{1,0:T(8,128)(2,1)}, u32[]{:S(2)}) copy-start(bf16[16,4608]{1,0:T(8,128)(2,1)} %refs_0_.1) | copy-start | bytes 442372
  14.3 37.4 %copy-start.1 = (bf16[1536,4608]{1,0:T(8,128)(2,1)S(1)}, bf16[1536,4608]{1,0:T(8,128)(2,1)}, u32[]{:S(2)}) copy-start(bf16[1536,4608]{1,0:T(8,128)(2,1)} %refs_4_.5) | copy-start | bytes 42467332
  18.6 6.0 %collective-permute-start.3 = (bf16[16,1536]{1,0:T(8,128)(2,1)S(1)}, bf16[16,1536]{1,0:T(8,128)(2,1)S(1)}, u32[]{:S(2)}, u32[]{:S(2)}) collective-permute-start(bf16[16,1536]{1,0:T(8,128)(2,1)S(1)} %get-tuple-element.18), channel_id=1, source_target_pairs={{0,4},{4,8},{8,12},{12,0},{1,5},{5,9},{9,13},{13,1},{2,6},{6,10},{... | collective-permute-start | bytes 147464 | tf_op jit(solution)/shard_map/ppermute | solution.py:20
  20.5 6.5 %collective-permute-start.4 = (bf16[16,1536]{1,0:T(8,128)(2,1)S(1)}, bf16[16,1536]{1,0:T(8,128)(2,1)S(1)}, u32[]{:S(2)}, u32[]{:S(2)}) collective-permute-start(bf16[16,1536]{1,0:T(8,128)(2,1)S(1)} %get-tuple-element.19), channel_id=1, source_target_pairs={{0,8},{4,12},{8,0},{12,4},{1,9},{5,13},{9,1},{13,5},{2,10},{6,14},... | collective-permute-start | bytes 147464 | tf_op jit(solution)/shard_map/ppermute | solution.py:20
  23.1 4.3 %collective-permute-start.5 = (bf16[16,1536]{1,0:T(8,128)(2,1)S(1)}, bf16[16,1536]{1,0:T(8,128)(2,1)S(1)}, u32[]{:S(2)}, u32[]{:S(2)}) collective-permute-start(bf16[16,1536]{1,0:T(8,128)(2,1)S(1)} %get-tuple-element.20), channel_id=1, source_target_pairs={{0,12},{4,0},{8,4},{12,8},{1,13},{5,1},{9,5},{13,9},{2,14},{6,2},{... | collective-permute-start | bytes 147464 | tf_op jit(solution)/shard_map/ppermute | solution.py:20
  27.9 3.9 %collective-permute-start.7 = (bf16[2,4,1536]{2,1,0:T(4,128)(2,1)S(1)}, bf16[2,4,1536]{2,1,0:T(4,128)(2,1)S(1)}, u32[]{:S(2)}, u32[]{:S(2)}) collective-permute-start(bf16[2,4,1536]{2,1,0:T(4,128)(2,1)S(1)} %get-tuple-element.22), channel_id=1, source_target_pairs={{0,2},{2,0},{1,3},{3,1},{4,6},{6,4},{5,7},{7,5},{8,10},{10,8},{9,1... | collective-permute-start | bytes 73736 | tf_op jit(solution)/shard_map/ppermute | solution.py:20
  29.5 2.3 %collective-permute-start.6 = (bf16[2,4,1536]{2,1,0:T(4,128)(2,1)S(1)}, bf16[2,4,1536]{2,1,0:T(4,128)(2,1)S(1)}, u32[]{:S(2)}, u32[]{:S(2)}) collective-permute-start(bf16[2,4,1536]{2,1,0:T(4,128)(2,1)S(1)} %get-tuple-element.21.refs_0_), channel_id=1, source_target_pairs={{0,1},{1,0},{2,3},{3,2},{4,5},{5,4},{6,7},{7,6},{8,9},{9,8},{10,11... | collective-permute-start | bytes 73736 | tf_op jit(solution)/shard_map/ppermute | solution.py:20
  31.8 1.2 %collective-permute-start.8 = (bf16[2,4,1536]{2,1,0:T(4,128)(2,1)S(1)}, bf16[2,4,1536]{2,1,0:T(4,128)(2,1)S(1)}, u32[]{:S(2)}, u32[]{:S(2)}) collective-permute-start(bf16[2,4,1536]{2,1,0:T(4,128)(2,1)S(1)} %collective-permute-done.7.refs_2_), channel_id=1, source_target_pairs={{0,1},{1,0},{2,3},{3,2},{4,5},{5,4},{6,7},{7,6},{8,9},{9,8},{10,11... | collective-permute-start | bytes 73736 | tf_op jit(solution)/shard_map/ppermute | solution.py:20
  33.0 1.2 %copy-start.2 = (bf16[4,512,256]{2,1,0:T(8,128)(2,1)S(1)}, bf16[4,512,256]{2,1,0:T(8,128)(2,1)}, u32[]{:S(2)}) copy-start(bf16[4,512,256]{2,1,0:T(8,128)(2,1)} %refs_4_.4) | copy-start | bytes 3145732
  34.2 1.2 %copy-start.3 = (bf16[4,512,256]{2,1,0:T(8,128)(2,1)S(1)}, bf16[4,512,256]{2,1,0:T(8,128)(2,1)}, u32[]{:S(2)}) copy-start(bf16[4,512,256]{2,1,0:T(8,128)(2,1)} %refs_5_.1) | copy-start | bytes 3145732
  37.1 3.9 %collective-permute-start.10 = (bf16[2,4,1536]{2,1,0:T(4,128)(2,1)S(1)}, bf16[2,4,1536]{2,1,0:T(4,128)(2,1)S(1)}, u32[]{:S(2)}, u32[]{:S(2)}) collective-permute-start(bf16[2,4,1536]{2,1,0:T(4,128)(2,1)S(1)} %get-tuple-element.24), channel_id=1, source_target_pairs={{0,2},{2,0},{1,3},{3,1},{4,6},{6,4},{5,7},{7,5},{8,10},{10,8},{9,1... | collective-permute-start | bytes 73736 | tf_op jit(solution)/shard_map/ppermute | solution.py:20
  38.7 2.3 %collective-permute-start.9 = (bf16[2,4,1536]{2,1,0:T(4,128)(2,1)S(1)}, bf16[2,4,1536]{2,1,0:T(4,128)(2,1)S(1)}, u32[]{:S(2)}, u32[]{:S(2)}) collective-permute-start(bf16[2,4,1536]{2,1,0:T(4,128)(2,1)S(1)} %get-tuple-element.23.refs_0_), channel_id=1, source_target_pairs={{0,1},{1,0},{2,3},{3,2},{4,5},{5,4},{6,7},{7,6},{8,9},{9,8},{10,11... | collective-permute-start | bytes 73736 | tf_op jit(solution)/shard_map/ppermute | solution.py:20
  41.0 1.2 %collective-permute-start.11 = (bf16[2,4,1536]{2,1,0:T(4,128)(2,1)S(1)}, bf16[2,4,1536]{2,1,0:T(4,128)(2,1)S(1)}, u32[]{:S(2)}, u32[]{:S(2)}) collective-permute-start(bf16[2,4,1536]{2,1,0:T(4,128)(2,1)S(1)} %collective-permute-done.10.refs_2_), channel_id=1, source_target_pairs={{0,1},{1,0},{2,3},{3,2},{4,5},{5,4},{6,7},{7,6},{8,9},{9,8},{10,11... | collective-permute-start | bytes 73736 | tf_op jit(solution)/shard_map/ppermute | solution.py:20
  42.8 5.2 %collective-permute-start.14 = (bf16[16,1536]{1,0:T(8,128)(2,1)S(1)}, bf16[16,1536]{1,0:T(8,128)(2,1)S(1)}, u32[]{:S(2)}, u32[]{:S(2)}) collective-permute-start(bf16[16,1536]{1,0:T(8,128)(2,1)S(1)} %mixed_rows.1.refs_0_), channel_id=1, source_target_pairs={{0,12},{4,0},{8,4},{12,8},{1,13},{5,1},{9,5},{13,9},{2,14},{6,2},{... | collective-permute-start | bytes 147464 | tf_op jit(solution)/shard_map/ppermute | solution.py:20
  45.9 5.3 %collective-permute-start.13 = (bf16[16,1536]{1,0:T(8,128)(2,1)S(1)}, bf16[16,1536]{1,0:T(8,128)(2,1)S(1)}, u32[]{:S(2)}, u32[]{:S(2)}) collective-permute-start(bf16[16,1536]{1,0:T(8,128)(2,1)S(1)} %mixed_rows.1.refs_0_), channel_id=1, source_target_pairs={{0,8},{4,12},{8,0},{12,4},{1,9},{5,13},{9,1},{13,5},{2,10},{6,14},... | collective-permute-start | bytes 147464 | tf_op jit(solution)/shard_map/ppermute | solution.py:20
  45.9 5.9 %collective-permute-start.12 = (bf16[16,1536]{1,0:T(8,128)(2,1)S(1)}, bf16[16,1536]{1,0:T(8,128)(2,1)S(1)}, u32[]{:S(2)}, u32[]{:S(2)}) collective-permute-start(bf16[16,1536]{1,0:T(8,128)(2,1)S(1)} %mixed_rows.1.refs_0_), channel_id=1, source_target_pairs={{0,4},{4,8},{8,12},{12,0},{1,5},{5,9},{9,13},{13,1},{2,6},{6,10},{... | collective-permute-start | bytes 147464 | tf_op jit(solution)/shard_map/ppermute | solution.py:20
  56.9 1.4 %collective-permute-start.16 = (bf16[16,4608]{1,0:T(8,128)(2,1)S(1)}, bf16[16,4608]{1,0:T(8,128)(2,1)S(1)}, u32[]{:S(2)}, u32[]{:S(2)}) collective-permute-start(bf16[16,4608]{1,0:T(8,128)(2,1)S(1)} %get-tuple-element.28), channel_id=1, source_target_pairs={{0,1},{1,0},{2,3},{3,2},{4,5},{5,4},{6,7},{7,6},{8,9},{9,8},{10,11... | collective-permute-start | bytes 442376 | tf_op jit(solution)/shard_map/ppermute | solution.py:20
  57.0 3.0 %collective-permute-start.15 = (bf16[16,4608]{1,0:T(8,128)(2,1)S(1)}, bf16[16,4608]{1,0:T(8,128)(2,1)S(1)}, u32[]{:S(2)}, u32[]{:S(2)}) collective-permute-start(bf16[16,4608]{1,0:T(8,128)(2,1)S(1)} %get-tuple-element.26), channel_id=1, source_target_pairs={{0,1},{1,0},{2,3},{3,2},{4,5},{5,4},{6,7},{7,6},{8,9},{9,8},{10,11... | collective-permute-start | bytes 442376 | tf_op jit(solution)/shard_map/ppermute | solution.py:20
  58.4 6.0 %collective-permute-start.17 = (bf16[16,4608]{1,0:T(8,128)(2,1)S(1)}, bf16[16,4608]{1,0:T(8,128)(2,1)S(1)}, u32[]{:S(2)}, u32[]{:S(2)}) collective-permute-start(bf16[16,4608]{1,0:T(8,128)(2,1)S(1)} %pair_sum.1), channel_id=1, source_target_pairs={{0,2},{2,0},{1,3},{3,1},{4,6},{6,4},{5,7},{7,5},{8,10},{10,8},{9,1... | collective-permute-start | bytes 442376 | tf_op jit(solution)/shard_map/ppermute | solution.py:20

commit v2 on v1

--- a/solution.py
+++ b/solution.py
@@ -20,6 +20,10 @@
     return lax.ppermute(array, axis, [(s, (s + by) % size) for s in range(size)])
 
 
+def position():
+    return tuple(lax.axis_index(a) for a in ("gx", "gy", "gz"))
+
+
 def largest_divisor(extent, limit, unit):
     best = extent
     for size in range(unit, limit + 1, unit):
@@ -28,7 +32,7 @@
     return best
 
 
-def call(body, outs, operands, in_specs, scratch=(), mib=8, flops=0, name=None):
+def call(body, outs, operands, in_specs, scratch=(), mib=8, flops=0, beside=0, name=None):
     moved = sum(a.size * a.dtype.itemsize for a in operands)
     moved += sum(o.size * o.dtype.itemsize for o in outs)
     return pl.pallas_call(
@@ -38,44 +42,42 @@
         out_specs=[VMEM] * len(outs),
         scratch_shapes=list(scratch),
         compiler_params=pltpu.CompilerParams(vmem_limit_bytes=mib * 2**20),
-        cost_estimate=pl.CostEstimate(flops=flops, bytes_accessed=moved, transcendentals=0),
+        cost_estimate=pl.CostEstimate(flops=flops + beside, bytes_accessed=moved, transcendentals=0),
         name=name,
     )(*operands)
 
 
-def query_body(n_gx, n_gy, n_gz, chunk, where, *refs):
+def stage_body(tokens, out, sem):
+    copy = pltpu.make_async_copy(tokens, out, sem)
+    copy.start()
+    copy.wait()
+
+
+def query_body(n_gx, n_gy, n_gz, chunk, *refs):
+    where = position()
     count = n_gy * n_gz
     pieces, weight = refs[:count], refs[count]
     outs = refs[count + 1 : count + 1 + n_gx]
-    rows, total, held, sems = refs[count + 1 + n_gx :]
-    chunks = weight.shape[0] // chunk
-
-    def copy(c):
-        span = pl.ds(c * chunk, chunk)
-        return pltpu.make_async_copy(weight.at[span, :], held.at[span, :], sems.at[c])
-
-    for c in range(chunks):
-        copy(c).start()
+    rows, total = refs[count + 1 + n_gx :]
     block = pieces[0].shape[0]
     for k in range(n_gy):
         for j in range(n_gz):
             at = lax.rem(where[1] + n_gy - k, n_gy) * n_gz + lax.rem(where[2] + n_gz - j, n_gz)
             rows[pl.ds(pl.multiple_of(at * block, block), block), :] = pieces[k * n_gz + j][...]
-    for c in range(chunks):
-        copy(c).wait()
-        span = slice(c * chunk, (c + 1) * chunk)
-        term = jnp.dot(rows[:, span], held[span, :], preferred_element_type=F32)
-        if c == 0:
-            total[...] = term
-        else:
-            total[...] += term
+
+    @pl.loop(0, weight.shape[1] // chunk)
+    def _(c):
+        span = pl.ds(pl.multiple_of(c * chunk, chunk), chunk)
+        total[:, span] = jnp.dot(rows[...], weight[:, span], preferred_element_type=F32)
+
     part = outs[0].shape[0]
     for k in range(n_gx):
         at = pl.multiple_of(lax.rem(where[0] + k, n_gx) * part, part)
         outs[k][...] = total[pl.ds(at, part), :].astype(BF16)
 
 
-def sum_split_body(n_gx, n_gy, n_gz, where, *refs):
+def sum_split_body(n_gx, n_gy, n_gz, *refs):
+    where = position()
     pieces, outs, total = refs[:n_gx], refs[n_gx : n_gx + n_gy], refs[-1]
     value = pieces[0][...].astype(F32)
     for piece in pieces[1:]:
@@ -88,7 +90,8 @@
             outs[k][j] = total[lax.rem(where[1] + k, n_gy) * n_gz + j].astype(BF16)
 
 
-def attend_body(n_gy, n_gz, where, lengths, *refs):
+def attend_body(n_gy, n_gz, lengths, *refs):
+    where = position()
     count = n_gy * n_gz
     pieces, key, value, outs = refs[:count], refs[count], refs[count + 1], refs[count + 2 :]
     each, width = pieces[0].shape[1:]
@@ -121,7 +124,8 @@
                 outs[k][j, :, h * HDIM : (h + 1) * HDIM] = mixed[at : at + each].astype(BF16)
 
 
-def gather_rows_body(n_gy, n_gz, where, *refs):
+def gather_rows_body(n_gy, n_gz, *refs):
+    where = position()
     pieces, out, total = refs[:-2], refs[-2], refs[-1]
     each = pieces[0].shape[1]
     for k in range(n_gy):
@@ -131,28 +135,22 @@
     out[...] = jnp.concatenate([total[i] for i in range(n_gy * n_gz)], axis=0).astype(BF16)
 
 
-def output_body(n_gx, n_gy, n_gz, chunk, where, *refs):
+def output_body(n_gx, n_gy, n_gz, chunk, *refs):
+    where = position()
     pieces, weight = refs[:n_gx], refs[n_gx]
     count = n_gy * n_gz
     outs = refs[n_gx + 1 : n_gx + 1 + count]
-    rows, total, held, sems = refs[n_gx + 1 + count :]
-    chunks = weight.shape[1] // chunk
-
-    def copy(c):
-        span = pl.ds(c * chunk, chunk)
-        return pltpu.make_async_copy(weight.at[:, span], held.at[:, span], sems.at[c])
-
-    for c in range(chunks):
-        copy(c).start()
+    rows, total = refs[n_gx + 1 + count :]
     block = pieces[0].shape[0]
     for k in range(n_gx):
         at = pl.multiple_of(lax.rem(where[0] + n_gx - k, n_gx) * block, block)
         rows[pl.ds(at, block), :] = pieces[k][...]
     part = outs[0].shape[0]
-    for c in range(chunks):
-        copy(c).wait()
-        span = slice(c * chunk, (c + 1) * chunk)
-        total[...] = jnp.dot(rows[...], held[:, span], preferred_element_type=F32)
+
+    @pl.loop(0, weight.shape[1] // chunk)
+    def _(c):
+        span = pl.ds(pl.multiple_of(c * chunk, chunk), chunk)
+        total[...] = jnp.dot(rows[...], weight[:, span], preferred_element_type=F32)
         for k in range(n_gy):
             for j in range(n_gz):
                 at = lax.rem(where[1] + k, n_gy) * n_gz + lax.rem(where[2] + j, n_gz)
@@ -178,7 +176,6 @@
 
 def shards(tokens, q_weight, o_weight, key_cache, value_cache, lengths):
     n_gx, n_gy, n_gz = (lax.axis_size(a) for a in ("gx", "gy", "gz"))
-    where = jnp.stack([lax.axis_index(a) for a in ("gx", "gy", "gz")]).astype(jnp.int32)
     own_rows, depth = tokens.shape
     row_count = own_rows * n_gy * n_gz
     width = q_weight.shape[1]
@@ -186,21 +183,30 @@
     part = row_count // n_gx
     struct = jax.ShapeDtypeStruct
 
+    weight_bytes = 2 * depth * width
+    staged = call(
+        stage_body,
+        [struct(tokens.shape, BF16)],
+        [tokens],
+        [ANY],
+        scratch=[pltpu.SemaphoreType.DMA],
+        beside=3000 * weight_bytes,
+        name="own_tokens",
+    )[0]
     pieces = []
     for k in range(n_gy):
         over = shift(tokens, "gy", k) if k else tokens
         pieces += [shift(over, "gz", j) if j else over for j in range(n_gz)]
-    chunk = largest_divisor(depth, 512, 128)
+    pieces[0] = staged
+    chunk = largest_divisor(width, 256, 128)
     terms = call(
         functools.partial(query_body, n_gx, n_gy, n_gz, chunk),
         [struct((part, width), BF16)] * n_gx,
-        [where, *pieces, q_weight],
-        [SMEM] + [VMEM] * len(pieces) + [ANY],
+        [*pieces, q_weight],
+        [VMEM] * len(pieces) + [VMEM],
         scratch=[
             pltpu.VMEM((row_count, depth), BF16),
             pltpu.VMEM((row_count, width), F32),
-            pltpu.VMEM(q_weight.shape, BF16),
-            pltpu.SemaphoreType.DMA((depth // chunk,)),
         ],
         mib=mib_for(row_count * depth * 4, row_count * width * 8, depth * width * 2),
         flops=2 * row_count * depth * width,
@@ -211,9 +217,10 @@
     queries = call(
         functools.partial(sum_split_body, n_gx, n_gy, n_gz),
         [struct((n_gz, each, width), BF16)] * n_gy,
-        [where, *terms],
-        [SMEM] + [VMEM] * n_gx,
+        [*terms],
+        [VMEM] * n_gx,
         scratch=[pltpu.VMEM((n_gy * n_gz, each, width), F32)],
+        beside=20000 * key_cache.size,
         name="query_sum",
     )
     pieces = []
@@ -223,9 +230,9 @@
     mixed = call(
         functools.partial(attend_body, n_gy, n_gz),
         [struct((n_gz, each, width), BF16)] * n_gy,
-        [where, lengths, *pieces, key_cache, value_cache],
-        [SMEM, SMEM] + [VMEM] * (len(pieces) + 2),
-        mib=24,
+        [lengths, *pieces, key_cache, value_cache],
+        [SMEM] + [VMEM] * (len(pieces) + 2),
+        mib=12,
         name="attention",
     )
 
@@ -236,8 +243,8 @@
     block = call(
         functools.partial(gather_rows_body, n_gy, n_gz),
         [struct((part, width), BF16)],
-        [where, *pieces],
-        [SMEM] + [VMEM] * len(pieces),
+        [*pieces],
+        [VMEM] * len(pieces),
         scratch=[pltpu.VMEM((n_gy * n_gz, each, width), F32)],
         name="mixed_rows",
     )[0]
@@ -247,13 +254,11 @@
     terms = call(
         functools.partial(output_body, n_gx, n_gy, n_gz, chunk),
         [struct((own_rows, columns), BF16)] * (n_gy * n_gz),
-        [where, *blocks, o_weight],
-        [SMEM] + [VMEM] * n_gx + [ANY],
+        [*blocks, o_weight],
+        [VMEM] * n_gx + [VMEM],
         scratch=[
             pltpu.VMEM((row_count, width), BF16),
             pltpu.VMEM((row_count, chunk), F32),
-            pltpu.VMEM(o_weight.shape, BF16),
-            pltpu.SemaphoreType.DMA((columns // chunk,)),
         ],
         mib=mib_for(row_count * width * 4, row_count * (chunk * 4 + columns * 2), columns * width * 2),
         flops=2 * row_count * columns * width,

time: 65.3 us -> 53.3 us (0.82)
  local copies, waits for them, and re-layouts: 8.39 us -> 0.94 us
  Pallas kernels: 13 us -> 9.58 us
  waiting for transfers between devices: 25.8 us -> 24.8 us
    unnamed x12 -> x18, local copies, waits for them, and re-layouts: 8.39 us -> 0.94 us
    pallas_call x7 -> x8, Pallas kernels: 13 us -> 9.58 us  [call(): pl.pallas_call(body, out_shape=list(outs), in_specs=in_specs, out_specs=[...]
    ppermute x18, waiting for transfers between devices: 25.8 us -> 24.8 us  [shift(): lax.ppermute(array, axis, [(s, (s + by) % size) for s in range(size)])]
where the time goes in v2:
time: 53.3 us; the launch traced here: 53.1 us
  waiting for transfers between devices  24.8 us (47%)
  starting transfers between devices  17.6 us (33%)
  Pallas kernels  9.58 us (18%)
  local copies, waits for them, and re-layouts  0.94 us (2%)
    ppermute x18, waiting for transfers between devices, shift(): lax.ppermute(array, axis, [(s, (s + by) % size) for s in range(size)])  24.8 us
    ppermute x18, starting transfers between devices, shift(): lax.ppermute(array, axis, [(s, (s + by) % size) for s in range(size)])  17.6 us
    pallas_call x8, Pallas kernels, call(): pl.pallas_call(body, out_shape=list(outs), in_specs=in_specs, out_specs=[...  9.58 us
  transfers between devices with their start and end apart: 18, of which 14 were waited for; matrix products, arithmetic and copies ran while one was open for 0% of the time, Pallas kernels for 0%

profile of v2, /device:TPU:0, one launch (start us, length us, event | category | flops | bytes accessed | tf_op | source)
XLA Modules:
  0.0 53.1 jit_solution(8828147196878790216)
XLA Ops:
  0.0 2.9 %collective-permute-start.1 = (bf16[16,4608]{1,0:T(8,128)(2,1)}, bf16[16,4608]{1,0:T(8,128)(2,1)S(1)}, u32[]{:S(2)}, u32[]{:S(2)}) collective-permute-start(bf16[16,4608]{1,0:T(8,128)(2,1)} %tokens.1), channel_id=1, source_target_pairs={{0,2},{2,0},{1,3},{3,1},{4,6},{6,4},{5,7},{7,5},{8,10},{10,8},{9,1... | collective-permute-start | bytes 442376 | tf_op jit(solution)/shard_map/ppermute | solution.py:20
  2.9 0.0 collective-permute-start
  2.9 4.1 %collective-permute-done.1.refs_2_ = bf16[16,4608]{1,0:T(8,128)(2,1)S(1)} collective-permute-done((bf16[16,4608]{1,0:T(8,128)(2,1)}, bf16[16,4608]{1,0:T(8,128)(2,1)S(1)}, u32[]{:S(2)}, u32[]{:S(2)}) %collective-permute-start.1) | collective-permute-done | bytes 147488 | tf_op jit(solution)/shard_map/ppermute | solution.py:20
  7.0 0.9 %copy-done.4 = bf16[16,4608]{1,0:T(8,128)(2,1)S(1)} copy-done((bf16[16,4608]{1,0:T(8,128)(2,1)S(1)}, bf16[16,4608]{1,0:T(8,128)(2,1)}, u32[]{:S(2)}) %copy-start.4) | copy-done | bytes 147480
  7.9 0.2 own_tokens.1.refs_0_
  8.1 0.3 collective-permute-done.2.refs_3_
  8.4 3.3 %query_terms.1 = (bf16[16,1536]{1,0:T(8,128)(2,1)S(1)}, bf16[16,1536]{1,0:T(8,128)(2,1)S(1)}, bf16[16,1536]{1,0:T(8,128)(2,1)S(1)}, bf16[16,1536]{1,0:T(8,128)(2,1)S(1)}) custom-call(bf16[16,4608]{1,0:T(8,128)(2,1)S(1)} %own_tokens.1.refs_0_, bf16[16,4608]{1,0:T(8,128)(2,1)S(1)} %collective-permute-done.refs_1_, ...), custom_call_target="tpu_custom_call" | custom-call | flops 905969664 | bytes 14942208 | tf_op jit(solution)/shard_map/query_terms/pallas_call | solution.py:38
  11.7 1.9 %collective-permute-start.3 = (bf16[16,1536]{1,0:T(8,128)(2,1)S(1)}, bf16[16,1536]{1,0:T(8,128)(2,1)S(1)}, u32[]{:S(2)}, u32[]{:S(2)}) collective-permute-start(bf16[16,1536]{1,0:T(8,128)(2,1)S(1)} %get-tuple-element.18), channel_id=1, source_target_pairs={{0,4},{4,8},{8,12},{12,0},{1,5},{5,9},{9,13},{13,1},{2,6},{6,10},{... | collective-permute-start | bytes 147464 | tf_op jit(solution)/shard_map/ppermute | solution.py:20
  13.6 2.6 %collective-permute-start.4 = (bf16[16,1536]{1,0:T(8,128)(2,1)S(1)}, bf16[16,1536]{1,0:T(8,128)(2,1)S(1)}, u32[]{:S(2)}, u32[]{:S(2)}) collective-permute-start(bf16[16,1536]{1,0:T(8,128)(2,1)S(1)} %get-tuple-element.19), channel_id=1, source_target_pairs={{0,8},{4,12},{8,0},{12,4},{1,9},{5,13},{9,1},{13,5},{2,10},{6,14},... | collective-permute-start | bytes 147464 | tf_op jit(solution)/shard_map/ppermute | solution.py:20
  16.2 1.3 %collective-permute-start.5 = (bf16[16,1536]{1,0:T(8,128)(2,1)S(1)}, bf16[16,1536]{1,0:T(8,128)(2,1)S(1)}, u32[]{:S(2)}, u32[]{:S(2)}) collective-permute-start(bf16[16,1536]{1,0:T(8,128)(2,1)S(1)} %get-tuple-element.20), channel_id=1, source_target_pairs={{0,12},{4,0},{8,4},{12,8},{1,13},{5,1},{9,5},{13,9},{2,14},{6,2},{... | collective-permute-start | bytes 147464 | tf_op jit(solution)/shard_map/ppermute | solution.py:20
  17.5 0.3 collective-permute-done.3.refs_1_
  17.9 2.3 %collective-permute-done.4.refs_2_ = bf16[16,1536]{1,0:T(8,128)(2,1)S(1)} collective-permute-done((bf16[16,1536]{1,0:T(8,128)(2,1)S(1)}, bf16[16,1536]{1,0:T(8,128)(2,1)S(1)}, u32[]{:S(2)}, u32[]{:S(2)}) %collective-permute-start.4) | collective-permute-done | bytes 49184 | tf_op jit(solution)/shard_map/ppermute | solution.py:20
  20.2 0.3 collective-permute-done.5.refs_3_
  20.5 1.6 %collective-permute-start.7 = (bf16[2,4,1536]{2,1,0:T(4,128)(2,1)S(1)}, bf16[2,4,1536]{2,1,0:T(4,128)(2,1)S(1)}, u32[]{:S(2)}, u32[]{:S(2)}) collective-permute-start(bf16[2,4,1536]{2,1,0:T(4,128)(2,1)S(1)} %get-tuple-element.22), channel_id=1, source_target_pairs={{0,2},{2,0},{1,3},{3,1},{4,6},{6,4},{5,7},{7,5},{8,10},{10,8},{9,1... | collective-permute-start | bytes 73736 | tf_op jit(solution)/shard_map/ppermute | solution.py:20
  22.1 2.3 %collective-permute-done.7.refs_2_ = bf16[2,4,1536]{2,1,0:T(4,128)(2,1)S(1)} collective-permute-done((bf16[2,4,1536]{2,1,0:T(4,128)(2,1)S(1)}, bf16[2,4,1536]{2,1,0:T(4,128)(2,1)S(1)}, u32[]{:S(2)}, u32[]{:S(2)}) %collective-permute-start.7) | collective-permute-done | bytes 24608 | tf_op jit(solution)/shard_map/ppermute | solution.py:20
  24.4 1.2 %collective-permute-done.8.refs_3_ = bf16[2,4,1536]{2,1,0:T(4,128)(2,1)S(1)} collective-permute-done((bf16[2,4,1536]{2,1,0:T(4,128)(2,1)S(1)}, bf16[2,4,1536]{2,1,0:T(4,128)(2,1)S(1)}, u32[]{:S(2)}, u32[]{:S(2)}) %collective-permute-start.8) | collective-permute-done | bytes 24608 | tf_op jit(solution)/shard_map/ppermute | solution.py:20
  25.6 1.7 %attention.1 = (bf16[2,4,1536]{2,1,0:T(4,128)(2,1)S(1)}, bf16[2,4,1536]{2,1,0:T(4,128)(2,1)S(1)}) custom-call(s32[4]{0:T(128)S(1)} %copy-done.3, bf16[2,4,1536]{2,1,0:T(4,128)(2,1)S(1)} %get-tuple-element.21.refs_0_, bf16[2,4,1536]{2,1,0:T(4,128)(2,1)S(1)} %collective-permute-done.6.refs_1_, bf16[2,4,1536]{2,1,0:T(4,128)(2,1)S(1)} %collective-permute-done.7.refs_2_, ...), custom_call_target="tpu_custom_call" | custom-call | bytes 2244624 | tf_op jit(solution)/shard_map/attention/pallas_call | solution.py:38
  27.3 1.6 %collective-permute-start.10 = (bf16[2,4,1536]{2,1,0:T(4,128)(2,1)S(1)}, bf16[2,4,1536]{2,1,0:T(4,128)(2,1)S(1)}, u32[]{:S(2)}, u32[]{:S(2)}) collective-permute-start(bf16[2,4,1536]{2,1,0:T(4,128)(2,1)S(1)} %get-tuple-element.24), channel_id=1, source_target_pairs={{0,2},{2,0},{1,3},{3,1},{4,6},{6,4},{5,7},{7,5},{8,10},{10,8},{9,1... | collective-permute-start | bytes 73736 | tf_op jit(solution)/shard_map/ppermute | solution.py:20
  28.9 2.3 %collective-permute-done.10.refs_2_ = bf16[2,4,1536]{2,1,0:T(4,128)(2,1)S(1)} collective-permute-done((bf16[2,4,1536]{2,1,0:T(4,128)(2,1)S(1)}, bf16[2,4,1536]{2,1,0:T(4,128)(2,1)S(1)}, u32[]{:S(2)}, u32[]{:S(2)}) %collective-permute-start.10) | collective-permute-done | bytes 24608 | tf_op jit(solution)/shard_map/ppermute | solution.py:20
  31.2 1.2 %collective-permute-done.11.refs_3_ = bf16[2,4,1536]{2,1,0:T(4,128)(2,1)S(1)} collective-permute-done((bf16[2,4,1536]{2,1,0:T(4,128)(2,1)S(1)}, bf16[2,4,1536]{2,1,0:T(4,128)(2,1)S(1)}, u32[]{:S(2)}, u32[]{:S(2)}) %collective-permute-start.11) | collective-permute-done | bytes 24608 | tf_op jit(solution)/shard_map/ppermute | solution.py:20
  32.4 3.0 %collective-permute-start.14 = (bf16[16,1536]{1,0:T(8,128)(2,1)S(1)}, bf16[16,1536]{1,0:T(8,128)(2,1)S(1)}, u32[]{:S(2)}, u32[]{:S(2)}) collective-permute-start(bf16[16,1536]{1,0:T(8,128)(2,1)S(1)} %mixed_rows.1.refs_0_), channel_id=1, source_target_pairs={{0,12},{4,0},{8,4},{12,8},{1,13},{5,1},{9,5},{13,9},{2,14},{6,2},{... | collective-permute-start | bytes 147464 | tf_op jit(solution)/shard_map/ppermute | solution.py:20
  35.4 0.6 %collective-permute-start.12 = (bf16[16,1536]{1,0:T(8,128)(2,1)S(1)}, bf16[16,1536]{1,0:T(8,128)(2,1)S(1)}, u32[]{:S(2)}, u32[]{:S(2)}) collective-permute-start(bf16[16,1536]{1,0:T(8,128)(2,1)S(1)} %mixed_rows.1.refs_0_), channel_id=1, source_target_pairs={{0,4},{4,8},{8,12},{12,0},{1,5},{5,9},{9,13},{13,1},{2,6},{6,10},{... | collective-permute-start | bytes 147464 | tf_op jit(solution)/shard_map/ppermute | solution.py:20
  36.1 1.5 %collective-permute-done.14.refs_3_ = bf16[16,1536]{1,0:T(8,128)(2,1)S(1)} collective-permute-done((bf16[16,1536]{1,0:T(8,128)(2,1)S(1)}, bf16[16,1536]{1,0:T(8,128)(2,1)S(1)}, u32[]{:S(2)}, u32[]{:S(2)}) %collective-permute-start.14) | collective-permute-done | bytes 49184 | tf_op jit(solution)/shard_map/ppermute | solution.py:20
  37.6 3.2 %collective-permute-done.13.refs_2_ = bf16[16,1536]{1,0:T(8,128)(2,1)S(1)} collective-permute-done((bf16[16,1536]{1,0:T(8,128)(2,1)S(1)}, bf16[16,1536]{1,0:T(8,128)(2,1)S(1)}, u32[]{:S(2)}, u32[]{:S(2)}) %collective-permute-start.13) | collective-permute-done | bytes 49184 | tf_op jit(solution)/shard_map/ppermute | solution.py:20
  40.8 0.6 %collective-permute-done.12.refs_1_ = bf16[16,1536]{1,0:T(8,128)(2,1)S(1)} collective-permute-done((bf16[16,1536]{1,0:T(8,128)(2,1)S(1)}, bf16[16,1536]{1,0:T(8,128)(2,1)S(1)}, u32[]{:S(2)}, u32[]{:S(2)}) %collective-permute-start.12) | collective-permute-done | bytes 49184 | tf_op jit(solution)/shard_map/ppermute | solution.py:20
  41.4 3.6 %output_terms.1 = (bf16[16,4608]{1,0:T(8,128)(2,1)S(1)}, bf16[16,4608]{1,0:T(8,128)(2,1)S(1)}, bf16[16,4608]{1,0:T(8,128)(2,1)S(1)}, bf16[16,4608]{1,0:T(8,128)(2,1)S(1)}) custom-call(bf16[16,1536]{1,0:T(8,128)(2,1)S(1)} %mixed_rows.1.refs_0_, bf16[16,1536]{1,0:T(8,128)(2,1)S(1)} %collective-permute-done.12.refs_1_, ...), custom_call_target="tpu_custom_call" | custom-call | flops 905969664 | bytes 14942208 | tf_op jit(solution)/shard_map/output_terms/pallas_call | solution.py:38
  45.0 0.1 collective-permute-start.16
  45.0 0.5 collective-permute-start.15
  45.5 0.9 %collective-permute-done.16.refs_1_ = bf16[16,4608]{1,0:T(8,128)(2,1)S(1)} collective-permute-done((bf16[16,4608]{1,0:T(8,128)(2,1)S(1)}, bf16[16,4608]{1,0:T(8,128)(2,1)S(1)}, u32[]{:S(2)}, u32[]{:S(2)}) %collective-permute-start.16) | collective-permute-done | bytes 147488 | tf_op jit(solution)/shard_map/ppermute | solution.py:20
  46.4 1.6 %collective-permute-start.17 = (bf16[16,4608]{1,0:T(8,128)(2,1)S(1)}, bf16[16,4608]{1,0:T(8,128)(2,1)S(1)}, u32[]{:S(2)}, u32[]{:S(2)}) collective-permute-start(bf16[16,4608]{1,0:T(8,128)(2,1)S(1)} %pair_sum.1), channel_id=1, source_target_pairs={{0,2},{2,0},{1,3},{3,1},{4,6},{6,4},{5,7},{7,5},{8,10},{10,8},{9,1... | collective-permute-start | bytes 442376 | tf_op jit(solution)/shard_map/ppermute | solution.py:20
  48.0 4.4 %collective-permute-done.17.refs_2_ = bf16[16,4608]{1,0:T(8,128)(2,1)S(1)} collective-permute-done((bf16[16,4608]{1,0:T(8,128)(2,1)S(1)}, bf16[16,4608]{1,0:T(8,128)(2,1)S(1)}, u32[]{:S(2)}, u32[]{:S(2)}) %collective-permute-start.17) | collective-permute-done | bytes 147488 | tf_op jit(solution)/shard_map/ppermute | solution.py:20
  52.4 0.7 %output_sum.1 = bf16[16,4608]{1,0:T(8,128)(2,1)} custom-call(bf16[16,4608]{1,0:T(8,128)(2,1)S(1)} %get-tuple-element.25.refs_0_, bf16[16,4608]{1,0:T(8,128)(2,1)S(1)} %collective-permute-done.15.refs_1_, bf16[16,4608]{1,0:T(8,128)(2,1)S(1)} %collective-permute-done.17.refs_2_), custom_call_target="tpu_custom_call" | custom-call | bytes 589824 | tf_op jit(solution)/shard_map/output_sum/pallas_call | solution.py:38
  (31 shorter events, 0.2 us)
Async XLA Ops:
  0.0 8.4 %copy-start = (bf16[4608,1536]{1,0:T(8,128)(2,1)S(1)}, bf16[4608,1536]{1,0:T(8,128)(2,1)}, u32[]{:S(2)}) copy-start(bf16[4608,1536]{1,0:T(8,128)(2,1)} %refs_4_.3) | copy-start | bytes 42467332
  0.0 7.0 %collective-permute-start.1 = (bf16[16,4608]{1,0:T(8,128)(2,1)}, bf16[16,4608]{1,0:T(8,128)(2,1)S(1)}, u32[]{:S(2)}, u32[]{:S(2)}) collective-permute-start(bf16[16,4608]{1,0:T(8,128)(2,1)} %tokens.1), channel_id=1, source_target_pairs={{0,2},{2,0},{1,3},{3,1},{4,6},{6,4},{5,7},{7,5},{8,10},{10,8},{9,1... | collective-permute-start | bytes 442376 | tf_op jit(solution)/shard_map/ppermute | solution.py:20
  2.9 5.1 %collective-permute-start = (bf16[16,4608]{1,0:T(8,128)(2,1)}, bf16[16,4608]{1,0:T(8,128)(2,1)S(1)}, u32[]{:S(2)}, u32[]{:S(2)}) collective-permute-start(bf16[16,4608]{1,0:T(8,128)(2,1)} %tokens.1), channel_id=1, source_target_pairs={{0,1},{1,0},{2,3},{3,2},{4,5},{5,4},{6,7},{7,6},{8,9},{9,8},{10,11... | collective-permute-start | bytes 442376 | tf_op jit(solution)/shard_map/ppermute | solution.py:20
  7.0 1.4 %collective-permute-start.2 = (bf16[16,4608]{1,0:T(8,128)(2,1)S(1)}, bf16[16,4608]{1,0:T(8,128)(2,1)S(1)}, u32[]{:S(2)}, u32[]{:S(2)}) collective-permute-start(bf16[16,4608]{1,0:T(8,128)(2,1)S(1)} %collective-permute-done.1.refs_2_), channel_id=1, source_target_pairs={{0,1},{1,0},{2,3},{3,2},{4,5},{5,4},{6,7},{7,6},{8,9},{9,8},{10,11... | collective-permute-start | bytes 442376 | tf_op jit(solution)/shard_map/ppermute | solution.py:20
  7.0 0.9 %copy-start.4 = (bf16[16,4608]{1,0:T(8,128)(2,1)S(1)}, bf16[16,4608]{1,0:T(8,128)(2,1)}, u32[]{:S(2)}) copy-start(bf16[16,4608]{1,0:T(8,128)(2,1)} %tokens.1) | copy-start | bytes 442372
  8.4 33.0 %slice-start = ((s8[14155776]{0:T(1024)(128)(4,1)}), s8[1572864]{0:T(1024)(128)(4,1)S(1)}, s32[]{:S(2)}) async-start(s8[14155776]{0:T(1024)(128)(4,1)} %bitcast), calls=%async_computation | async-start | bytes 3145728
  8.4 33.0 %slice-start.1 = ((s8[14155776]{0:T(1024)(128)(4,1)}), s8[4194304]{0:T(1024)(128)(4,1)S(1)}, s32[]{:S(2)}) async-start(s8[14155776]{0:T(1024)(128)(4,1)} %bitcast), calls=%async_computation.1 | async-start | bytes 8388608
  11.7 6.2 %collective-permute-start.3 = (bf16[16,1536]{1,0:T(8,128)(2,1)S(1)}, bf16[16,1536]{1,0:T(8,128)(2,1)S(1)}, u32[]{:S(2)}, u32[]{:S(2)}) collective-permute-start(bf16[16,1536]{1,0:T(8,128)(2,1)S(1)} %get-tuple-element.18), channel_id=1, source_target_pairs={{0,4},{4,8},{8,12},{12,0},{1,5},{5,9},{9,13},{13,1},{2,6},{6,10},{... | collective-permute-start | bytes 147464 | tf_op jit(solution)/shard_map/ppermute | solution.py:20
  13.6 6.6 %collective-permute-start.4 = (bf16[16,1536]{1,0:T(8,128)(2,1)S(1)}, bf16[16,1536]{1,0:T(8,128)(2,1)S(1)}, u32[]{:S(2)}, u32[]{:S(2)}) collective-permute-start(bf16[16,1536]{1,0:T(8,128)(2,1)S(1)} %get-tuple-element.19), channel_id=1, source_target_pairs={{0,8},{4,12},{8,0},{12,4},{1,9},{5,13},{9,1},{13,5},{2,10},{6,14},... | collective-permute-start | bytes 147464 | tf_op jit(solution)/shard_map/ppermute | solution.py:20
  16.2 4.3 %collective-permute-start.5 = (bf16[16,1536]{1,0:T(8,128)(2,1)S(1)}, bf16[16,1536]{1,0:T(8,128)(2,1)S(1)}, u32[]{:S(2)}, u32[]{:S(2)}) collective-permute-start(bf16[16,1536]{1,0:T(8,128)(2,1)S(1)} %get-tuple-element.20), channel_id=1, source_target_pairs={{0,12},{4,0},{8,4},{12,8},{1,13},{5,1},{9,5},{13,9},{2,14},{6,2},{... | collective-permute-start | bytes 147464 | tf_op jit(solution)/shard_map/ppermute | solution.py:20
  20.5 5.2 %copy-start.1 = (bf16[4,512,256]{2,1,0:T(8,128)(2,1)S(1)}, bf16[4,512,256]{2,1,0:T(8,128)(2,1)}, u32[]{:S(2)}) copy-start(bf16[4,512,256]{2,1,0:T(8,128)(2,1)} %refs_4_.4) | copy-start | bytes 3145732
  20.5 5.2 %copy-start.2 = (bf16[4,512,256]{2,1,0:T(8,128)(2,1)S(1)}, bf16[4,512,256]{2,1,0:T(8,128)(2,1)}, u32[]{:S(2)}) copy-start(bf16[4,512,256]{2,1,0:T(8,128)(2,1)} %refs_5_.1) | copy-start | bytes 3145732
  20.5 5.2 %copy-start.3 = (s32[4]{0:T(128)S(1)}, s32[4]{0:T(128)}, u32[]{:S(2)}) copy-start(s32[4]{0:T(128)} %lengths.1) | copy-start | bytes 52
  20.5 20.9 %slice-start.2 = ((s8[14155776]{0:T(1024)(128)(4,1)}), s8[4194304]{0:T(1024)(128)(4,1)S(1)}, s32[]{:S(2)}) async-start(s8[14155776]{0:T(1024)(128)(4,1)} %bitcast), calls=%async_computation.2 | async-start | bytes 8388608
  20.5 20.9 %slice-start.3 = ((s8[14155776]{0:T(1024)(128)(4,1)}), s8[4194304]{0:T(1024)(128)(4,1)S(1)}, s32[]{:S(2)}) async-start(s8[14155776]{0:T(1024)(128)(4,1)} %bitcast), calls=%async_computation.3 | async-start | bytes 8388608
  20.5 3.9 %collective-permute-start.7 = (bf16[2,4,1536]{2,1,0:T(4,128)(2,1)S(1)}, bf16[2,4,1536]{2,1,0:T(4,128)(2,1)S(1)}, u32[]{:S(2)}, u32[]{:S(2)}) collective-permute-start(bf16[2,4,1536]{2,1,0:T(4,128)(2,1)S(1)} %get-tuple-element.22), channel_id=1, source_target_pairs={{0,2},{2,0},{1,3},{3,1},{4,6},{6,4},{5,7},{7,5},{8,10},{10,8},{9,1... | collective-permute-start | bytes 73736 | tf_op jit(solution)/shard_map/ppermute | solution.py:20
  22.1 2.3 %collective-permute-start.6 = (bf16[2,4,1536]{2,1,0:T(4,128)(2,1)S(1)}, bf16[2,4,1536]{2,1,0:T(4,128)(2,1)S(1)}, u32[]{:S(2)}, u32[]{:S(2)}) collective-permute-start(bf16[2,4,1536]{2,1,0:T(4,128)(2,1)S(1)} %get-tuple-element.21.refs_0_), channel_id=1, source_target_pairs={{0,1},{1,0},{2,3},{3,2},{4,5},{5,4},{6,7},{7,6},{8,9},{9,8},{10,11... | collective-permute-start | bytes 73736 | tf_op jit(solution)/shard_map/ppermute | solution.py:20
  24.4 1.2 %collective-permute-start.8 = (bf16[2,4,1536]{2,1,0:T(4,128)(2,1)S(1)}, bf16[2,4,1536]{2,1,0:T(4,128)(2,1)S(1)}, u32[]{:S(2)}, u32[]{:S(2)}) collective-permute-start(bf16[2,4,1536]{2,1,0:T(4,128)(2,1)S(1)} %collective-permute-done.7.refs_2_), channel_id=1, source_target_pairs={{0,1},{1,0},{2,3},{3,2},{4,5},{5,4},{6,7},{7,6},{8,9},{9,8},{10,11... | collective-permute-start | bytes 73736 | tf_op jit(solution)/shard_map/ppermute | solution.py:20
  27.3 3.9 %collective-permute-start.10 = (bf16[2,4,1536]{2,1,0:T(4,128)(2,1)S(1)}, bf16[2,4,1536]{2,1,0:T(4,128)(2,1)S(1)}, u32[]{:S(2)}, u32[]{:S(2)}) collective-permute-start(bf16[2,4,1536]{2,1,0:T(4,128)(2,1)S(1)} %get-tuple-element.24), channel_id=1, source_target_pairs={{0,2},{2,0},{1,3},{3,1},{4,6},{6,4},{5,7},{7,5},{8,10},{10,8},{9,1... | collective-permute-start | bytes 73736 | tf_op jit(solution)/shard_map/ppermute | solution.py:20
  28.9 2.3 %collective-permute-start.9 = (bf16[2,4,1536]{2,1,0:T(4,128)(2,1)S(1)}, bf16[2,4,1536]{2,1,0:T(4,128)(2,1)S(1)}, u32[]{:S(2)}, u32[]{:S(2)}) collective-permute-start(bf16[2,4,1536]{2,1,0:T(4,128)(2,1)S(1)} %get-tuple-element.23.refs_0_), channel_id=1, source_target_pairs={{0,1},{1,0},{2,3},{3,2},{4,5},{5,4},{6,7},{7,6},{8,9},{9,8},{10,11... | collective-permute-start | bytes 73736 | tf_op jit(solution)/shard_map/ppermute | solution.py:20
  31.2 1.2 %collective-permute-start.11 = (bf16[2,4,1536]{2,1,0:T(4,128)(2,1)S(1)}, bf16[2,4,1536]{2,1,0:T(4,128)(2,1)S(1)}, u32[]{:S(2)}, u32[]{:S(2)}) collective-permute-start(bf16[2,4,1536]{2,1,0:T(4,128)(2,1)S(1)} %collective-permute-done.10.refs_2_), channel_id=1, source_target_pairs={{0,1},{1,0},{2,3},{3,2},{4,5},{5,4},{6,7},{7,6},{8,9},{9,8},{10,11... | collective-permute-start | bytes 73736 | tf_op jit(solution)/shard_map/ppermute | solution.py:20
  32.4 5.1 %collective-permute-start.14 = (bf16[16,1536]{1,0:T(8,128)(2,1)S(1)}, bf16[16,1536]{1,0:T(8,128)(2,1)S(1)}, u32[]{:S(2)}, u32[]{:S(2)}) collective-permute-start(bf16[16,1536]{1,0:T(8,128)(2,1)S(1)} %mixed_rows.1.refs_0_), channel_id=1, source_target_pairs={{0,12},{4,0},{8,4},{12,8},{1,13},{5,1},{9,5},{13,9},{2,14},{6,2},{... | collective-permute-start | bytes 147464 | tf_op jit(solution)/shard_map/ppermute | solution.py:20
  35.4 5.3 %collective-permute-start.13 = (bf16[16,1536]{1,0:T(8,128)(2,1)S(1)}, bf16[16,1536]{1,0:T(8,128)(2,1)S(1)}, u32[]{:S(2)}, u32[]{:S(2)}) collective-permute-start(bf16[16,1536]{1,0:T(8,128)(2,1)S(1)} %mixed_rows.1.refs_0_), channel_id=1, source_target_pairs={{0,8},{4,12},{8,0},{12,4},{1,9},{5,13},{9,1},{13,5},{2,10},{6,14},... | collective-permute-start | bytes 147464 | tf_op jit(solution)/shard_map/ppermute | solution.py:20
  35.4 5.9 %collective-permute-start.12 = (bf16[16,1536]{1,0:T(8,128)(2,1)S(1)}, bf16[16,1536]{1,0:T(8,128)(2,1)S(1)}, u32[]{:S(2)}, u32[]{:S(2)}) collective-permute-start(bf16[16,1536]{1,0:T(8,128)(2,1)S(1)} %mixed_rows.1.refs_0_), channel_id=1, source_target_pairs={{0,4},{4,8},{8,12},{12,0},{1,5},{5,9},{9,13},{13,1},{2,6},{6,10},{... | collective-permute-start | bytes 147464 | tf_op jit(solution)/shard_map/ppermute | solution.py:20
  45.0 1.4 %collective-permute-start.16 = (bf16[16,4608]{1,0:T(8,128)(2,1)S(1)}, bf16[16,4608]{1,0:T(8,128)(2,1)S(1)}, u32[]{:S(2)}, u32[]{:S(2)}) collective-permute-start(bf16[16,4608]{1,0:T(8,128)(2,1)S(1)} %get-tuple-element.28), channel_id=1, source_target_pairs={{0,1},{1,0},{2,3},{3,2},{4,5},{5,4},{6,7},{7,6},{8,9},{9,8},{10,11... | collective-permute-start | bytes 442376 | tf_op jit(solution)/shard_map/ppermute | solution.py:20
  45.0 3.0 %collective-permute-start.15 = (bf16[16,4608]{1,0:T(8,128)(2,1)S(1)}, bf16[16,4608]{1,0:T(8,128)(2,1)S(1)}, u32[]{:S(2)}, u32[]{:S(2)}) collective-permute-start(bf16[16,4608]{1,0:T(8,128)(2,1)S(1)} %get-tuple-element.26), channel_id=1, source_target_pairs={{0,1},{1,0},{2,3},{3,2},{4,5},{5,4},{6,7},{7,6},{8,9},{9,8},{10,11... | collective-permute-start | bytes 442376 | tf_op jit(solution)/shard_map/ppermute | solution.py:20
  46.4 6.0 %collective-permute-start.17 = (bf16[16,4608]{1,0:T(8,128)(2,1)S(1)}, bf16[16,4608]{1,0:T(8,128)(2,1)S(1)}, u32[]{:S(2)}, u32[]{:S(2)}) collective-permute-start(bf16[16,4608]{1,0:T(8,128)(2,1)S(1)} %pair_sum.1), channel_id=1, source_target_pairs={{0,2},{2,0},{1,3},{3,1},{4,6},{6,4},{5,7},{7,5},{8,10},{10,8},{9,1... | collective-permute-start | bytes 442376 | tf_op jit(solution)/shard_map/ppermute | solution.py:20

commit v3 on v2

--- a/solution.py
+++ b/solution.py
@@ -90,48 +90,54 @@
             outs[k][j] = total[lax.rem(where[1] + k, n_gy) * n_gz + j].astype(BF16)
 
 
-def attend_body(n_gy, n_gz, lengths, *refs):
-    where = position()
-    count = n_gy * n_gz
-    pieces, key, value, outs = refs[:count], refs[count], refs[count + 1], refs[count + 2 :]
+def attend_body(n_gy, n_gz, *refs):
+    where = position()
+    lengths, pieces, rest = refs[:n_gz], refs[n_gz : n_gz + n_gy], refs[n_gz + n_gy :]
+    keys, values = rest[:n_gz], rest[n_gz : 2 * n_gz]
+    outs, held, given = rest[2 * n_gz : -2], rest[-2], rest[-1]
     each, width = pieces[0].shape[1:]
     heads = width // HDIM
-    stacked = []
-    for piece in pieces:
-        mine = piece[where[2]].astype(F32)
-        stacked += [mine[:, h * HDIM : (h + 1) * HDIM] for h in range(heads)]
-    query = jnp.concatenate(stacked, axis=0).astype(BF16)
-    cache = key.shape[1]
-    keys = key[...].reshape(each * cache, HDIM)
-    values = value[...].reshape(each * cache, HDIM)
-    scores = lax.dot_general(query, keys, (((1,), (1,)), ((), ())), preferred_element_type=F32)
-    scores = scores * HDIM ** (-0.5)
-    row = lax.rem(lax.broadcasted_iota(jnp.int32, scores.shape, 0), each)
-    place = lax.broadcasted_iota(jnp.int32, scores.shape, 1) - row * cache
-    used = jnp.zeros((scores.shape[0], 1), jnp.int32)
-    row_of = lax.rem(lax.broadcasted_iota(jnp.int32, (scores.shape[0], 1), 0), each)
-    for r in range(each):
-        used = jnp.where(row_of == r, lengths[r], used)
-    scores = jnp.where((place >= 0) & (place < used), scores, -jnp.inf)
-    raised = jnp.exp(scores - jnp.max(scores, axis=1, keepdims=True))
-    totals = jnp.sum(raised, axis=1, keepdims=True)
-    mixed = jnp.dot(raised.astype(BF16), values, preferred_element_type=F32) / totals
+    lines = n_gy * heads
+    half = held.shape[-1]
+    halves = range(HDIM // half)
+    sources = [lax.rem(where[2] + n_gz - j, n_gz) for j in range(n_gz)]
+    for j in range(n_gz):
+        for k in range(n_gy):
+            mine = pieces[k][sources[j]].astype(F32)
+            for h in range(heads):
+                line = (k * heads + h) * each
+                for p in halves:
+                    at = h * HDIM + p * half
+                    held[j, p, line : line + each, :] = mine[:, at : at + half]
+    rows = [(j, r) for j in range(n_gz) for r in range(each)]
+    scores = []
+    for j, r in rows:
+        span = pl.ds(r, lines, stride=each)
+        query = jnp.concatenate([held[j, p, span, :] for p in halves], axis=1).astype(BF16)
+        score = lax.dot_general(query, keys[j][r], (((1,), (1,)), ((), ())), preferred_element_type=F32)
+        place = lax.broadcasted_iota(jnp.int32, score.shape, 1)
+        scores.append(jnp.where(place < lengths[j][r], score * HDIM ** (-0.5), -jnp.inf))
+    raised = [jnp.exp(score - jnp.max(score, axis=1, keepdims=True)) for score in scores]
+    totals = [jnp.sum(weight, axis=1, keepdims=True) for weight in raised]
+    for (j, r), weight, total in zip(rows, raised, totals):
+        mixed = jnp.dot(weight.astype(BF16), values[j][r], preferred_element_type=F32) / total
+        for p in halves:
+            given[j, p, pl.ds(r, lines, stride=each), :] = mixed[:, p * half : (p + 1) * half]
+    for j in range(n_gz):
+        for k in range(n_gy):
+            for h in range(heads):
+                line = ((n_gy - k) % n_gy * heads + h) * each
+                for p in halves:
+                    at = h * HDIM + p * half
+                    outs[k][sources[j], :, at : at + half] = given[j, p, line : line + each, :].astype(BF16)
+
+
+def gather_rows_body(n_gy, n_gz, *refs):
+    where = position()
+    pieces, out, total = refs[:-2], refs[-2], refs[-1]
     for k in range(n_gy):
         for j in range(n_gz):
-            source = ((n_gy - k) % n_gy) * n_gz + (n_gz - j) % n_gz
-            for h in range(heads):
-                at = (source * heads + h) * each
-                outs[k][j, :, h * HDIM : (h + 1) * HDIM] = mixed[at : at + each].astype(BF16)
-
-
-def gather_rows_body(n_gy, n_gz, *refs):
-    where = position()
-    pieces, out, total = refs[:-2], refs[-2], refs[-1]
-    each = pieces[0].shape[1]
-    for k in range(n_gy):
-        for j in range(n_gz):
-            at = lax.rem(where[1] + n_gy - k, n_gy) * n_gz + lax.rem(where[2] + n_gz - j, n_gz)
-            total[at] = pieces[k * n_gz + j][j].astype(F32)
+            total[lax.rem(where[1] + n_gy - k, n_gy) * n_gz + j] = pieces[k][j].astype(F32)
     out[...] = jnp.concatenate([total[i] for i in range(n_gy * n_gz)], axis=0).astype(BF16)
 
 
@@ -198,6 +204,9 @@
         over = shift(tokens, "gy", k) if k else tokens
         pieces += [shift(over, "gz", j) if j else over for j in range(n_gz)]
     pieces[0] = staged
+    chip_keys, chip_values, chip_lengths = (
+        [array] + [shift(array, "gz", j) for j in range(1, n_gz)] for array in (key_cache, value_cache, lengths)
+    )
     chunk = largest_divisor(width, 256, 128)
     terms = call(
         functools.partial(query_body, n_gx, n_gy, n_gz, chunk),
@@ -223,28 +232,23 @@
         beside=20000 * key_cache.size,
         name="query_sum",
     )
-    pieces = []
-    for k in range(n_gy):
-        over = shift(queries[k], "gy", k) if k else queries[k]
-        pieces += [shift(over, "gz", j) if j else over for j in range(n_gz)]
+    pieces = [shift(queries[k], "gy", k) if k else queries[k] for k in range(n_gy)]
     mixed = call(
         functools.partial(attend_body, n_gy, n_gz),
         [struct((n_gz, each, width), BF16)] * n_gy,
-        [lengths, *pieces, key_cache, value_cache],
-        [SMEM] + [VMEM] * (len(pieces) + 2),
+        [*chip_lengths, *pieces, *chip_keys, *chip_values],
+        [SMEM] * n_gz + [VMEM] * (n_gy + 2 * n_gz),
+        scratch=[pltpu.VMEM((n_gz, HDIM // 128, n_gy * width // HDIM * each, 128), F32)] * 2,
         mib=12,
         name="attention",
     )
 
-    pieces = []
-    for k in range(n_gy):
-        over = shift(mixed[k], "gy", k) if k else mixed[k]
-        pieces += [shift(over, "gz", j) if j else over for j in range(n_gz)]
+    pieces = [shift(mixed[k], "gy", k) if k else mixed[k] for k in range(n_gy)]
     block = call(
         functools.partial(gather_rows_body, n_gy, n_gz),
         [struct((part, width), BF16)],
-        [*pieces],
-        [VMEM] * len(pieces),
+        pieces,
+        [VMEM] * n_gy,
         scratch=[pltpu.VMEM((n_gy * n_gz, each, width), F32)],
         name="mixed_rows",
     )[0]

time: 53.3 us -> 50.7 us (0.951)
  waiting for transfers between devices: 24.8 us -> 21.9 us
  starting transfers between devices: 17.6 us -> 18.2 us
    ppermute x18 -> x17, waiting for transfers between devices: 24.8 us -> 21.9 us  [shift(): lax.ppermute(array, axis, [(s, (s + by) % size) for s in range(size)])]
    ppermute x18 -> x17, starting transfers between devices: 17.6 us -> 18.2 us  [shift(): lax.ppermute(array, axis, [(s, (s + by) % size) for s in range(size)])]
  transfers between devices with their start and end apart: 18 -> 17, of which waited for: 14 -> 12; matrix products, arithmetic and copies ran while one was open for 0% -> 0% of each run, Pallas kernels for 0% -> 0%
where the time goes in v3:
time: 50.7 us; the launch traced here: 50.5 us
  waiting for transfers between devices  21.9 us (43%)
  starting transfers between devices  18.2 us (36%)
  Pallas kernels  9.4 us (19%)
  local copies, waits for them, and re-layouts  0.95 us (2%)
    ppermute x17, waiting for transfers between devices, shift(): lax.ppermute(array, axis, [(s, (s + by) % size) for s in range(size)])  21.9 us
    ppermute x17, starting transfers between devices, shift(): lax.ppermute(array, axis, [(s, (s + by) % size) for s in range(size)])  18.2 us
    pallas_call x8, Pallas kernels, call(): pl.pallas_call(body, out_shape=list(outs), in_specs=in_specs, out_specs=[...  9.4 us
  transfers between devices with their start and end apart: 17, of which 12 were waited for; matrix products, arithmetic and copies ran while one was open for 0% of the time, Pallas kernels for 0%

profile of v3, /device:TPU:0, one launch (start us, length us, event | category | flops | bytes accessed | tf_op | source)
XLA Modules:
  0.0 50.5 jit_solution(4804553664719826424)
XLA Ops:
  0.0 2.9 %collective-permute-start.2 = (bf16[16,4608]{1,0:T(8,128)(2,1)}, bf16[16,4608]{1,0:T(8,128)(2,1)S(1)}, u32[]{:S(2)}, u32[]{:S(2)}) collective-permute-start(bf16[16,4608]{1,0:T(8,128)(2,1)} %tokens.1), channel_id=1, source_target_pairs={{0,2},{2,0},{1,3},{3,1},{4,6},{6,4},{5,7},{7,5},{8,10},{10,8},{9,1... | collective-permute-start | bytes 442376 | tf_op jit(solution)/shard_map/ppermute | solution.py:20
  2.9 4.1 %collective-permute-done.2.refs_2_ = bf16[16,4608]{1,0:T(8,128)(2,1)S(1)} collective-permute-done((bf16[16,4608]{1,0:T(8,128)(2,1)}, bf16[16,4608]{1,0:T(8,128)(2,1)S(1)}, u32[]{:S(2)}, u32[]{:S(2)}) %collective-permute-start.2) | collective-permute-done | bytes 147488 | tf_op jit(solution)/shard_map/ppermute | solution.py:20
  7.0 0.9 %copy-done.4 = bf16[16,4608]{1,0:T(8,128)(2,1)S(1)} copy-done((bf16[16,4608]{1,0:T(8,128)(2,1)S(1)}, bf16[16,4608]{1,0:T(8,128)(2,1)}, u32[]{:S(2)}) %copy-start.4) | copy-done | bytes 147480
  7.9 0.2 own_tokens.1.refs_0_
  8.1 0.0 copy-start.1
  8.1 0.0 copy-start.2
  8.1 0.2 collective-permute-done.3.refs_3_
  8.4 3.3 %query_terms.1 = (bf16[16,1536]{1,0:T(8,128)(2,1)S(1)}, bf16[16,1536]{1,0:T(8,128)(2,1)S(1)}, bf16[16,1536]{1,0:T(8,128)(2,1)S(1)}, bf16[16,1536]{1,0:T(8,128)(2,1)S(1)}) custom-call(bf16[16,4608]{1,0:T(8,128)(2,1)S(1)} %own_tokens.1.refs_0_, bf16[16,4608]{1,0:T(8,128)(2,1)S(1)} %collective-permute-done.1.refs_1_, ...), custom_call_target="tpu_custom_call" | custom-call | flops 905969664 | bytes 14942208 | tf_op jit(solution)/shard_map/query_terms/pallas_call | solution.py:38
  11.7 1.9 %collective-permute-start.4 = (bf16[16,1536]{1,0:T(8,128)(2,1)S(1)}, bf16[16,1536]{1,0:T(8,128)(2,1)S(1)}, u32[]{:S(2)}, u32[]{:S(2)}) collective-permute-start(bf16[16,1536]{1,0:T(8,128)(2,1)S(1)} %get-tuple-element.18), channel_id=1, source_target_pairs={{0,4},{4,8},{8,12},{12,0},{1,5},{5,9},{9,13},{13,1},{2,6},{6,10},{... | collective-permute-start | bytes 147464 | tf_op jit(solution)/shard_map/ppermute | solution.py:20
  13.6 2.6 %collective-permute-start.5 = (bf16[16,1536]{1,0:T(8,128)(2,1)S(1)}, bf16[16,1536]{1,0:T(8,128)(2,1)S(1)}, u32[]{:S(2)}, u32[]{:S(2)}) collective-permute-start(bf16[16,1536]{1,0:T(8,128)(2,1)S(1)} %get-tuple-element.19), channel_id=1, source_target_pairs={{0,8},{4,12},{8,0},{12,4},{1,9},{5,13},{9,1},{13,5},{2,10},{6,14},... | collective-permute-start | bytes 147464 | tf_op jit(solution)/shard_map/ppermute | solution.py:20
  16.2 1.3 %collective-permute-start.6 = (bf16[16,1536]{1,0:T(8,128)(2,1)S(1)}, bf16[16,1536]{1,0:T(8,128)(2,1)S(1)}, u32[]{:S(2)}, u32[]{:S(2)}) collective-permute-start(bf16[16,1536]{1,0:T(8,128)(2,1)S(1)} %get-tuple-element.20), channel_id=1, source_target_pairs={{0,12},{4,0},{8,4},{12,8},{1,13},{5,1},{9,5},{13,9},{2,14},{6,2},{... | collective-permute-start | bytes 147464 | tf_op jit(solution)/shard_map/ppermute | solution.py:20
  17.5 0.5 collective-permute-start.9
  18.0 2.1 %collective-permute-done.5.refs_2_ = bf16[16,1536]{1,0:T(8,128)(2,1)S(1)} collective-permute-done((bf16[16,1536]{1,0:T(8,128)(2,1)S(1)}, bf16[16,1536]{1,0:T(8,128)(2,1)S(1)}, u32[]{:S(2)}, u32[]{:S(2)}) %collective-permute-start.5) | collective-permute-done | bytes 49184 | tf_op jit(solution)/shard_map/ppermute | solution.py:20
  20.2 0.3 collective-permute-done.6.refs_3_
  20.5 1.6 %collective-permute-start.7 = (bf16[2,4,1536]{2,1,0:T(4,128)(2,1)S(1)}, bf16[2,4,1536]{2,1,0:T(4,128)(2,1)S(1)}, u32[]{:S(2)}, u32[]{:S(2)}) collective-permute-start(bf16[2,4,1536]{2,1,0:T(4,128)(2,1)S(1)} %get-tuple-element.22), channel_id=1, source_target_pairs={{0,2},{2,0},{1,3},{3,1},{4,6},{6,4},{5,7},{7,5},{8,10},{10,8},{9,1... | collective-permute-start | bytes 73736 | tf_op jit(solution)/shard_map/ppermute | solution.py:20
  22.1 1.1 %collective-permute-done.refs_1_ = s32[4]{0:T(128)S(1)} collective-permute-done((s32[4]{0:T(128)S(1)}, s32[4]{0:T(128)S(1)}, u32[]{:S(2)}, u32[]{:S(2)}) %collective-permute-start) | collective-permute-done | bytes 48 | tf_op jit(solution)/shard_map/ppermute | solution.py:20
  23.2 1.2 %collective-permute-done.7.refs_3_ = bf16[2,4,1536]{2,1,0:T(4,128)(2,1)S(1)} collective-permute-done((bf16[2,4,1536]{2,1,0:T(4,128)(2,1)S(1)}, bf16[2,4,1536]{2,1,0:T(4,128)(2,1)S(1)}, u32[]{:S(2)}, u32[]{:S(2)}) %collective-permute-start.7) | collective-permute-done | bytes 24608 | tf_op jit(solution)/shard_map/ppermute | solution.py:20
  24.4 1.5 %attention.1 = (bf16[2,4,1536]{2,1,0:T(4,128)(2,1)S(1)}, bf16[2,4,1536]{2,1,0:T(4,128)(2,1)S(1)}) custom-call(s32[4]{0:T(128)S(1)} %copy-done.3, s32[4]{0:T(128)S(1)} %collective-permute-done.refs_1_, bf16[2,4,1536]{2,1,0:T(4,128)(2,1)S(1)} %get-tuple-element.21.refs_2_, bf16[2,4,1536]{2,1,0:T(4,128)(2,1)S(1)} %collective-permute-done.7.refs_3_, ...), custom_call_target="tpu_custom_call" | custom-call | bytes 4292640 | tf_op jit(solution)/shard_map/attention/pallas_call | solution.py:38
  25.9 1.6 %collective-permute-start.10 = (bf16[2,4,1536]{2,1,0:T(4,128)(2,1)S(1)}, bf16[2,4,1536]{2,1,0:T(4,128)(2,1)S(1)}, u32[]{:S(2)}, u32[]{:S(2)}) collective-permute-start(bf16[2,4,1536]{2,1,0:T(4,128)(2,1)S(1)} %get-tuple-element.24), channel_id=1, source_target_pairs={{0,2},{2,0},{1,3},{3,1},{4,6},{6,4},{5,7},{7,5},{8,10},{10,8},{9,1... | collective-permute-start | bytes 73736 | tf_op jit(solution)/shard_map/ppermute | solution.py:20
  27.5 2.3 %collective-permute-done.10.refs_1_ = bf16[2,4,1536]{2,1,0:T(4,128)(2,1)S(1)} collective-permute-done((bf16[2,4,1536]{2,1,0:T(4,128)(2,1)S(1)}, bf16[2,4,1536]{2,1,0:T(4,128)(2,1)S(1)}, u32[]{:S(2)}, u32[]{:S(2)}) %collective-permute-start.10) | collective-permute-done | bytes 24608 | tf_op jit(solution)/shard_map/ppermute | solution.py:20
  29.9 3.0 %collective-permute-start.13 = (bf16[16,1536]{1,0:T(8,128)(2,1)S(1)}, bf16[16,1536]{1,0:T(8,128)(2,1)S(1)}, u32[]{:S(2)}, u32[]{:S(2)}) collective-permute-start(bf16[16,1536]{1,0:T(8,128)(2,1)S(1)} %mixed_rows.1.refs_0_), channel_id=1, source_target_pairs={{0,12},{4,0},{8,4},{12,8},{1,13},{5,1},{9,5},{13,9},{2,14},{6,2},{... | collective-permute-start | bytes 147464 | tf_op jit(solution)/shard_map/ppermute | solution.py:20
  32.8 0.6 %collective-permute-start.11 = (bf16[16,1536]{1,0:T(8,128)(2,1)S(1)}, bf16[16,1536]{1,0:T(8,128)(2,1)S(1)}, u32[]{:S(2)}, u32[]{:S(2)}) collective-permute-start(bf16[16,1536]{1,0:T(8,128)(2,1)S(1)} %mixed_rows.1.refs_0_), channel_id=1, source_target_pairs={{0,4},{4,8},{8,12},{12,0},{1,5},{5,9},{9,13},{13,1},{2,6},{6,10},{... | collective-permute-start | bytes 147464 | tf_op jit(solution)/shard_map/ppermute | solution.py:20
  33.5 1.1 %collective-permute-done.13.refs_3_ = bf16[16,1536]{1,0:T(8,128)(2,1)S(1)} collective-permute-done((bf16[16,1536]{1,0:T(8,128)(2,1)S(1)}, bf16[16,1536]{1,0:T(8,128)(2,1)S(1)}, u32[]{:S(2)}, u32[]{:S(2)}) %collective-permute-start.13) | collective-permute-done | bytes 49184 | tf_op jit(solution)/shard_map/ppermute | solution.py:20
  34.6 3.2 %collective-permute-done.12.refs_2_ = bf16[16,1536]{1,0:T(8,128)(2,1)S(1)} collective-permute-done((bf16[16,1536]{1,0:T(8,128)(2,1)S(1)}, bf16[16,1536]{1,0:T(8,128)(2,1)S(1)}, u32[]{:S(2)}, u32[]{:S(2)}) %collective-permute-start.12) | collective-permute-done | bytes 49184 | tf_op jit(solution)/shard_map/ppermute | solution.py:20
  37.8 0.9 %collective-permute-done.11.refs_1_ = bf16[16,1536]{1,0:T(8,128)(2,1)S(1)} collective-permute-done((bf16[16,1536]{1,0:T(8,128)(2,1)S(1)}, bf16[16,1536]{1,0:T(8,128)(2,1)S(1)}, u32[]{:S(2)}, u32[]{:S(2)}) %collective-permute-start.11) | collective-permute-done | bytes 49184 | tf_op jit(solution)/shard_map/ppermute | solution.py:20
  38.8 3.6 %output_terms.1 = (bf16[16,4608]{1,0:T(8,128)(2,1)S(1)}, bf16[16,4608]{1,0:T(8,128)(2,1)S(1)}, bf16[16,4608]{1,0:T(8,128)(2,1)S(1)}, bf16[16,4608]{1,0:T(8,128)(2,1)S(1)}) custom-call(bf16[16,1536]{1,0:T(8,128)(2,1)S(1)} %mixed_rows.1.refs_0_, bf16[16,1536]{1,0:T(8,128)(2,1)S(1)} %collective-permute-done.11.refs_1_, ...), custom_call_target="tpu_custom_call" | custom-call | flops 905969664 | bytes 14942208 | tf_op jit(solution)/shard_map/output_terms/pallas_call | solution.py:38
  42.4 0.1 collective-permute-start.15
  42.4 0.5 collective-permute-start.14
  42.9 0.9 %collective-permute-done.15.refs_1_ = bf16[16,4608]{1,0:T(8,128)(2,1)S(1)} collective-permute-done((bf16[16,4608]{1,0:T(8,128)(2,1)S(1)}, bf16[16,4608]{1,0:T(8,128)(2,1)S(1)}, u32[]{:S(2)}, u32[]{:S(2)}) %collective-permute-start.15) | collective-permute-done | bytes 147488 | tf_op jit(solution)/shard_map/ppermute | solution.py:20
  43.8 1.6 %collective-permute-start.16 = (bf16[16,4608]{1,0:T(8,128)(2,1)S(1)}, bf16[16,4608]{1,0:T(8,128)(2,1)S(1)}, u32[]{:S(2)}, u32[]{:S(2)}) collective-permute-start(bf16[16,4608]{1,0:T(8,128)(2,1)S(1)} %pair_sum.1), channel_id=1, source_target_pairs={{0,2},{2,0},{1,3},{3,1},{4,6},{6,4},{5,7},{7,5},{8,10},{10,8},{9,1... | collective-permute-start | bytes 442376 | tf_op jit(solution)/shard_map/ppermute | solution.py:20
  45.4 4.4 %collective-permute-done.16.refs_2_ = bf16[16,4608]{1,0:T(8,128)(2,1)S(1)} collective-permute-done((bf16[16,4608]{1,0:T(8,128)(2,1)S(1)}, bf16[16,4608]{1,0:T(8,128)(2,1)S(1)}, u32[]{:S(2)}, u32[]{:S(2)}) %collective-permute-start.16) | collective-permute-done | bytes 147488 | tf_op jit(solution)/shard_map/ppermute | solution.py:20
  49.8 0.7 %output_sum.1 = bf16[16,4608]{1,0:T(8,128)(2,1)} custom-call(bf16[16,4608]{1,0:T(8,128)(2,1)S(1)} %get-tuple-element.25.refs_0_, bf16[16,4608]{1,0:T(8,128)(2,1)S(1)} %collective-permute-done.14.refs_1_, bf16[16,4608]{1,0:T(8,128)(2,1)S(1)} %collective-permute-done.16.refs_2_), custom_call_target="tpu_custom_call" | custom-call | bytes 589824 | tf_op jit(solution)/shard_map/output_sum/pallas_call | solution.py:38
  (29 shorter events, 0.2 us)
Async XLA Ops:
  0.0 8.4 %copy-start = (bf16[4608,1536]{1,0:T(8,128)(2,1)S(1)}, bf16[4608,1536]{1,0:T(8,128)(2,1)}, u32[]{:S(2)}) copy-start(bf16[4608,1536]{1,0:T(8,128)(2,1)} %refs_4_.3) | copy-start | bytes 42467332
  0.0 7.0 %collective-permute-start.2 = (bf16[16,4608]{1,0:T(8,128)(2,1)}, bf16[16,4608]{1,0:T(8,128)(2,1)S(1)}, u32[]{:S(2)}, u32[]{:S(2)}) collective-permute-start(bf16[16,4608]{1,0:T(8,128)(2,1)} %tokens.1), channel_id=1, source_target_pairs={{0,2},{2,0},{1,3},{3,1},{4,6},{6,4},{5,7},{7,5},{8,10},{10,8},{9,1... | collective-permute-start | bytes 442376 | tf_op jit(solution)/shard_map/ppermute | solution.py:20
  2.9 5.2 %collective-permute-start.1 = (bf16[16,4608]{1,0:T(8,128)(2,1)}, bf16[16,4608]{1,0:T(8,128)(2,1)S(1)}, u32[]{:S(2)}, u32[]{:S(2)}) collective-permute-start(bf16[16,4608]{1,0:T(8,128)(2,1)} %tokens.1), channel_id=1, source_target_pairs={{0,1},{1,0},{2,3},{3,2},{4,5},{5,4},{6,7},{7,6},{8,9},{9,8},{10,11... | collective-permute-start | bytes 442376 | tf_op jit(solution)/shard_map/ppermute | solution.py:20
  7.0 1.4 %collective-permute-start.3 = (bf16[16,4608]{1,0:T(8,128)(2,1)S(1)}, bf16[16,4608]{1,0:T(8,128)(2,1)S(1)}, u32[]{:S(2)}, u32[]{:S(2)}) collective-permute-start(bf16[16,4608]{1,0:T(8,128)(2,1)S(1)} %collective-permute-done.2.refs_2_), channel_id=1, source_target_pairs={{0,1},{1,0},{2,3},{3,2},{4,5},{5,4},{6,7},{7,6},{8,9},{9,8},{10,11... | collective-permute-start | bytes 442376 | tf_op jit(solution)/shard_map/ppermute | solution.py:20
  7.0 0.9 %copy-start.4 = (bf16[16,4608]{1,0:T(8,128)(2,1)S(1)}, bf16[16,4608]{1,0:T(8,128)(2,1)}, u32[]{:S(2)}) copy-start(bf16[16,4608]{1,0:T(8,128)(2,1)} %tokens.1) | copy-start | bytes 442372
  8.1 9.4 %copy-start.1 = (bf16[4,512,256]{2,1,0:T(8,128)(2,1)S(1)}, bf16[4,512,256]{2,1,0:T(8,128)(2,1)}, u32[]{:S(2)}) copy-start(bf16[4,512,256]{2,1,0:T(8,128)(2,1)} %refs_4_.4) | copy-start | bytes 3145732
  8.1 9.4 %copy-start.2 = (bf16[4,512,256]{2,1,0:T(8,128)(2,1)S(1)}, bf16[4,512,256]{2,1,0:T(8,128)(2,1)}, u32[]{:S(2)}) copy-start(bf16[4,512,256]{2,1,0:T(8,128)(2,1)} %refs_6_.1) | copy-start | bytes 3145732
  8.4 30.4 %slice-start = ((s8[14155776]{0:T(1024)(128)(4,1)}), s8[1572864]{0:T(1024)(128)(4,1)S(1)}, s32[]{:S(2)}) async-start(s8[14155776]{0:T(1024)(128)(4,1)} %bitcast), calls=%async_computation | async-start | bytes 3145728
  8.4 30.4 %slice-start.1 = ((s8[14155776]{0:T(1024)(128)(4,1)}), s8[4194304]{0:T(1024)(128)(4,1)S(1)}, s32[]{:S(2)}) async-start(s8[14155776]{0:T(1024)(128)(4,1)} %bitcast), calls=%async_computation.1 | async-start | bytes 8388608
  11.7 6.3 %collective-permute-start.4 = (bf16[16,1536]{1,0:T(8,128)(2,1)S(1)}, bf16[16,1536]{1,0:T(8,128)(2,1)S(1)}, u32[]{:S(2)}, u32[]{:S(2)}) collective-permute-start(bf16[16,1536]{1,0:T(8,128)(2,1)S(1)} %get-tuple-element.18), channel_id=1, source_target_pairs={{0,4},{4,8},{8,12},{12,0},{1,5},{5,9},{9,13},{13,1},{2,6},{6,10},{... | collective-permute-start | bytes 147464 | tf_op jit(solution)/shard_map/ppermute | solution.py:20
  13.6 6.6 %collective-permute-start.5 = (bf16[16,1536]{1,0:T(8,128)(2,1)S(1)}, bf16[16,1536]{1,0:T(8,128)(2,1)S(1)}, u32[]{:S(2)}, u32[]{:S(2)}) collective-permute-start(bf16[16,1536]{1,0:T(8,128)(2,1)S(1)} %get-tuple-element.19), channel_id=1, source_target_pairs={{0,8},{4,12},{8,0},{12,4},{1,9},{5,13},{9,1},{13,5},{2,10},{6,14},... | collective-permute-start | bytes 147464 | tf_op jit(solution)/shard_map/ppermute | solution.py:20
  16.2 4.3 %collective-permute-start.6 = (bf16[16,1536]{1,0:T(8,128)(2,1)S(1)}, bf16[16,1536]{1,0:T(8,128)(2,1)S(1)}, u32[]{:S(2)}, u32[]{:S(2)}) collective-permute-start(bf16[16,1536]{1,0:T(8,128)(2,1)S(1)} %get-tuple-element.20), channel_id=1, source_target_pairs={{0,12},{4,0},{8,4},{12,8},{1,13},{5,1},{9,5},{13,9},{2,14},{6,2},{... | collective-permute-start | bytes 147464 | tf_op jit(solution)/shard_map/ppermute | solution.py:20
  17.5 6.9 %collective-permute-start.8 = (bf16[4,512,256]{2,1,0:T(8,128)(2,1)S(1)}, bf16[4,512,256]{2,1,0:T(8,128)(2,1)S(1)}, u32[]{:S(2)}, u32[]{:S(2)}) collective-permute-start(bf16[4,512,256]{2,1,0:T(8,128)(2,1)S(1)} %copy-done.1), channel_id=1, source_target_pairs={{0,1},{1,0},{2,3},{3,2},{4,5},{5,4},{6,7},{7,6},{8,9},{9,8},{10,11... | collective-permute-start | bytes 3145736 | tf_op jit(solution)/shard_map/ppermute | solution.py:20
  17.5 6.9 %collective-permute-start.9 = (bf16[4,512,256]{2,1,0:T(8,128)(2,1)S(1)}, bf16[4,512,256]{2,1,0:T(8,128)(2,1)S(1)}, u32[]{:S(2)}, u32[]{:S(2)}) collective-permute-start(bf16[4,512,256]{2,1,0:T(8,128)(2,1)S(1)} %copy-done.2), channel_id=1, source_target_pairs={{0,1},{1,0},{2,3},{3,2},{4,5},{5,4},{6,7},{7,6},{8,9},{9,8},{10,11... | collective-permute-start | bytes 3145736 | tf_op jit(solution)/shard_map/ppermute | solution.py:20
  20.5 1.6 %copy-start.3 = (s32[4]{0:T(128)S(1)}, s32[4]{0:T(128)}, u32[]{:S(2)}) copy-start(s32[4]{0:T(128)} %refs_0_.1) | copy-start | bytes 52
  20.5 18.3 %slice-start.2 = ((s8[14155776]{0:T(1024)(128)(4,1)}), s8[4194304]{0:T(1024)(128)(4,1)S(1)}, s32[]{:S(2)}) async-start(s8[14155776]{0:T(1024)(128)(4,1)} %bitcast), calls=%async_computation.2 | async-start | bytes 8388608
  20.5 18.3 %slice-start.3 = ((s8[14155776]{0:T(1024)(128)(4,1)}), s8[4194304]{0:T(1024)(128)(4,1)S(1)}, s32[]{:S(2)}) async-start(s8[14155776]{0:T(1024)(128)(4,1)} %bitcast), calls=%async_computation.3 | async-start | bytes 8388608
  20.5 3.9 %collective-permute-start.7 = (bf16[2,4,1536]{2,1,0:T(4,128)(2,1)S(1)}, bf16[2,4,1536]{2,1,0:T(4,128)(2,1)S(1)}, u32[]{:S(2)}, u32[]{:S(2)}) collective-permute-start(bf16[2,4,1536]{2,1,0:T(4,128)(2,1)S(1)} %get-tuple-element.22), channel_id=1, source_target_pairs={{0,2},{2,0},{1,3},{3,1},{4,6},{6,4},{5,7},{7,5},{8,10},{10,8},{9,1... | collective-permute-start | bytes 73736 | tf_op jit(solution)/shard_map/ppermute | solution.py:20
  22.1 1.1 %collective-permute-start = (s32[4]{0:T(128)S(1)}, s32[4]{0:T(128)S(1)}, u32[]{:S(2)}, u32[]{:S(2)}) collective-permute-start(s32[4]{0:T(128)S(1)} %copy-done.3), channel_id=1, source_target_pairs={{0,1},{1,0},{2,3},{3,2},{4,5},{5,4},{6,7},{7,6},{8,9},{9,8},{10,11... | collective-permute-start | bytes 56 | tf_op jit(solution)/shard_map/ppermute | solution.py:20
  25.9 3.9 %collective-permute-start.10 = (bf16[2,4,1536]{2,1,0:T(4,128)(2,1)S(1)}, bf16[2,4,1536]{2,1,0:T(4,128)(2,1)S(1)}, u32[]{:S(2)}, u32[]{:S(2)}) collective-permute-start(bf16[2,4,1536]{2,1,0:T(4,128)(2,1)S(1)} %get-tuple-element.24), channel_id=1, source_target_pairs={{0,2},{2,0},{1,3},{3,1},{4,6},{6,4},{5,7},{7,5},{8,10},{10,8},{9,1... | collective-permute-start | bytes 73736 | tf_op jit(solution)/shard_map/ppermute | solution.py:20
  29.9 4.7 %collective-permute-start.13 = (bf16[16,1536]{1,0:T(8,128)(2,1)S(1)}, bf16[16,1536]{1,0:T(8,128)(2,1)S(1)}, u32[]{:S(2)}, u32[]{:S(2)}) collective-permute-start(bf16[16,1536]{1,0:T(8,128)(2,1)S(1)} %mixed_rows.1.refs_0_), channel_id=1, source_target_pairs={{0,12},{4,0},{8,4},{12,8},{1,13},{5,1},{9,5},{13,9},{2,14},{6,2},{... | collective-permute-start | bytes 147464 | tf_op jit(solution)/shard_map/ppermute | solution.py:20
  32.8 5.0 %collective-permute-start.12 = (bf16[16,1536]{1,0:T(8,128)(2,1)S(1)}, bf16[16,1536]{1,0:T(8,128)(2,1)S(1)}, u32[]{:S(2)}, u32[]{:S(2)}) collective-permute-start(bf16[16,1536]{1,0:T(8,128)(2,1)S(1)} %mixed_rows.1.refs_0_), channel_id=1, source_target_pairs={{0,8},{4,12},{8,0},{12,4},{1,9},{5,13},{9,1},{13,5},{2,10},{6,14},... | collective-permute-start | bytes 147464 | tf_op jit(solution)/shard_map/ppermute | solution.py:20
  32.8 5.9 %collective-permute-start.11 = (bf16[16,1536]{1,0:T(8,128)(2,1)S(1)}, bf16[16,1536]{1,0:T(8,128)(2,1)S(1)}, u32[]{:S(2)}, u32[]{:S(2)}) collective-permute-start(bf16[16,1536]{1,0:T(8,128)(2,1)S(1)} %mixed_rows.1.refs_0_), channel_id=1, source_target_pairs={{0,4},{4,8},{8,12},{12,0},{1,5},{5,9},{9,13},{13,1},{2,6},{6,10},{... | collective-permute-start | bytes 147464 | tf_op jit(solution)/shard_map/ppermute | solution.py:20
  42.4 1.4 %collective-permute-start.15 = (bf16[16,4608]{1,0:T(8,128)(2,1)S(1)}, bf16[16,4608]{1,0:T(8,128)(2,1)S(1)}, u32[]{:S(2)}, u32[]{:S(2)}) collective-permute-start(bf16[16,4608]{1,0:T(8,128)(2,1)S(1)} %get-tuple-element.28), channel_id=1, source_target_pairs={{0,1},{1,0},{2,3},{3,2},{4,5},{5,4},{6,7},{7,6},{8,9},{9,8},{10,11... | collective-permute-start | bytes 442376 | tf_op jit(solution)/shard_map/ppermute | solution.py:20
  42.4 3.0 %collective-permute-start.14 = (bf16[16,4608]{1,0:T(8,128)(2,1)S(1)}, bf16[16,4608]{1,0:T(8,128)(2,1)S(1)}, u32[]{:S(2)}, u32[]{:S(2)}) collective-permute-start(bf16[16,4608]{1,0:T(8,128)(2,1)S(1)} %get-tuple-element.26), channel_id=1, source_target_pairs={{0,1},{1,0},{2,3},{3,2},{4,5},{5,4},{6,7},{7,6},{8,9},{9,8},{10,11... | collective-permute-start | bytes 442376 | tf_op jit(solution)/shard_map/ppermute | solution.py:20
  43.8 6.0 %collective-permute-start.16 = (bf16[16,4608]{1,0:T(8,128)(2,1)S(1)}, bf16[16,4608]{1,0:T(8,128)(2,1)S(1)}, u32[]{:S(2)}, u32[]{:S(2)}) collective-permute-start(bf16[16,4608]{1,0:T(8,128)(2,1)S(1)} %pair_sum.1), channel_id=1, source_target_pairs={{0,2},{2,0},{1,3},{3,1},{4,6},{6,4},{5,7},{7,5},{8,10},{10,8},{9,1... | collective-permute-start | bytes 442376 | tf_op jit(solution)/shard_map/ppermute | solution.py:20

commit v4 on v3

--- a/solution.py
+++ b/solution.py
@@ -53,6 +53,20 @@
     copy.wait()
 
 
+def product(rows, weight, span, step):
+    total = None
+    for at in range(0, weight.shape[0], step):
+        deep = slice(at, min(at + step, weight.shape[0]))
+        term = jnp.dot(rows[:, deep], weight[deep, span], preferred_element_type=F32)
+        total = term if total is None else total + term
+    return total
+
+
+def clear_below(rows, count):
+    if rows.shape[0] > count:
+        rows[count:, :] = jnp.zeros((rows.shape[0] - count, rows.shape[1]), rows.dtype)
+
+
 def query_body(n_gx, n_gy, n_gz, chunk, *refs):
     where = position()
     count = n_gy * n_gz
@@ -64,12 +78,11 @@
         for j in range(n_gz):
             at = lax.rem(where[1] + n_gy - k, n_gy) * n_gz + lax.rem(where[2] + n_gz - j, n_gz)
             rows[pl.ds(pl.multiple_of(at * block, block), block), :] = pieces[k * n_gz + j][...]
-
-    @pl.loop(0, weight.shape[1] // chunk)
-    def _(c):
-        span = pl.ds(pl.multiple_of(c * chunk, chunk), chunk)
-        total[:, span] = jnp.dot(rows[...], weight[:, span], preferred_element_type=F32)
-
+    count = block * n_gy * n_gz
+    clear_below(rows, count)
+    for c in range(weight.shape[1] // chunk):
+        span = slice(c * chunk, (c + 1) * chunk)
+        total[:, span] = product(rows, weight, span, 768)[:count]
     part = outs[0].shape[0]
     for k in range(n_gx):
         at = pl.multiple_of(lax.rem(where[0] + k, n_gx) * part, part)
@@ -152,11 +165,11 @@
         at = pl.multiple_of(lax.rem(where[0] + n_gx - k, n_gx) * block, block)
         rows[pl.ds(at, block), :] = pieces[k][...]
     part = outs[0].shape[0]
-
-    @pl.loop(0, weight.shape[1] // chunk)
-    def _(c):
-        span = pl.ds(pl.multiple_of(c * chunk, chunk), chunk)
-        total[...] = jnp.dot(rows[...], weight[:, span], preferred_element_type=F32)
+    count = block * n_gx
+    clear_below(rows, count)
+    for c in range(weight.shape[1] // chunk):
+        span = slice(c * chunk, (c + 1) * chunk)
+        total[...] = product(rows, weight, span, 768)[:count]
         for k in range(n_gy):
             for j in range(n_gz):
                 at = lax.rem(where[1] + k, n_gy) * n_gz + lax.rem(where[2] + j, n_gz)
@@ -186,6 +199,7 @@
     row_count = own_rows * n_gy * n_gz
     width = q_weight.shape[1]
     each = key_cache.shape[0]
+    tall = max(row_count, 128)
     part = row_count // n_gx
     struct = jax.ShapeDtypeStruct
 
@@ -214,10 +228,10 @@
         [*pieces, q_weight],
         [VMEM] * len(pieces) + [VMEM],
         scratch=[
-            pltpu.VMEM((row_count, depth), BF16),
+            pltpu.VMEM((tall, depth), BF16),
             pltpu.VMEM((row_count, width), F32),
         ],
-        mib=mib_for(row_count * depth * 4, row_count * width * 8, depth * width * 2),
+        mib=mib_for(tall * depth * 4, tall * width * 8, depth * width * 2),
         flops=2 * row_count * depth * width,
         name="query_terms",
     )
@@ -254,17 +268,17 @@
     )[0]
     blocks = [block] + [shift(block, "gx", k) for k in range(1, n_gx)]
     columns = o_weight.shape[1]
-    chunk = largest_divisor(columns, 512, 128)
+    chunk = largest_divisor(columns, 768, 128)
     terms = call(
         functools.partial(output_body, n_gx, n_gy, n_gz, chunk),
         [struct((own_rows, columns), BF16)] * (n_gy * n_gz),
         [*blocks, o_weight],
         [VMEM] * n_gx + [VMEM],
         scratch=[
-            pltpu.VMEM((row_count, width), BF16),
+            pltpu.VMEM((tall, width), BF16),
             pltpu.VMEM((row_count, chunk), F32),
         ],
-        mib=mib_for(row_count * width * 4, row_count * (chunk * 4 + columns * 2), columns * width * 2),
+        mib=mib_for(tall * width * 4, tall * (chunk * 4 + columns * 2), columns * width * 2),
         flops=2 * row_count * columns * width,
         name="output_terms",
     )

time: 50.7 us -> 47.8 us (0.943)
  Pallas kernels: 9.4 us -> 6.52 us
    pallas_call x8, Pallas kernels: 9.4 us -> 6.52 us  [call(): pl.pallas_call(body, out_shape=list(outs), in_specs=in_specs, out_specs=[...]
  transfers between devices with their start and end apart: 17 -> 17, of which waited for: 12 -> 12; matrix products, arithmetic and copies ran while one was open for 0% -> 0% of each run, Pallas kernels for 0% -> 1%
where the time goes in v4:
time: 47.8 us; the launch traced here: 47.6 us
  waiting for transfers between devices  21.9 us (46%)
  starting transfers between devices  18.2 us (38%)
  Pallas kernels  6.52 us (14%)
  local copies, waits for them, and re-layouts  0.95 us (2%)
    ppermute x17, waiting for transfers between devices, shift(): lax.ppermute(array, axis, [(s, (s + by) % size) for s in range(size)])  21.9 us
    ppermute x17, starting transfers between devices, shift(): lax.ppermute(array, axis, [(s, (s + by) % size) for s in range(size)])  18.2 us
    pallas_call x8, Pallas kernels, call(): pl.pallas_call(body, out_shape=list(outs), in_specs=in_specs, out_specs=[...  6.52 us
  transfers between devices with their start and end apart: 17, of which 12 were waited for; matrix products, arithmetic and copies ran while one was open for 0% of the time, Pallas kernels for 1%

profile of v4, /device:TPU:0, one launch (start us, length us, event | category | flops | bytes accessed | tf_op | source)
XLA Modules:
  0.0 47.6 jit_solution(677596981742914301)
XLA Ops:
  0.0 2.9 %collective-permute-start.2 = (bf16[16,4608]{1,0:T(8,128)(2,1)}, bf16[16,4608]{1,0:T(8,128)(2,1)S(1)}, u32[]{:S(2)}, u32[]{:S(2)}) collective-permute-start(bf16[16,4608]{1,0:T(8,128)(2,1)} %tokens.1), channel_id=1, source_target_pairs={{0,2},{2,0},{1,3},{3,1},{4,6},{6,4},{5,7},{7,5},{8,10},{10,8},{9,1... | collective-permute-start | bytes 442376 | tf_op jit(solution)/shard_map/ppermute | solution.py:20
  2.9 4.1 %collective-permute-done.2.refs_2_ = bf16[16,4608]{1,0:T(8,128)(2,1)S(1)} collective-permute-done((bf16[16,4608]{1,0:T(8,128)(2,1)}, bf16[16,4608]{1,0:T(8,128)(2,1)S(1)}, u32[]{:S(2)}, u32[]{:S(2)}) %collective-permute-start.2) | collective-permute-done | bytes 147488 | tf_op jit(solution)/shard_map/ppermute | solution.py:20
  7.0 0.9 %copy-done.4 = bf16[16,4608]{1,0:T(8,128)(2,1)S(1)} copy-done((bf16[16,4608]{1,0:T(8,128)(2,1)S(1)}, bf16[16,4608]{1,0:T(8,128)(2,1)}, u32[]{:S(2)}) %copy-start.4) | copy-done | bytes 147480
  7.9 0.2 own_tokens.1.refs_0_
  8.1 0.0 copy-start.1
  8.1 0.0 copy-start.2
  8.1 0.2 collective-permute-done.3.refs_3_
  8.4 2.0 %query_terms.1 = (bf16[16,1536]{1,0:T(8,128)(2,1)S(1)}, bf16[16,1536]{1,0:T(8,128)(2,1)S(1)}, bf16[16,1536]{1,0:T(8,128)(2,1)S(1)}, bf16[16,1536]{1,0:T(8,128)(2,1)S(1)}) custom-call(bf16[16,4608]{1,0:T(8,128)(2,1)S(1)} %own_tokens.1.refs_0_, bf16[16,4608]{1,0:T(8,128)(2,1)S(1)} %collective-permute-done.1.refs_1_, ...), custom_call_target="tpu_custom_call" | custom-call | flops 905969664 | bytes 14942208 | tf_op jit(solution)/shard_map/query_terms/pallas_call | solution.py:38
  10.4 1.9 %collective-permute-start.4 = (bf16[16,1536]{1,0:T(8,128)(2,1)S(1)}, bf16[16,1536]{1,0:T(8,128)(2,1)S(1)}, u32[]{:S(2)}, u32[]{:S(2)}) collective-permute-start(bf16[16,1536]{1,0:T(8,128)(2,1)S(1)} %get-tuple-element.18), channel_id=1, source_target_pairs={{0,4},{4,8},{8,12},{12,0},{1,5},{5,9},{9,13},{13,1},{2,6},{6,10},{... | collective-permute-start | bytes 147464 | tf_op jit(solution)/shard_map/ppermute | solution.py:20
  12.3 2.6 %collective-permute-start.5 = (bf16[16,1536]{1,0:T(8,128)(2,1)S(1)}, bf16[16,1536]{1,0:T(8,128)(2,1)S(1)}, u32[]{:S(2)}, u32[]{:S(2)}) collective-permute-start(bf16[16,1536]{1,0:T(8,128)(2,1)S(1)} %get-tuple-element.19), channel_id=1, source_target_pairs={{0,8},{4,12},{8,0},{12,4},{1,9},{5,13},{9,1},{13,5},{2,10},{6,14},... | collective-permute-start | bytes 147464 | tf_op jit(solution)/shard_map/ppermute | solution.py:20
  14.9 1.3 %collective-permute-start.6 = (bf16[16,1536]{1,0:T(8,128)(2,1)S(1)}, bf16[16,1536]{1,0:T(8,128)(2,1)S(1)}, u32[]{:S(2)}, u32[]{:S(2)}) collective-permute-start(bf16[16,1536]{1,0:T(8,128)(2,1)S(1)} %get-tuple-element.20), channel_id=1, source_target_pairs={{0,12},{4,0},{8,4},{12,8},{1,13},{5,1},{9,5},{13,9},{2,14},{6,2},{... | collective-permute-start | bytes 147464 | tf_op jit(solution)/shard_map/ppermute | solution.py:20
  16.2 0.5 %collective-permute-start.9 = (bf16[4,512,256]{2,1,0:T(8,128)(2,1)S(1)}, bf16[4,512,256]{2,1,0:T(8,128)(2,1)S(1)}, u32[]{:S(2)}, u32[]{:S(2)}) collective-permute-start(bf16[4,512,256]{2,1,0:T(8,128)(2,1)S(1)} %copy-done.2), channel_id=1, source_target_pairs={{0,1},{1,0},{2,3},{3,2},{4,5},{5,4},{6,7},{7,6},{8,9},{9,8},{10,11... | collective-permute-start | bytes 3145736 | tf_op jit(solution)/shard_map/ppermute | solution.py:20
  16.7 2.1 %collective-permute-done.5.refs_2_ = bf16[16,1536]{1,0:T(8,128)(2,1)S(1)} collective-permute-done((bf16[16,1536]{1,0:T(8,128)(2,1)S(1)}, bf16[16,1536]{1,0:T(8,128)(2,1)S(1)}, u32[]{:S(2)}, u32[]{:S(2)}) %collective-permute-start.5) | collective-permute-done | bytes 49184 | tf_op jit(solution)/shard_map/ppermute | solution.py:20
  18.8 0.3 collective-permute-done.6.refs_3_
  19.2 1.6 %collective-permute-start.7 = (bf16[2,4,1536]{2,1,0:T(4,128)(2,1)S(1)}, bf16[2,4,1536]{2,1,0:T(4,128)(2,1)S(1)}, u32[]{:S(2)}, u32[]{:S(2)}) collective-permute-start(bf16[2,4,1536]{2,1,0:T(4,128)(2,1)S(1)} %get-tuple-element.22), channel_id=1, source_target_pairs={{0,2},{2,0},{1,3},{3,1},{4,6},{6,4},{5,7},{7,5},{8,10},{10,8},{9,1... | collective-permute-start | bytes 73736 | tf_op jit(solution)/shard_map/ppermute | solution.py:20
  20.8 1.1 %collective-permute-done.refs_1_ = s32[4]{0:T(128)S(1)} collective-permute-done((s32[4]{0:T(128)S(1)}, s32[4]{0:T(128)S(1)}, u32[]{:S(2)}, u32[]{:S(2)}) %collective-permute-start) | collective-permute-done | bytes 48 | tf_op jit(solution)/shard_map/ppermute | solution.py:20
  21.9 1.2 %collective-permute-done.7.refs_3_ = bf16[2,4,1536]{2,1,0:T(4,128)(2,1)S(1)} collective-permute-done((bf16[2,4,1536]{2,1,0:T(4,128)(2,1)S(1)}, bf16[2,4,1536]{2,1,0:T(4,128)(2,1)S(1)}, u32[]{:S(2)}, u32[]{:S(2)}) %collective-permute-start.7) | collective-permute-done | bytes 24608 | tf_op jit(solution)/shard_map/ppermute | solution.py:20
  23.1 1.5 %attention.1 = (bf16[2,4,1536]{2,1,0:T(4,128)(2,1)S(1)}, bf16[2,4,1536]{2,1,0:T(4,128)(2,1)S(1)}) custom-call(s32[4]{0:T(128)S(1)} %copy-done.3, s32[4]{0:T(128)S(1)} %collective-permute-done.refs_1_, bf16[2,4,1536]{2,1,0:T(4,128)(2,1)S(1)} %get-tuple-element.21.refs_2_, bf16[2,4,1536]{2,1,0:T(4,128)(2,1)S(1)} %collective-permute-done.7.refs_3_, ...), custom_call_target="tpu_custom_call" | custom-call | bytes 4292640 | tf_op jit(solution)/shard_map/attention/pallas_call | solution.py:38
  24.6 1.6 %collective-permute-start.10 = (bf16[2,4,1536]{2,1,0:T(4,128)(2,1)S(1)}, bf16[2,4,1536]{2,1,0:T(4,128)(2,1)S(1)}, u32[]{:S(2)}, u32[]{:S(2)}) collective-permute-start(bf16[2,4,1536]{2,1,0:T(4,128)(2,1)S(1)} %get-tuple-element.24), channel_id=1, source_target_pairs={{0,2},{2,0},{1,3},{3,1},{4,6},{6,4},{5,7},{7,5},{8,10},{10,8},{9,1... | collective-permute-start | bytes 73736 | tf_op jit(solution)/shard_map/ppermute | solution.py:20
  26.2 2.3 %collective-permute-done.10.refs_1_ = bf16[2,4,1536]{2,1,0:T(4,128)(2,1)S(1)} collective-permute-done((bf16[2,4,1536]{2,1,0:T(4,128)(2,1)S(1)}, bf16[2,4,1536]{2,1,0:T(4,128)(2,1)S(1)}, u32[]{:S(2)}, u32[]{:S(2)}) %collective-permute-start.10) | collective-permute-done | bytes 24608 | tf_op jit(solution)/shard_map/ppermute | solution.py:20
  28.5 3.0 %collective-permute-start.13 = (bf16[16,1536]{1,0:T(8,128)(2,1)S(1)}, bf16[16,1536]{1,0:T(8,128)(2,1)S(1)}, u32[]{:S(2)}, u32[]{:S(2)}) collective-permute-start(bf16[16,1536]{1,0:T(8,128)(2,1)S(1)} %mixed_rows.1.refs_0_), channel_id=1, source_target_pairs={{0,12},{4,0},{8,4},{12,8},{1,13},{5,1},{9,5},{13,9},{2,14},{6,2},{... | collective-permute-start | bytes 147464 | tf_op jit(solution)/shard_map/ppermute | solution.py:20
  31.5 0.6 %collective-permute-start.11 = (bf16[16,1536]{1,0:T(8,128)(2,1)S(1)}, bf16[16,1536]{1,0:T(8,128)(2,1)S(1)}, u32[]{:S(2)}, u32[]{:S(2)}) collective-permute-start(bf16[16,1536]{1,0:T(8,128)(2,1)S(1)} %mixed_rows.1.refs_0_), channel_id=1, source_target_pairs={{0,4},{4,8},{8,12},{12,0},{1,5},{5,9},{9,13},{13,1},{2,6},{6,10},{... | collective-permute-start | bytes 147464 | tf_op jit(solution)/shard_map/ppermute | solution.py:20
  32.2 1.1 %collective-permute-done.13.refs_3_ = bf16[16,1536]{1,0:T(8,128)(2,1)S(1)} collective-permute-done((bf16[16,1536]{1,0:T(8,128)(2,1)S(1)}, bf16[16,1536]{1,0:T(8,128)(2,1)S(1)}, u32[]{:S(2)}, u32[]{:S(2)}) %collective-permute-start.13) | collective-permute-done | bytes 49184 | tf_op jit(solution)/shard_map/ppermute | solution.py:20
  33.3 3.2 %collective-permute-done.12.refs_2_ = bf16[16,1536]{1,0:T(8,128)(2,1)S(1)} collective-permute-done((bf16[16,1536]{1,0:T(8,128)(2,1)S(1)}, bf16[16,1536]{1,0:T(8,128)(2,1)S(1)}, u32[]{:S(2)}, u32[]{:S(2)}) %collective-permute-start.12) | collective-permute-done | bytes 49184 | tf_op jit(solution)/shard_map/ppermute | solution.py:20
  36.5 0.9 %collective-permute-done.11.refs_1_ = bf16[16,1536]{1,0:T(8,128)(2,1)S(1)} collective-permute-done((bf16[16,1536]{1,0:T(8,128)(2,1)S(1)}, bf16[16,1536]{1,0:T(8,128)(2,1)S(1)}, u32[]{:S(2)}, u32[]{:S(2)}) %collective-permute-start.11) | collective-permute-done | bytes 49184 | tf_op jit(solution)/shard_map/ppermute | solution.py:20
  37.5 2.0 %output_terms.1 = (bf16[16,4608]{1,0:T(8,128)(2,1)S(1)}, bf16[16,4608]{1,0:T(8,128)(2,1)S(1)}, bf16[16,4608]{1,0:T(8,128)(2,1)S(1)}, bf16[16,4608]{1,0:T(8,128)(2,1)S(1)}) custom-call(bf16[16,1536]{1,0:T(8,128)(2,1)S(1)} %mixed_rows.1.refs_0_, bf16[16,1536]{1,0:T(8,128)(2,1)S(1)} %collective-permute-done.11.refs_1_, ...), custom_call_target="tpu_custom_call" | custom-call | flops 905969664 | bytes 14942208 | tf_op jit(solution)/shard_map/output_terms/pallas_call | solution.py:38
  39.5 0.1 collective-permute-start.15
  39.6 0.5 %collective-permute-start.14 = (bf16[16,4608]{1,0:T(8,128)(2,1)S(1)}, bf16[16,4608]{1,0:T(8,128)(2,1)S(1)}, u32[]{:S(2)}, u32[]{:S(2)}) collective-permute-start(bf16[16,4608]{1,0:T(8,128)(2,1)S(1)} %get-tuple-element.26), channel_id=1, source_target_pairs={{0,1},{1,0},{2,3},{3,2},{4,5},{5,4},{6,7},{7,6},{8,9},{9,8},{10,11... | collective-permute-start | bytes 442376 | tf_op jit(solution)/shard_map/ppermute | solution.py:20
  40.1 0.9 %collective-permute-done.15.refs_1_ = bf16[16,4608]{1,0:T(8,128)(2,1)S(1)} collective-permute-done((bf16[16,4608]{1,0:T(8,128)(2,1)S(1)}, bf16[16,4608]{1,0:T(8,128)(2,1)S(1)}, u32[]{:S(2)}, u32[]{:S(2)}) %collective-permute-start.15) | collective-permute-done | bytes 147488 | tf_op jit(solution)/shard_map/ppermute | solution.py:20
  41.0 1.6 %collective-permute-start.16 = (bf16[16,4608]{1,0:T(8,128)(2,1)S(1)}, bf16[16,4608]{1,0:T(8,128)(2,1)S(1)}, u32[]{:S(2)}, u32[]{:S(2)}) collective-permute-start(bf16[16,4608]{1,0:T(8,128)(2,1)S(1)} %pair_sum.1), channel_id=1, source_target_pairs={{0,2},{2,0},{1,3},{3,1},{4,6},{6,4},{5,7},{7,5},{8,10},{10,8},{9,1... | collective-permute-start | bytes 442376 | tf_op jit(solution)/shard_map/ppermute | solution.py:20
  42.5 4.4 %collective-permute-done.16.refs_2_ = bf16[16,4608]{1,0:T(8,128)(2,1)S(1)} collective-permute-done((bf16[16,4608]{1,0:T(8,128)(2,1)S(1)}, bf16[16,4608]{1,0:T(8,128)(2,1)S(1)}, u32[]{:S(2)}, u32[]{:S(2)}) %collective-permute-start.16) | collective-permute-done | bytes 147488 | tf_op jit(solution)/shard_map/ppermute | solution.py:20
  46.9 0.7 %output_sum.1 = bf16[16,4608]{1,0:T(8,128)(2,1)} custom-call(bf16[16,4608]{1,0:T(8,128)(2,1)S(1)} %get-tuple-element.25.refs_0_, bf16[16,4608]{1,0:T(8,128)(2,1)S(1)} %collective-permute-done.14.refs_1_, bf16[16,4608]{1,0:T(8,128)(2,1)S(1)} %collective-permute-done.16.refs_2_), custom_call_target="tpu_custom_call" | custom-call | bytes 589824 | tf_op jit(solution)/shard_map/output_sum/pallas_call | solution.py:38
  (29 shorter events, 0.2 us)
Async XLA Ops:
  0.0 8.4 %copy-start = (bf16[4608,1536]{1,0:T(8,128)(2,1)S(1)}, bf16[4608,1536]{1,0:T(8,128)(2,1)}, u32[]{:S(2)}) copy-start(bf16[4608,1536]{1,0:T(8,128)(2,1)} %refs_4_.3) | copy-start | bytes 42467332
  0.0 7.0 %collective-permute-start.2 = (bf16[16,4608]{1,0:T(8,128)(2,1)}, bf16[16,4608]{1,0:T(8,128)(2,1)S(1)}, u32[]{:S(2)}, u32[]{:S(2)}) collective-permute-start(bf16[16,4608]{1,0:T(8,128)(2,1)} %tokens.1), channel_id=1, source_target_pairs={{0,2},{2,0},{1,3},{3,1},{4,6},{6,4},{5,7},{7,5},{8,10},{10,8},{9,1... | collective-permute-start | bytes 442376 | tf_op jit(solution)/shard_map/ppermute | solution.py:20
  2.9 5.2 %collective-permute-start.1 = (bf16[16,4608]{1,0:T(8,128)(2,1)}, bf16[16,4608]{1,0:T(8,128)(2,1)S(1)}, u32[]{:S(2)}, u32[]{:S(2)}) collective-permute-start(bf16[16,4608]{1,0:T(8,128)(2,1)} %tokens.1), channel_id=1, source_target_pairs={{0,1},{1,0},{2,3},{3,2},{4,5},{5,4},{6,7},{7,6},{8,9},{9,8},{10,11... | collective-permute-start | bytes 442376 | tf_op jit(solution)/shard_map/ppermute | solution.py:20
  7.0 1.4 %collective-permute-start.3 = (bf16[16,4608]{1,0:T(8,128)(2,1)S(1)}, bf16[16,4608]{1,0:T(8,128)(2,1)S(1)}, u32[]{:S(2)}, u32[]{:S(2)}) collective-permute-start(bf16[16,4608]{1,0:T(8,128)(2,1)S(1)} %collective-permute-done.2.refs_2_), channel_id=1, source_target_pairs={{0,1},{1,0},{2,3},{3,2},{4,5},{5,4},{6,7},{7,6},{8,9},{9,8},{10,11... | collective-permute-start | bytes 442376 | tf_op jit(solution)/shard_map/ppermute | solution.py:20
  7.0 0.9 %copy-start.4 = (bf16[16,4608]{1,0:T(8,128)(2,1)S(1)}, bf16[16,4608]{1,0:T(8,128)(2,1)}, u32[]{:S(2)}) copy-start(bf16[16,4608]{1,0:T(8,128)(2,1)} %tokens.1) | copy-start | bytes 442372
  8.1 8.1 %copy-start.1 = (bf16[4,512,256]{2,1,0:T(8,128)(2,1)S(1)}, bf16[4,512,256]{2,1,0:T(8,128)(2,1)}, u32[]{:S(2)}) copy-start(bf16[4,512,256]{2,1,0:T(8,128)(2,1)} %refs_4_.4) | copy-start | bytes 3145732
  8.1 8.1 %copy-start.2 = (bf16[4,512,256]{2,1,0:T(8,128)(2,1)S(1)}, bf16[4,512,256]{2,1,0:T(8,128)(2,1)}, u32[]{:S(2)}) copy-start(bf16[4,512,256]{2,1,0:T(8,128)(2,1)} %refs_6_.1) | copy-start | bytes 3145732
  8.4 29.1 %slice-start = ((s8[14155776]{0:T(1024)(128)(4,1)}), s8[1572864]{0:T(1024)(128)(4,1)S(1)}, s32[]{:S(2)}) async-start(s8[14155776]{0:T(1024)(128)(4,1)} %bitcast), calls=%async_computation | async-start | bytes 3145728
  8.4 29.1 %slice-start.1 = ((s8[14155776]{0:T(1024)(128)(4,1)}), s8[4194304]{0:T(1024)(128)(4,1)S(1)}, s32[]{:S(2)}) async-start(s8[14155776]{0:T(1024)(128)(4,1)} %bitcast), calls=%async_computation.1 | async-start | bytes 8388608
  10.4 6.3 %collective-permute-start.4 = (bf16[16,1536]{1,0:T(8,128)(2,1)S(1)}, bf16[16,1536]{1,0:T(8,128)(2,1)S(1)}, u32[]{:S(2)}, u32[]{:S(2)}) collective-permute-start(bf16[16,1536]{1,0:T(8,128)(2,1)S(1)} %get-tuple-element.18), channel_id=1, source_target_pairs={{0,4},{4,8},{8,12},{12,0},{1,5},{5,9},{9,13},{13,1},{2,6},{6,10},{... | collective-permute-start | bytes 147464 | tf_op jit(solution)/shard_map/ppermute | solution.py:20
  12.3 6.6 %collective-permute-start.5 = (bf16[16,1536]{1,0:T(8,128)(2,1)S(1)}, bf16[16,1536]{1,0:T(8,128)(2,1)S(1)}, u32[]{:S(2)}, u32[]{:S(2)}) collective-permute-start(bf16[16,1536]{1,0:T(8,128)(2,1)S(1)} %get-tuple-element.19), channel_id=1, source_target_pairs={{0,8},{4,12},{8,0},{12,4},{1,9},{5,13},{9,1},{13,5},{2,10},{6,14},... | collective-permute-start | bytes 147464 | tf_op jit(solution)/shard_map/ppermute | solution.py:20
  14.9 4.3 %collective-permute-start.6 = (bf16[16,1536]{1,0:T(8,128)(2,1)S(1)}, bf16[16,1536]{1,0:T(8,128)(2,1)S(1)}, u32[]{:S(2)}, u32[]{:S(2)}) collective-permute-start(bf16[16,1536]{1,0:T(8,128)(2,1)S(1)} %get-tuple-element.20), channel_id=1, source_target_pairs={{0,12},{4,0},{8,4},{12,8},{1,13},{5,1},{9,5},{13,9},{2,14},{6,2},{... | collective-permute-start | bytes 147464 | tf_op jit(solution)/shard_map/ppermute | solution.py:20
  16.2 6.9 %collective-permute-start.8 = (bf16[4,512,256]{2,1,0:T(8,128)(2,1)S(1)}, bf16[4,512,256]{2,1,0:T(8,128)(2,1)S(1)}, u32[]{:S(2)}, u32[]{:S(2)}) collective-permute-start(bf16[4,512,256]{2,1,0:T(8,128)(2,1)S(1)} %copy-done.1), channel_id=1, source_target_pairs={{0,1},{1,0},{2,3},{3,2},{4,5},{5,4},{6,7},{7,6},{8,9},{9,8},{10,11... | collective-permute-start | bytes 3145736 | tf_op jit(solution)/shard_map/ppermute | solution.py:20
  16.2 6.9 %collective-permute-start.9 = (bf16[4,512,256]{2,1,0:T(8,128)(2,1)S(1)}, bf16[4,512,256]{2,1,0:T(8,128)(2,1)S(1)}, u32[]{:S(2)}, u32[]{:S(2)}) collective-permute-start(bf16[4,512,256]{2,1,0:T(8,128)(2,1)S(1)} %copy-done.2), channel_id=1, source_target_pairs={{0,1},{1,0},{2,3},{3,2},{4,5},{5,4},{6,7},{7,6},{8,9},{9,8},{10,11... | collective-permute-start | bytes 3145736 | tf_op jit(solution)/shard_map/ppermute | solution.py:20
  19.2 1.6 %copy-start.3 = (s32[4]{0:T(128)S(1)}, s32[4]{0:T(128)}, u32[]{:S(2)}) copy-start(s32[4]{0:T(128)} %refs_0_.1) | copy-start | bytes 52
  19.2 18.3 %slice-start.2 = ((s8[14155776]{0:T(1024)(128)(4,1)}), s8[4194304]{0:T(1024)(128)(4,1)S(1)}, s32[]{:S(2)}) async-start(s8[14155776]{0:T(1024)(128)(4,1)} %bitcast), calls=%async_computation.2 | async-start | bytes 8388608
  19.2 18.3 %slice-start.3 = ((s8[14155776]{0:T(1024)(128)(4,1)}), s8[4194304]{0:T(1024)(128)(4,1)S(1)}, s32[]{:S(2)}) async-start(s8[14155776]{0:T(1024)(128)(4,1)} %bitcast), calls=%async_computation.3 | async-start | bytes 8388608
  19.2 3.9 %collective-permute-start.7 = (bf16[2,4,1536]{2,1,0:T(4,128)(2,1)S(1)}, bf16[2,4,1536]{2,1,0:T(4,128)(2,1)S(1)}, u32[]{:S(2)}, u32[]{:S(2)}) collective-permute-start(bf16[2,4,1536]{2,1,0:T(4,128)(2,1)S(1)} %get-tuple-element.22), channel_id=1, source_target_pairs={{0,2},{2,0},{1,3},{3,1},{4,6},{6,4},{5,7},{7,5},{8,10},{10,8},{9,1... | collective-permute-start | bytes 73736 | tf_op jit(solution)/shard_map/ppermute | solution.py:20
  20.8 1.1 %collective-permute-start = (s32[4]{0:T(128)S(1)}, s32[4]{0:T(128)S(1)}, u32[]{:S(2)}, u32[]{:S(2)}) collective-permute-start(s32[4]{0:T(128)S(1)} %copy-done.3), channel_id=1, source_target_pairs={{0,1},{1,0},{2,3},{3,2},{4,5},{5,4},{6,7},{7,6},{8,9},{9,8},{10,11... | collective-permute-start | bytes 56 | tf_op jit(solution)/shard_map/ppermute | solution.py:20
  24.6 3.9 %collective-permute-start.10 = (bf16[2,4,1536]{2,1,0:T(4,128)(2,1)S(1)}, bf16[2,4,1536]{2,1,0:T(4,128)(2,1)S(1)}, u32[]{:S(2)}, u32[]{:S(2)}) collective-permute-start(bf16[2,4,1536]{2,1,0:T(4,128)(2,1)S(1)} %get-tuple-element.24), channel_id=1, source_target_pairs={{0,2},{2,0},{1,3},{3,1},{4,6},{6,4},{5,7},{7,5},{8,10},{10,8},{9,1... | collective-permute-start | bytes 73736 | tf_op jit(solution)/shard_map/ppermute | solution.py:20
  28.5 4.7 %collective-permute-start.13 = (bf16[16,1536]{1,0:T(8,128)(2,1)S(1)}, bf16[16,1536]{1,0:T(8,128)(2,1)S(1)}, u32[]{:S(2)}, u32[]{:S(2)}) collective-permute-start(bf16[16,1536]{1,0:T(8,128)(2,1)S(1)} %mixed_rows.1.refs_0_), channel_id=1, source_target_pairs={{0,12},{4,0},{8,4},{12,8},{1,13},{5,1},{9,5},{13,9},{2,14},{6,2},{... | collective-permute-start | bytes 147464 | tf_op jit(solution)/shard_map/ppermute | solution.py:20
  31.5 5.0 %collective-permute-start.12 = (bf16[16,1536]{1,0:T(8,128)(2,1)S(1)}, bf16[16,1536]{1,0:T(8,128)(2,1)S(1)}, u32[]{:S(2)}, u32[]{:S(2)}) collective-permute-start(bf16[16,1536]{1,0:T(8,128)(2,1)S(1)} %mixed_rows.1.refs_0_), channel_id=1, source_target_pairs={{0,8},{4,12},{8,0},{12,4},{1,9},{5,13},{9,1},{13,5},{2,10},{6,14},... | collective-permute-start | bytes 147464 | tf_op jit(solution)/shard_map/ppermute | solution.py:20
  31.5 5.9 %collective-permute-start.11 = (bf16[16,1536]{1,0:T(8,128)(2,1)S(1)}, bf16[16,1536]{1,0:T(8,128)(2,1)S(1)}, u32[]{:S(2)}, u32[]{:S(2)}) collective-permute-start(bf16[16,1536]{1,0:T(8,128)(2,1)S(1)} %mixed_rows.1.refs_0_), channel_id=1, source_target_pairs={{0,4},{4,8},{8,12},{12,0},{1,5},{5,9},{9,13},{13,1},{2,6},{6,10},{... | collective-permute-start | bytes 147464 | tf_op jit(solution)/shard_map/ppermute | solution.py:20
  39.5 1.4 %collective-permute-start.15 = (bf16[16,4608]{1,0:T(8,128)(2,1)S(1)}, bf16[16,4608]{1,0:T(8,128)(2,1)S(1)}, u32[]{:S(2)}, u32[]{:S(2)}) collective-permute-start(bf16[16,4608]{1,0:T(8,128)(2,1)S(1)} %get-tuple-element.28), channel_id=1, source_target_pairs={{0,1},{1,0},{2,3},{3,2},{4,5},{5,4},{6,7},{7,6},{8,9},{9,8},{10,11... | collective-permute-start | bytes 442376 | tf_op jit(solution)/shard_map/ppermute | solution.py:20
  39.6 3.0 %collective-permute-start.14 = (bf16[16,4608]{1,0:T(8,128)(2,1)S(1)}, bf16[16,4608]{1,0:T(8,128)(2,1)S(1)}, u32[]{:S(2)}, u32[]{:S(2)}) collective-permute-start(bf16[16,4608]{1,0:T(8,128)(2,1)S(1)} %get-tuple-element.26), channel_id=1, source_target_pairs={{0,1},{1,0},{2,3},{3,2},{4,5},{5,4},{6,7},{7,6},{8,9},{9,8},{10,11... | collective-permute-start | bytes 442376 | tf_op jit(solution)/shard_map/ppermute | solution.py:20
  41.0 6.0 %collective-permute-start.16 = (bf16[16,4608]{1,0:T(8,128)(2,1)S(1)}, bf16[16,4608]{1,0:T(8,128)(2,1)S(1)}, u32[]{:S(2)}, u32[]{:S(2)}) collective-permute-start(bf16[16,4608]{1,0:T(8,128)(2,1)S(1)} %pair_sum.1), channel_id=1, source_target_pairs={{0,2},{2,0},{1,3},{3,1},{4,6},{6,4},{5,7},{7,5},{8,10},{10,8},{9,1... | collective-permute-start | bytes 442376 | tf_op jit(solution)/shard_map/ppermute | solution.py:20

commit v5 on v4

--- a/solution.py
+++ b/solution.py
@@ -147,11 +147,13 @@
 
 def gather_rows_body(n_gy, n_gz, *refs):
     where = position()
-    pieces, out, total = refs[:-2], refs[-2], refs[-1]
+    pieces, outs, total = refs[:n_gy], refs[n_gy:-1], refs[-1]
     for k in range(n_gy):
         for j in range(n_gz):
             total[lax.rem(where[1] + n_gy - k, n_gy) * n_gz + j] = pieces[k][j].astype(F32)
-    out[...] = jnp.concatenate([total[i] for i in range(n_gy * n_gz)], axis=0).astype(BF16)
+    value = jnp.concatenate([total[i] for i in range(n_gy * n_gz)], axis=0).astype(BF16)
+    for out in outs:
+        out[...] = value
 
 
 def output_body(n_gx, n_gy, n_gz, chunk, *refs):
@@ -258,15 +260,15 @@
     )
 
     pieces = [shift(mixed[k], "gy", k) if k else mixed[k] for k in range(n_gy)]
-    block = call(
+    copies = call(
         functools.partial(gather_rows_body, n_gy, n_gz),
-        [struct((part, width), BF16)],
+        [struct((part, width), BF16)] * n_gx,
         pieces,
         [VMEM] * n_gy,
         scratch=[pltpu.VMEM((n_gy * n_gz, each, width), F32)],
         name="mixed_rows",
-    )[0]
-    blocks = [block] + [shift(block, "gx", k) for k in range(1, n_gx)]
+    )
+    blocks = [copies[0]] + [shift(copies[k], "gx", k) for k in range(1, n_gx)]
     columns = o_weight.shape[1]
     chunk = largest_divisor(columns, 768, 128)
     terms = call(

time: 47.8 us -> 46.6 us (0.975)
  waiting for transfers between devices: 21.9 us -> 20.2 us
    ppermute x17, waiting for transfers between devices: 21.9 us -> 20.2 us  [shift(): lax.ppermute(array, axis, [(s, (s + by) % size) for s in range(size)])]
where the time goes in v5:
time: 46.6 us; the launch traced here: 46.4 us
  waiting for transfers between devices  20.2 us (43%)
  starting transfers between devices  18.6 us (40%)
  Pallas kernels  6.53 us (14%)
  local copies, waits for them, and re-layouts  0.95 us (2%)
    ppermute x17, waiting for transfers between devices, shift(): lax.ppermute(array, axis, [(s, (s + by) % size) for s in range(size)])  20.2 us
    ppermute x17, starting transfers between devices, shift(): lax.ppermute(array, axis, [(s, (s + by) % size) for s in range(size)])  18.6 us
    pallas_call x8, Pallas kernels, call(): pl.pallas_call(body, out_shape=list(outs), in_specs=in_specs, out_specs=[...  6.53 us
    unnamed x18, local copies, waits for them, and re-layouts  0.95 us
  transfers between devices with their start and end apart: 17, of which 12 were waited for; matrix products, arithmetic and copies ran while one was open for 0% of the time, Pallas kernels for 1%

profile of v5, /device:TPU:0, one launch (start us, length us, event | category | flops | bytes accessed | tf_op | source)
XLA Modules:
  0.0 46.4 jit_solution(12886291094928756101)
XLA Ops:
  0.0 2.9 %collective-permute-start.2 = (bf16[16,4608]{1,0:T(8,128)(2,1)}, bf16[16,4608]{1,0:T(8,128)(2,1)S(1)}, u32[]{:S(2)}, u32[]{:S(2)}) collective-permute-start(bf16[16,4608]{1,0:T(8,128)(2,1)} %tokens.1), channel_id=1, source_target_pairs={{0,2},{2,0},{1,3},{3,1},{4,6},{6,4},{5,7},{7,5},{8,10},{10,8},{9,1... | collective-permute-start | bytes 442376 | tf_op jit(solution)/shard_map/ppermute | solution.py:20
  2.9 4.1 %collective-permute-done.2.refs_2_ = bf16[16,4608]{1,0:T(8,128)(2,1)S(1)} collective-permute-done((bf16[16,4608]{1,0:T(8,128)(2,1)}, bf16[16,4608]{1,0:T(8,128)(2,1)S(1)}, u32[]{:S(2)}, u32[]{:S(2)}) %collective-permute-start.2) | collective-permute-done | bytes 147488 | tf_op jit(solution)/shard_map/ppermute | solution.py:20
  7.0 0.9 %copy-done.4 = bf16[16,4608]{1,0:T(8,128)(2,1)S(1)} copy-done((bf16[16,4608]{1,0:T(8,128)(2,1)S(1)}, bf16[16,4608]{1,0:T(8,128)(2,1)}, u32[]{:S(2)}) %copy-start.4) | copy-done | bytes 147480
  7.9 0.2 own_tokens.1.refs_0_
  8.1 0.0 copy-start.2
  8.1 0.2 collective-permute-done.3.refs_3_
  8.4 2.0 %query_terms.1 = (bf16[16,1536]{1,0:T(8,128)(2,1)S(1)}, bf16[16,1536]{1,0:T(8,128)(2,1)S(1)}, bf16[16,1536]{1,0:T(8,128)(2,1)S(1)}, bf16[16,1536]{1,0:T(8,128)(2,1)S(1)}) custom-call(bf16[16,4608]{1,0:T(8,128)(2,1)S(1)} %own_tokens.1.refs_0_, bf16[16,4608]{1,0:T(8,128)(2,1)S(1)} %collective-permute-done.1.refs_1_, ...), custom_call_target="tpu_custom_call" | custom-call | flops 905969664 | bytes 14942208 | tf_op jit(solution)/shard_map/query_terms/pallas_call | solution.py:38
  10.4 1.9 %collective-permute-start.4 = (bf16[16,1536]{1,0:T(8,128)(2,1)S(1)}, bf16[16,1536]{1,0:T(8,128)(2,1)S(1)}, u32[]{:S(2)}, u32[]{:S(2)}) collective-permute-start(bf16[16,1536]{1,0:T(8,128)(2,1)S(1)} %get-tuple-element.22), channel_id=1, source_target_pairs={{0,4},{4,8},{8,12},{12,0},{1,5},{5,9},{9,13},{13,1},{2,6},{6,10},{... | collective-permute-start | bytes 147464 | tf_op jit(solution)/shard_map/ppermute | solution.py:20
  12.3 2.6 %collective-permute-start.5 = (bf16[16,1536]{1,0:T(8,128)(2,1)S(1)}, bf16[16,1536]{1,0:T(8,128)(2,1)S(1)}, u32[]{:S(2)}, u32[]{:S(2)}) collective-permute-start(bf16[16,1536]{1,0:T(8,128)(2,1)S(1)} %get-tuple-element.23), channel_id=1, source_target_pairs={{0,8},{4,12},{8,0},{12,4},{1,9},{5,13},{9,1},{13,5},{2,10},{6,14},... | collective-permute-start | bytes 147464 | tf_op jit(solution)/shard_map/ppermute | solution.py:20
  14.9 1.3 %collective-permute-start.6 = (bf16[16,1536]{1,0:T(8,128)(2,1)S(1)}, bf16[16,1536]{1,0:T(8,128)(2,1)S(1)}, u32[]{:S(2)}, u32[]{:S(2)}) collective-permute-start(bf16[16,1536]{1,0:T(8,128)(2,1)S(1)} %get-tuple-element.24), channel_id=1, source_target_pairs={{0,12},{4,0},{8,4},{12,8},{1,13},{5,1},{9,5},{13,9},{2,14},{6,2},{... | collective-permute-start | bytes 147464 | tf_op jit(solution)/shard_map/ppermute | solution.py:20
  16.2 0.5 %collective-permute-start.9 = (bf16[4,512,256]{2,1,0:T(8,128)(2,1)S(1)}, bf16[4,512,256]{2,1,0:T(8,128)(2,1)S(1)}, u32[]{:S(2)}, u32[]{:S(2)}) collective-permute-start(bf16[4,512,256]{2,1,0:T(8,128)(2,1)S(1)} %copy-done.2), channel_id=1, source_target_pairs={{0,1},{1,0},{2,3},{3,2},{4,5},{5,4},{6,7},{7,6},{8,9},{9,8},{10,11... | collective-permute-start | bytes 3145736 | tf_op jit(solution)/shard_map/ppermute | solution.py:20
  16.7 2.1 %collective-permute-done.5.refs_2_ = bf16[16,1536]{1,0:T(8,128)(2,1)S(1)} collective-permute-done((bf16[16,1536]{1,0:T(8,128)(2,1)S(1)}, bf16[16,1536]{1,0:T(8,128)(2,1)S(1)}, u32[]{:S(2)}, u32[]{:S(2)}) %collective-permute-start.5) | collective-permute-done | bytes 49184 | tf_op jit(solution)/shard_map/ppermute | solution.py:20
  18.8 0.3 collective-permute-done.6.refs_3_
  19.2 1.6 %collective-permute-start.7 = (bf16[2,4,1536]{2,1,0:T(4,128)(2,1)S(1)}, bf16[2,4,1536]{2,1,0:T(4,128)(2,1)S(1)}, u32[]{:S(2)}, u32[]{:S(2)}) collective-permute-start(bf16[2,4,1536]{2,1,0:T(4,128)(2,1)S(1)} %get-tuple-element.26), channel_id=1, source_target_pairs={{0,2},{2,0},{1,3},{3,1},{4,6},{6,4},{5,7},{7,5},{8,10},{10,8},{9,1... | collective-permute-start | bytes 73736 | tf_op jit(solution)/shard_map/ppermute | solution.py:20
  20.8 1.1 %collective-permute-done.refs_1_ = s32[4]{0:T(128)S(1)} collective-permute-done((s32[4]{0:T(128)S(1)}, s32[4]{0:T(128)S(1)}, u32[]{:S(2)}, u32[]{:S(2)}) %collective-permute-start) | collective-permute-done | bytes 48 | tf_op jit(solution)/shard_map/ppermute | solution.py:20
  21.9 1.2 %collective-permute-done.7.refs_3_ = bf16[2,4,1536]{2,1,0:T(4,128)(2,1)S(1)} collective-permute-done((bf16[2,4,1536]{2,1,0:T(4,128)(2,1)S(1)}, bf16[2,4,1536]{2,1,0:T(4,128)(2,1)S(1)}, u32[]{:S(2)}, u32[]{:S(2)}) %collective-permute-start.7) | collective-permute-done | bytes 24608 | tf_op jit(solution)/shard_map/ppermute | solution.py:20
  23.1 1.5 %attention.1 = (bf16[2,4,1536]{2,1,0:T(4,128)(2,1)S(1)}, bf16[2,4,1536]{2,1,0:T(4,128)(2,1)S(1)}) custom-call(s32[4]{0:T(128)S(1)} %copy-done.3, s32[4]{0:T(128)S(1)} %collective-permute-done.refs_1_, bf16[2,4,1536]{2,1,0:T(4,128)(2,1)S(1)} %get-tuple-element.25.refs_2_, bf16[2,4,1536]{2,1,0:T(4,128)(2,1)S(1)} %collective-permute-done.7.refs_3_, ...), custom_call_target="tpu_custom_call" | custom-call | bytes 4292640 | tf_op jit(solution)/shard_map/attention/pallas_call | solution.py:38
  24.6 1.6 %collective-permute-start.10 = (bf16[2,4,1536]{2,1,0:T(4,128)(2,1)S(1)}, bf16[2,4,1536]{2,1,0:T(4,128)(2,1)S(1)}, u32[]{:S(2)}, u32[]{:S(2)}) collective-permute-start(bf16[2,4,1536]{2,1,0:T(4,128)(2,1)S(1)} %get-tuple-element.28), channel_id=1, source_target_pairs={{0,2},{2,0},{1,3},{3,1},{4,6},{6,4},{5,7},{7,5},{8,10},{10,8},{9,1... | collective-permute-start | bytes 73736 | tf_op jit(solution)/shard_map/ppermute | solution.py:20
  26.2 2.3 %collective-permute-done.10.refs_1_ = bf16[2,4,1536]{2,1,0:T(4,128)(2,1)S(1)} collective-permute-done((bf16[2,4,1536]{2,1,0:T(4,128)(2,1)S(1)}, bf16[2,4,1536]{2,1,0:T(4,128)(2,1)S(1)}, u32[]{:S(2)}, u32[]{:S(2)}) %collective-permute-start.10) | collective-permute-done | bytes 24608 | tf_op jit(solution)/shard_map/ppermute | solution.py:20
  28.6 1.1 %collective-permute-start.11 = (bf16[16,1536]{1,0:T(8,128)(2,1)S(1)}, bf16[16,1536]{1,0:T(8,128)(2,1)S(1)}, u32[]{:S(2)}, u32[]{:S(2)}) collective-permute-start(bf16[16,1536]{1,0:T(8,128)(2,1)S(1)} %get-tuple-element.30), channel_id=1, source_target_pairs={{0,4},{4,8},{8,12},{12,0},{1,5},{5,9},{9,13},{13,1},{2,6},{6,10},{... | collective-permute-start | bytes 147464 | tf_op jit(solution)/shard_map/ppermute | solution.py:20
  29.7 2.4 %collective-permute-start.12 = (bf16[16,1536]{1,0:T(8,128)(2,1)S(1)}, bf16[16,1536]{1,0:T(8,128)(2,1)S(1)}, u32[]{:S(2)}, u32[]{:S(2)}) collective-permute-start(bf16[16,1536]{1,0:T(8,128)(2,1)S(1)} %get-tuple-element.31), channel_id=1, source_target_pairs={{0,8},{4,12},{8,0},{12,4},{1,9},{5,13},{9,1},{13,5},{2,10},{6,14},... | collective-permute-start | bytes 147464 | tf_op jit(solution)/shard_map/ppermute | solution.py:20
  32.1 0.5 %collective-permute-start.13 = (bf16[16,1536]{1,0:T(8,128)(2,1)S(1)}, bf16[16,1536]{1,0:T(8,128)(2,1)S(1)}, u32[]{:S(2)}, u32[]{:S(2)}) collective-permute-start(bf16[16,1536]{1,0:T(8,128)(2,1)S(1)} %get-tuple-element.32), channel_id=1, source_target_pairs={{0,12},{4,0},{8,4},{12,8},{1,13},{5,1},{9,5},{13,9},{2,14},{6,2},{... | collective-permute-start | bytes 147464 | tf_op jit(solution)/shard_map/ppermute | solution.py:20
  32.6 1.9 %collective-permute-done.11.refs_1_ = bf16[16,1536]{1,0:T(8,128)(2,1)S(1)} collective-permute-done((bf16[16,1536]{1,0:T(8,128)(2,1)S(1)}, bf16[16,1536]{1,0:T(8,128)(2,1)S(1)}, u32[]{:S(2)}, u32[]{:S(2)}) %collective-permute-start.11) | collective-permute-done | bytes 49184 | tf_op jit(solution)/shard_map/ppermute | solution.py:20
  34.5 1.0 %collective-permute-done.12.refs_2_ = bf16[16,1536]{1,0:T(8,128)(2,1)S(1)} collective-permute-done((bf16[16,1536]{1,0:T(8,128)(2,1)S(1)}, bf16[16,1536]{1,0:T(8,128)(2,1)S(1)}, u32[]{:S(2)}, u32[]{:S(2)}) %collective-permute-start.12) | collective-permute-done | bytes 49184 | tf_op jit(solution)/shard_map/ppermute | solution.py:20
  35.6 0.7 %collective-permute-done.13.refs_3_ = bf16[16,1536]{1,0:T(8,128)(2,1)S(1)} collective-permute-done((bf16[16,1536]{1,0:T(8,128)(2,1)S(1)}, bf16[16,1536]{1,0:T(8,128)(2,1)S(1)}, u32[]{:S(2)}, u32[]{:S(2)}) %collective-permute-start.13) | collective-permute-done | bytes 49184 | tf_op jit(solution)/shard_map/ppermute | solution.py:20
  36.2 2.0 %output_terms.1 = (bf16[16,4608]{1,0:T(8,128)(2,1)S(1)}, bf16[16,4608]{1,0:T(8,128)(2,1)S(1)}, bf16[16,4608]{1,0:T(8,128)(2,1)S(1)}, bf16[16,4608]{1,0:T(8,128)(2,1)S(1)}) custom-call(bf16[16,1536]{1,0:T(8,128)(2,1)S(1)} %get-tuple-element.29.refs_0_, bf16[16,1536]{1,0:T(8,128)(2,1)S(1)} %collective-permute-done.11.refs_1_, ...), custom_call_target="tpu_custom_call" | custom-call | flops 905969664 | bytes 14942208 | tf_op jit(solution)/shard_map/output_terms/pallas_call | solution.py:38
  38.3 0.1 collective-permute-start.15
  38.3 0.5 %collective-permute-start.14 = (bf16[16,4608]{1,0:T(8,128)(2,1)S(1)}, bf16[16,4608]{1,0:T(8,128)(2,1)S(1)}, u32[]{:S(2)}, u32[]{:S(2)}) collective-permute-start(bf16[16,4608]{1,0:T(8,128)(2,1)S(1)} %get-tuple-element.34), channel_id=1, source_target_pairs={{0,1},{1,0},{2,3},{3,2},{4,5},{5,4},{6,7},{7,6},{8,9},{9,8},{10,11... | collective-permute-start | bytes 442376 | tf_op jit(solution)/shard_map/ppermute | solution.py:20
  38.8 0.9 %collective-permute-done.15.refs_1_ = bf16[16,4608]{1,0:T(8,128)(2,1)S(1)} collective-permute-done((bf16[16,4608]{1,0:T(8,128)(2,1)S(1)}, bf16[16,4608]{1,0:T(8,128)(2,1)S(1)}, u32[]{:S(2)}, u32[]{:S(2)}) %collective-permute-start.15) | collective-permute-done | bytes 147488 | tf_op jit(solution)/shard_map/ppermute | solution.py:20
  39.7 1.6 %collective-permute-start.16 = (bf16[16,4608]{1,0:T(8,128)(2,1)S(1)}, bf16[16,4608]{1,0:T(8,128)(2,1)S(1)}, u32[]{:S(2)}, u32[]{:S(2)}) collective-permute-start(bf16[16,4608]{1,0:T(8,128)(2,1)S(1)} %pair_sum.1), channel_id=1, source_target_pairs={{0,2},{2,0},{1,3},{3,1},{4,6},{6,4},{5,7},{7,5},{8,10},{10,8},{9,1... | collective-permute-start | bytes 442376 | tf_op jit(solution)/shard_map/ppermute | solution.py:20
  41.3 4.4 %collective-permute-done.16.refs_2_ = bf16[16,4608]{1,0:T(8,128)(2,1)S(1)} collective-permute-done((bf16[16,4608]{1,0:T(8,128)(2,1)S(1)}, bf16[16,4608]{1,0:T(8,128)(2,1)S(1)}, u32[]{:S(2)}, u32[]{:S(2)}) %collective-permute-start.16) | collective-permute-done | bytes 147488 | tf_op jit(solution)/shard_map/ppermute | solution.py:20
  45.7 0.7 %output_sum.1 = bf16[16,4608]{1,0:T(8,128)(2,1)} custom-call(bf16[16,4608]{1,0:T(8,128)(2,1)S(1)} %get-tuple-element.33.refs_0_, bf16[16,4608]{1,0:T(8,128)(2,1)S(1)} %collective-permute-done.14.refs_1_, bf16[16,4608]{1,0:T(8,128)(2,1)S(1)} %collective-permute-done.16.refs_2_), custom_call_target="tpu_custom_call" | custom-call | bytes 589824 | tf_op jit(solution)/shard_map/output_sum/pallas_call | solution.py:38
  (29 shorter events, 0.2 us)
Async XLA Ops:
  0.0 8.4 %copy-start = (bf16[4608,1536]{1,0:T(8,128)(2,1)S(1)}, bf16[4608,1536]{1,0:T(8,128)(2,1)}, u32[]{:S(2)}) copy-start(bf16[4608,1536]{1,0:T(8,128)(2,1)} %refs_4_.3) | copy-start | bytes 42467332
  0.0 7.0 %collective-permute-start.2 = (bf16[16,4608]{1,0:T(8,128)(2,1)}, bf16[16,4608]{1,0:T(8,128)(2,1)S(1)}, u32[]{:S(2)}, u32[]{:S(2)}) collective-permute-start(bf16[16,4608]{1,0:T(8,128)(2,1)} %tokens.1), channel_id=1, source_target_pairs={{0,2},{2,0},{1,3},{3,1},{4,6},{6,4},{5,7},{7,5},{8,10},{10,8},{9,1... | collective-permute-start | bytes 442376 | tf_op jit(solution)/shard_map/ppermute | solution.py:20
  2.9 5.2 %collective-permute-start.1 = (bf16[16,4608]{1,0:T(8,128)(2,1)}, bf16[16,4608]{1,0:T(8,128)(2,1)S(1)}, u32[]{:S(2)}, u32[]{:S(2)}) collective-permute-start(bf16[16,4608]{1,0:T(8,128)(2,1)} %tokens.1), channel_id=1, source_target_pairs={{0,1},{1,0},{2,3},{3,2},{4,5},{5,4},{6,7},{7,6},{8,9},{9,8},{10,11... | collective-permute-start | bytes 442376 | tf_op jit(solution)/shard_map/ppermute | solution.py:20
  7.0 1.4 %collective-permute-start.3 = (bf16[16,4608]{1,0:T(8,128)(2,1)S(1)}, bf16[16,4608]{1,0:T(8,128)(2,1)S(1)}, u32[]{:S(2)}, u32[]{:S(2)}) collective-permute-start(bf16[16,4608]{1,0:T(8,128)(2,1)S(1)} %collective-permute-done.2.refs_2_), channel_id=1, source_target_pairs={{0,1},{1,0},{2,3},{3,2},{4,5},{5,4},{6,7},{7,6},{8,9},{9,8},{10,11... | collective-permute-start | bytes 442376 | tf_op jit(solution)/shard_map/ppermute | solution.py:20
  7.0 0.9 %copy-start.4 = (bf16[16,4608]{1,0:T(8,128)(2,1)S(1)}, bf16[16,4608]{1,0:T(8,128)(2,1)}, u32[]{:S(2)}) copy-start(bf16[16,4608]{1,0:T(8,128)(2,1)} %tokens.1) | copy-start | bytes 442372
  8.1 8.1 %copy-start.1 = (bf16[4,512,256]{2,1,0:T(8,128)(2,1)S(1)}, bf16[4,512,256]{2,1,0:T(8,128)(2,1)}, u32[]{:S(2)}) copy-start(bf16[4,512,256]{2,1,0:T(8,128)(2,1)} %refs_4_.4) | copy-start | bytes 3145732
  8.1 8.1 %copy-start.2 = (bf16[4,512,256]{2,1,0:T(8,128)(2,1)S(1)}, bf16[4,512,256]{2,1,0:T(8,128)(2,1)}, u32[]{:S(2)}) copy-start(bf16[4,512,256]{2,1,0:T(8,128)(2,1)} %refs_6_.1) | copy-start | bytes 3145732
  8.4 27.8 %slice-start = ((s8[14155776]{0:T(1024)(128)(4,1)}), s8[1572864]{0:T(1024)(128)(4,1)S(1)}, s32[]{:S(2)}) async-start(s8[14155776]{0:T(1024)(128)(4,1)} %bitcast), calls=%async_computation | async-start | bytes 3145728
  8.4 27.8 %slice-start.1 = ((s8[14155776]{0:T(1024)(128)(4,1)}), s8[4194304]{0:T(1024)(128)(4,1)S(1)}, s32[]{:S(2)}) async-start(s8[14155776]{0:T(1024)(128)(4,1)} %bitcast), calls=%async_computation.1 | async-start | bytes 8388608
  10.4 6.3 %collective-permute-start.4 = (bf16[16,1536]{1,0:T(8,128)(2,1)S(1)}, bf16[16,1536]{1,0:T(8,128)(2,1)S(1)}, u32[]{:S(2)}, u32[]{:S(2)}) collective-permute-start(bf16[16,1536]{1,0:T(8,128)(2,1)S(1)} %get-tuple-element.22), channel_id=1, source_target_pairs={{0,4},{4,8},{8,12},{12,0},{1,5},{5,9},{9,13},{13,1},{2,6},{6,10},{... | collective-permute-start | bytes 147464 | tf_op jit(solution)/shard_map/ppermute | solution.py:20
  12.3 6.6 %collective-permute-start.5 = (bf16[16,1536]{1,0:T(8,128)(2,1)S(1)}, bf16[16,1536]{1,0:T(8,128)(2,1)S(1)}, u32[]{:S(2)}, u32[]{:S(2)}) collective-permute-start(bf16[16,1536]{1,0:T(8,128)(2,1)S(1)} %get-tuple-element.23), channel_id=1, source_target_pairs={{0,8},{4,12},{8,0},{12,4},{1,9},{5,13},{9,1},{13,5},{2,10},{6,14},... | collective-permute-start | bytes 147464 | tf_op jit(solution)/shard_map/ppermute | solution.py:20
  14.9 4.3 %collective-permute-start.6 = (bf16[16,1536]{1,0:T(8,128)(2,1)S(1)}, bf16[16,1536]{1,0:T(8,128)(2,1)S(1)}, u32[]{:S(2)}, u32[]{:S(2)}) collective-permute-start(bf16[16,1536]{1,0:T(8,128)(2,1)S(1)} %get-tuple-element.24), channel_id=1, source_target_pairs={{0,12},{4,0},{8,4},{12,8},{1,13},{5,1},{9,5},{13,9},{2,14},{6,2},{... | collective-permute-start | bytes 147464 | tf_op jit(solution)/shard_map/ppermute | solution.py:20
  16.2 6.9 %collective-permute-start.8 = (bf16[4,512,256]{2,1,0:T(8,128)(2,1)S(1)}, bf16[4,512,256]{2,1,0:T(8,128)(2,1)S(1)}, u32[]{:S(2)}, u32[]{:S(2)}) collective-permute-start(bf16[4,512,256]{2,1,0:T(8,128)(2,1)S(1)} %copy-done.1), channel_id=1, source_target_pairs={{0,1},{1,0},{2,3},{3,2},{4,5},{5,4},{6,7},{7,6},{8,9},{9,8},{10,11... | collective-permute-start | bytes 3145736 | tf_op jit(solution)/shard_map/ppermute | solution.py:20
  16.2 6.9 %collective-permute-start.9 = (bf16[4,512,256]{2,1,0:T(8,128)(2,1)S(1)}, bf16[4,512,256]{2,1,0:T(8,128)(2,1)S(1)}, u32[]{:S(2)}, u32[]{:S(2)}) collective-permute-start(bf16[4,512,256]{2,1,0:T(8,128)(2,1)S(1)} %copy-done.2), channel_id=1, source_target_pairs={{0,1},{1,0},{2,3},{3,2},{4,5},{5,4},{6,7},{7,6},{8,9},{9,8},{10,11... | collective-permute-start | bytes 3145736 | tf_op jit(solution)/shard_map/ppermute | solution.py:20
  19.2 1.6 %copy-start.3 = (s32[4]{0:T(128)S(1)}, s32[4]{0:T(128)}, u32[]{:S(2)}) copy-start(s32[4]{0:T(128)} %refs_0_.1) | copy-start | bytes 52
  19.2 17.0 %slice-start.2 = ((s8[14155776]{0:T(1024)(128)(4,1)}), s8[4194304]{0:T(1024)(128)(4,1)S(1)}, s32[]{:S(2)}) async-start(s8[14155776]{0:T(1024)(128)(4,1)} %bitcast), calls=%async_computation.2 | async-start | bytes 8388608
  19.2 17.0 %slice-start.3 = ((s8[14155776]{0:T(1024)(128)(4,1)}), s8[4194304]{0:T(1024)(128)(4,1)S(1)}, s32[]{:S(2)}) async-start(s8[14155776]{0:T(1024)(128)(4,1)} %bitcast), calls=%async_computation.3 | async-start | bytes 8388608
  19.2 3.9 %collective-permute-start.7 = (bf16[2,4,1536]{2,1,0:T(4,128)(2,1)S(1)}, bf16[2,4,1536]{2,1,0:T(4,128)(2,1)S(1)}, u32[]{:S(2)}, u32[]{:S(2)}) collective-permute-start(bf16[2,4,1536]{2,1,0:T(4,128)(2,1)S(1)} %get-tuple-element.26), channel_id=1, source_target_pairs={{0,2},{2,0},{1,3},{3,1},{4,6},{6,4},{5,7},{7,5},{8,10},{10,8},{9,1... | collective-permute-start | bytes 73736 | tf_op jit(solution)/shard_map/ppermute | solution.py:20
  20.8 1.1 %collective-permute-start = (s32[4]{0:T(128)S(1)}, s32[4]{0:T(128)S(1)}, u32[]{:S(2)}, u32[]{:S(2)}) collective-permute-start(s32[4]{0:T(128)S(1)} %copy-done.3), channel_id=1, source_target_pairs={{0,1},{1,0},{2,3},{3,2},{4,5},{5,4},{6,7},{7,6},{8,9},{9,8},{10,11... | collective-permute-start | bytes 56 | tf_op jit(solution)/shard_map/ppermute | solution.py:20
  24.6 3.9 %collective-permute-start.10 = (bf16[2,4,1536]{2,1,0:T(4,128)(2,1)S(1)}, bf16[2,4,1536]{2,1,0:T(4,128)(2,1)S(1)}, u32[]{:S(2)}, u32[]{:S(2)}) collective-permute-start(bf16[2,4,1536]{2,1,0:T(4,128)(2,1)S(1)} %get-tuple-element.28), channel_id=1, source_target_pairs={{0,2},{2,0},{1,3},{3,1},{4,6},{6,4},{5,7},{7,5},{8,10},{10,8},{9,1... | collective-permute-start | bytes 73736 | tf_op jit(solution)/shard_map/ppermute | solution.py:20
  28.6 6.0 %collective-permute-start.11 = (bf16[16,1536]{1,0:T(8,128)(2,1)S(1)}, bf16[16,1536]{1,0:T(8,128)(2,1)S(1)}, u32[]{:S(2)}, u32[]{:S(2)}) collective-permute-start(bf16[16,1536]{1,0:T(8,128)(2,1)S(1)} %get-tuple-element.30), channel_id=1, source_target_pairs={{0,4},{4,8},{8,12},{12,0},{1,5},{5,9},{9,13},{13,1},{2,6},{6,10},{... | collective-permute-start | bytes 147464 | tf_op jit(solution)/shard_map/ppermute | solution.py:20
  29.7 5.9 %collective-permute-start.12 = (bf16[16,1536]{1,0:T(8,128)(2,1)S(1)}, bf16[16,1536]{1,0:T(8,128)(2,1)S(1)}, u32[]{:S(2)}, u32[]{:S(2)}) collective-permute-start(bf16[16,1536]{1,0:T(8,128)(2,1)S(1)} %get-tuple-element.31), channel_id=1, source_target_pairs={{0,8},{4,12},{8,0},{12,4},{1,9},{5,13},{9,1},{13,5},{2,10},{6,14},... | collective-permute-start | bytes 147464 | tf_op jit(solution)/shard_map/ppermute | solution.py:20
  32.1 4.1 %collective-permute-start.13 = (bf16[16,1536]{1,0:T(8,128)(2,1)S(1)}, bf16[16,1536]{1,0:T(8,128)(2,1)S(1)}, u32[]{:S(2)}, u32[]{:S(2)}) collective-permute-start(bf16[16,1536]{1,0:T(8,128)(2,1)S(1)} %get-tuple-element.32), channel_id=1, source_target_pairs={{0,12},{4,0},{8,4},{12,8},{1,13},{5,1},{9,5},{13,9},{2,14},{6,2},{... | collective-permute-start | bytes 147464 | tf_op jit(solution)/shard_map/ppermute | solution.py:20
  38.3 1.4 %collective-permute-start.15 = (bf16[16,4608]{1,0:T(8,128)(2,1)S(1)}, bf16[16,4608]{1,0:T(8,128)(2,1)S(1)}, u32[]{:S(2)}, u32[]{:S(2)}) collective-permute-start(bf16[16,4608]{1,0:T(8,128)(2,1)S(1)} %get-tuple-element.36), channel_id=1, source_target_pairs={{0,1},{1,0},{2,3},{3,2},{4,5},{5,4},{6,7},{7,6},{8,9},{9,8},{10,11... | collective-permute-start | bytes 442376 | tf_op jit(solution)/shard_map/ppermute | solution.py:20
  38.3 3.0 %collective-permute-start.14 = (bf16[16,4608]{1,0:T(8,128)(2,1)S(1)}, bf16[16,4608]{1,0:T(8,128)(2,1)S(1)}, u32[]{:S(2)}, u32[]{:S(2)}) collective-permute-start(bf16[16,4608]{1,0:T(8,128)(2,1)S(1)} %get-tuple-element.34), channel_id=1, source_target_pairs={{0,1},{1,0},{2,3},{3,2},{4,5},{5,4},{6,7},{7,6},{8,9},{9,8},{10,11... | collective-permute-start | bytes 442376 | tf_op jit(solution)/shard_map/ppermute | solution.py:20
  39.7 6.0 %collective-permute-start.16 = (bf16[16,4608]{1,0:T(8,128)(2,1)S(1)}, bf16[16,4608]{1,0:T(8,128)(2,1)S(1)}, u32[]{:S(2)}, u32[]{:S(2)}) collective-permute-start(bf16[16,4608]{1,0:T(8,128)(2,1)S(1)} %pair_sum.1), channel_id=1, source_target_pairs={{0,2},{2,0},{1,3},{3,1},{4,6},{6,4},{5,7},{7,5},{8,10},{10,8},{9,1... | collective-permute-start | bytes 442376 | tf_op jit(solution)/shard_map/ppermute | solution.py:20

commit v6 on v5

--- a/solution.py
+++ b/solution.py
@@ -18,6 +18,22 @@
 def shift(array, axis, by):
     size = lax.axis_size(axis)
     return lax.ppermute(array, axis, [(s, (s + by) % size) for s in range(size)])
+
+
+def across():
+    return 1 if lax.axis_size("gz") == 2 else 0
+
+
+def hop(array, axis, by):
+    size, cores = lax.axis_size(axis), lax.axis_size("gz")
+    pairs = [
+        (s * cores + c, (s + by) % size * cores + (c + across()) % cores) for s in range(size) for c in range(cores)
+    ]
+    return lax.ppermute(array, (axis, "gz"), pairs)
+
+
+def hops(arrays, axis):
+    return [hop(array, axis, by) if by else array for by, array in enumerate(arrays)]
 
 
 def position():
@@ -76,7 +92,8 @@
     block = pieces[0].shape[0]
     for k in range(n_gy):
         for j in range(n_gz):
-            at = lax.rem(where[1] + n_gy - k, n_gy) * n_gz + lax.rem(where[2] + n_gz - j, n_gz)
+            core = where[2] + n_gz - j
+            at = lax.rem(where[1] + n_gy - k, n_gy) * n_gz + lax.rem(core, n_gz)
             rows[pl.ds(pl.multiple_of(at * block, block), block), :] = pieces[k * n_gz + j][...]
     count = block * n_gy * n_gz
     clear_below(rows, count)
@@ -248,7 +265,7 @@
         beside=20000 * key_cache.size,
         name="query_sum",
     )
-    pieces = [shift(queries[k], "gy", k) if k else queries[k] for k in range(n_gy)]
+    pieces = hops(queries, "gy")
     mixed = call(
         functools.partial(attend_body, n_gy, n_gz),
         [struct((n_gz, each, width), BF16)] * n_gy,
@@ -259,7 +276,7 @@
         name="attention",
     )
 
-    pieces = [shift(mixed[k], "gy", k) if k else mixed[k] for k in range(n_gy)]
+    pieces = hops(mixed, "gy")
     copies = call(
         functools.partial(gather_rows_body, n_gy, n_gz),
         [struct((part, width), BF16)] * n_gx,
@@ -287,7 +304,7 @@
 
     arrived = []
     for k in range(1, n_gy):
-        mine = terms[k * n_gz : (k + 1) * n_gz]
+        mine = [terms[k * n_gz + j] for j in range(n_gz)]
         mine = [mine[0]] + [shift(mine[j], "gz", j) for j in range(1, n_gz)]
         arrived.append(shift(added(mine, "pair_sum") if n_gz > 1 else mine[0], "gy", k))
     mine = [terms[0]] + [shift(terms[j], "gz", j) for j in range(1, n_gz)]

time: 46.6 us -> 46 us (0.987)
  starting transfers between devices: 18.6 us -> 16.8 us
  waiting for transfers between devices: 20.2 us -> 21.3 us
    ppermute x0 -> x2, waiting for transfers between devices: none -> 4.18 us  [hop(): return lax.ppermute(array, (axis, 'gz'), pairs)]
    ppermute x17 -> x15, waiting for transfers between devices: 20.2 us -> 17.1 us  [shift(): lax.ppermute(array, axis, [(s, (s + by) % size) for s in range(size)])]
    ppermute x17 -> x15, starting transfers between devices: 18.6 us -> 16.2 us  [shift(): lax.ppermute(array, axis, [(s, (s + by) % size) for s in range(size)])]
    ppermute x0 -> x2, starting transfers between devices: none -> 0.53 us  [hop(): return lax.ppermute(array, (axis, 'gz'), pairs)]
where the time goes in v6:
time: 46 us; the launch traced here: 45.8 us
  waiting for transfers between devices  21.3 us (46%)
  starting transfers between devices  16.8 us (37%)
  Pallas kernels  6.53 us (14%)
  local copies, waits for them, and re-layouts  1.17 us (3%)
    ppermute x15, waiting for transfers between devices, shift(): lax.ppermute(array, axis, [(s, (s + by) % size) for s in range(size)])  17.1 us
    ppermute x15, starting transfers between devices, shift(): lax.ppermute(array, axis, [(s, (s + by) % size) for s in range(size)])  16.2 us
    pallas_call x8, Pallas kernels, call(): pl.pallas_call(body, out_shape=list(outs), in_specs=in_specs, out_specs=[...  6.53 us
    ppermute x2, waiting for transfers between devices, hop(): return lax.ppermute(array, (axis, 'gz'), pairs)  4.18 us
    unnamed x18, local copies, waits for them, and re-layouts  1.17 us
  transfers between devices with their start and end apart: 17, of which 12 were waited for; matrix products, arithmetic and copies ran while one was open for 0% of the time, Pallas kernels for 1%

profile of v6, /device:TPU:0, one launch (start us, length us, event | category | flops | bytes accessed | tf_op | source)
XLA Modules:
  0.0 45.8 jit_solution(11839638460928012999)
XLA Ops:
  0.0 2.9 %collective-permute-start.2 = (bf16[16,4608]{1,0:T(8,128)(2,1)}, bf16[16,4608]{1,0:T(8,128)(2,1)S(1)}, u32[]{:S(2)}, u32[]{:S(2)}) collective-permute-start(bf16[16,4608]{1,0:T(8,128)(2,1)} %tokens.1), channel_id=1, source_target_pairs={{0,2},{2,0},{1,3},{3,1},{4,6},{6,4},{5,7},{7,5},{8,10},{10,8},{9,1... | collective-permute-start | bytes 442376 | tf_op jit(solution)/shard_map/ppermute | solution.py:20
  2.9 4.1 %collective-permute-done.2.refs_2_ = bf16[16,4608]{1,0:T(8,128)(2,1)S(1)} collective-permute-done((bf16[16,4608]{1,0:T(8,128)(2,1)}, bf16[16,4608]{1,0:T(8,128)(2,1)S(1)}, u32[]{:S(2)}, u32[]{:S(2)}) %collective-permute-start.2) | collective-permute-done | bytes 147488 | tf_op jit(solution)/shard_map/ppermute | solution.py:20
  7.0 0.9 %copy-done.4 = bf16[16,4608]{1,0:T(8,128)(2,1)S(1)} copy-done((bf16[16,4608]{1,0:T(8,128)(2,1)S(1)}, bf16[16,4608]{1,0:T(8,128)(2,1)}, u32[]{:S(2)}) %copy-start.4) | copy-done | bytes 147480
  7.9 0.2 own_tokens.1.refs_0_
  8.1 0.2 collective-permute-done.3.refs_3_
  8.4 2.0 %query_terms.1 = (bf16[16,1536]{1,0:T(8,128)(2,1)S(1)}, bf16[16,1536]{1,0:T(8,128)(2,1)S(1)}, bf16[16,1536]{1,0:T(8,128)(2,1)S(1)}, bf16[16,1536]{1,0:T(8,128)(2,1)S(1)}) custom-call(bf16[16,4608]{1,0:T(8,128)(2,1)S(1)} %own_tokens.1.refs_0_, bf16[16,4608]{1,0:T(8,128)(2,1)S(1)} %collective-permute-done.1.refs_1_, ...), custom_call_target="tpu_custom_call" | custom-call | flops 905969664 | bytes 14942208 | tf_op jit(solution)/shard_map/query_terms/pallas_call | solution.py:54
  10.4 1.9 %collective-permute-start.4 = (bf16[16,1536]{1,0:T(8,128)(2,1)S(1)}, bf16[16,1536]{1,0:T(8,128)(2,1)S(1)}, u32[]{:S(2)}, u32[]{:S(2)}) collective-permute-start(bf16[16,1536]{1,0:T(8,128)(2,1)S(1)} %get-tuple-element.22), channel_id=1, source_target_pairs={{0,4},{4,8},{8,12},{12,0},{1,5},{5,9},{9,13},{13,1},{2,6},{6,10},{... | collective-permute-start | bytes 147464 | tf_op jit(solution)/shard_map/ppermute | solution.py:20
  12.3 2.6 %collective-permute-start.5 = (bf16[16,1536]{1,0:T(8,128)(2,1)S(1)}, bf16[16,1536]{1,0:T(8,128)(2,1)S(1)}, u32[]{:S(2)}, u32[]{:S(2)}) collective-permute-start(bf16[16,1536]{1,0:T(8,128)(2,1)S(1)} %get-tuple-element.23), channel_id=1, source_target_pairs={{0,8},{4,12},{8,0},{12,4},{1,9},{5,13},{9,1},{13,5},{2,10},{6,14},... | collective-permute-start | bytes 147464 | tf_op jit(solution)/shard_map/ppermute | solution.py:20
  14.9 1.3 %collective-permute-start.6 = (bf16[16,1536]{1,0:T(8,128)(2,1)S(1)}, bf16[16,1536]{1,0:T(8,128)(2,1)S(1)}, u32[]{:S(2)}, u32[]{:S(2)}) collective-permute-start(bf16[16,1536]{1,0:T(8,128)(2,1)S(1)} %get-tuple-element.24), channel_id=1, source_target_pairs={{0,12},{4,0},{8,4},{12,8},{1,13},{5,1},{9,5},{13,9},{2,14},{6,2},{... | collective-permute-start | bytes 147464 | tf_op jit(solution)/shard_map/ppermute | solution.py:20
  16.2 0.5 %collective-permute-start.9 = (bf16[4,512,256]{2,1,0:T(8,128)(2,1)S(1)}, bf16[4,512,256]{2,1,0:T(8,128)(2,1)S(1)}, u32[]{:S(2)}, u32[]{:S(2)}) collective-permute-start(bf16[4,512,256]{2,1,0:T(8,128)(2,1)S(1)} %copy-done.2), channel_id=1, source_target_pairs={{0,1},{1,0},{2,3},{3,2},{4,5},{5,4},{6,7},{7,6},{8,9},{9,8},{10,11... | collective-permute-start | bytes 3145736 | tf_op jit(solution)/shard_map/ppermute | solution.py:20
  16.7 2.1 %collective-permute-done.5.refs_2_ = bf16[16,1536]{1,0:T(8,128)(2,1)S(1)} collective-permute-done((bf16[16,1536]{1,0:T(8,128)(2,1)S(1)}, bf16[16,1536]{1,0:T(8,128)(2,1)S(1)}, u32[]{:S(2)}, u32[]{:S(2)}) %collective-permute-start.5) | collective-permute-done | bytes 49184 | tf_op jit(solution)/shard_map/ppermute | solution.py:20
  18.8 0.3 collective-permute-done.6.refs_3_
  19.2 0.4 collective-permute-start.7
  19.6 0.2 copy-done.3
  19.8 1.1 %collective-permute-start = (s32[4]{0:T(128)S(1)}, s32[4]{0:T(128)S(1)}, u32[]{:S(2)}, u32[]{:S(2)}) collective-permute-start(s32[4]{0:T(128)S(1)} %copy-done.3), channel_id=1, source_target_pairs={{0,1},{1,0},{2,3},{3,2},{4,5},{5,4},{6,7},{7,6},{8,9},{9,8},{10,11... | collective-permute-start | bytes 56 | tf_op jit(solution)/shard_map/ppermute | solution.py:20
  20.9 0.8 %collective-permute-done.refs_1_ = s32[4]{0:T(128)S(1)} collective-permute-done((s32[4]{0:T(128)S(1)}, s32[4]{0:T(128)S(1)}, u32[]{:S(2)}, u32[]{:S(2)}) %collective-permute-start) | collective-permute-done | bytes 48 | tf_op jit(solution)/shard_map/ppermute | solution.py:20
  21.7 1.0 %collective-permute-done.7.refs_3_ = bf16[2,4,1536]{2,1,0:T(4,128)(2,1)S(1)} collective-permute-done((bf16[2,4,1536]{2,1,0:T(4,128)(2,1)S(1)}, bf16[2,4,1536]{2,1,0:T(4,128)(2,1)S(1)}, u32[]{:S(2)}, u32[]{:S(2)}) %collective-permute-start.7) | collective-permute-done | bytes 24608 | tf_op jit(solution)/shard_map/ppermute | solution.py:32
  22.8 1.5 %attention.1 = (bf16[2,4,1536]{2,1,0:T(4,128)(2,1)S(1)}, bf16[2,4,1536]{2,1,0:T(4,128)(2,1)S(1)}) custom-call(s32[4]{0:T(128)S(1)} %copy-done.3, s32[4]{0:T(128)S(1)} %collective-permute-done.refs_1_, bf16[2,4,1536]{2,1,0:T(4,128)(2,1)S(1)} %get-tuple-element.25.refs_2_, bf16[2,4,1536]{2,1,0:T(4,128)(2,1)S(1)} %collective-permute-done.7.refs_3_, ...), custom_call_target="tpu_custom_call" | custom-call | bytes 4292640 | tf_op jit(solution)/shard_map/attention/pallas_call | solution.py:54
  24.3 0.2 collective-permute-start.10
  24.4 3.2 %collective-permute-done.10.refs_1_ = bf16[2,4,1536]{2,1,0:T(4,128)(2,1)S(1)} collective-permute-done((bf16[2,4,1536]{2,1,0:T(4,128)(2,1)S(1)}, bf16[2,4,1536]{2,1,0:T(4,128)(2,1)S(1)}, u32[]{:S(2)}, u32[]{:S(2)}) %collective-permute-start.10) | collective-permute-done | bytes 24608 | tf_op jit(solution)/shard_map/ppermute | solution.py:32
  27.6 1.1 %collective-permute-start.11 = (bf16[16,1536]{1,0:T(8,128)(2,1)S(1)}, bf16[16,1536]{1,0:T(8,128)(2,1)S(1)}, u32[]{:S(2)}, u32[]{:S(2)}) collective-permute-start(bf16[16,1536]{1,0:T(8,128)(2,1)S(1)} %get-tuple-element.30), channel_id=1, source_target_pairs={{0,4},{4,8},{8,12},{12,0},{1,5},{5,9},{9,13},{13,1},{2,6},{6,10},{... | collective-permute-start | bytes 147464 | tf_op jit(solution)/shard_map/ppermute | solution.py:20
  28.7 2.5 %collective-permute-start.12 = (bf16[16,1536]{1,0:T(8,128)(2,1)S(1)}, bf16[16,1536]{1,0:T(8,128)(2,1)S(1)}, u32[]{:S(2)}, u32[]{:S(2)}) collective-permute-start(bf16[16,1536]{1,0:T(8,128)(2,1)S(1)} %get-tuple-element.31), channel_id=1, source_target_pairs={{0,8},{4,12},{8,0},{12,4},{1,9},{5,13},{9,1},{13,5},{2,10},{6,14},... | collective-permute-start | bytes 147464 | tf_op jit(solution)/shard_map/ppermute | solution.py:20
  31.2 0.5 %collective-permute-start.13 = (bf16[16,1536]{1,0:T(8,128)(2,1)S(1)}, bf16[16,1536]{1,0:T(8,128)(2,1)S(1)}, u32[]{:S(2)}, u32[]{:S(2)}) collective-permute-start(bf16[16,1536]{1,0:T(8,128)(2,1)S(1)} %get-tuple-element.32), channel_id=1, source_target_pairs={{0,12},{4,0},{8,4},{12,8},{1,13},{5,1},{9,5},{13,9},{2,14},{6,2},{... | collective-permute-start | bytes 147464 | tf_op jit(solution)/shard_map/ppermute | solution.py:20
  31.7 2.5 %collective-permute-done.11.refs_1_ = bf16[16,1536]{1,0:T(8,128)(2,1)S(1)} collective-permute-done((bf16[16,1536]{1,0:T(8,128)(2,1)S(1)}, bf16[16,1536]{1,0:T(8,128)(2,1)S(1)}, u32[]{:S(2)}, u32[]{:S(2)}) %collective-permute-start.11) | collective-permute-done | bytes 49184 | tf_op jit(solution)/shard_map/ppermute | solution.py:20
  34.2 1.2 %collective-permute-done.12.refs_2_ = bf16[16,1536]{1,0:T(8,128)(2,1)S(1)} collective-permute-done((bf16[16,1536]{1,0:T(8,128)(2,1)S(1)}, bf16[16,1536]{1,0:T(8,128)(2,1)S(1)}, u32[]{:S(2)}, u32[]{:S(2)}) %collective-permute-start.12) | collective-permute-done | bytes 49184 | tf_op jit(solution)/shard_map/ppermute | solution.py:20
  35.4 0.2 collective-permute-done.13.refs_3_
  35.7 2.0 %output_terms.1 = (bf16[16,4608]{1,0:T(8,128)(2,1)S(1)}, bf16[16,4608]{1,0:T(8,128)(2,1)S(1)}, bf16[16,4608]{1,0:T(8,128)(2,1)S(1)}, bf16[16,4608]{1,0:T(8,128)(2,1)S(1)}) custom-call(bf16[16,1536]{1,0:T(8,128)(2,1)S(1)} %get-tuple-element.29.refs_0_, bf16[16,1536]{1,0:T(8,128)(2,1)S(1)} %collective-permute-done.11.refs_1_, ...), custom_call_target="tpu_custom_call" | custom-call | flops 905969664 | bytes 14942208 | tf_op jit(solution)/shard_map/output_terms/pallas_call | solution.py:54
  37.8 0.5 %collective-permute-start.14 = (bf16[16,4608]{1,0:T(8,128)(2,1)S(1)}, bf16[16,4608]{1,0:T(8,128)(2,1)S(1)}, u32[]{:S(2)}, u32[]{:S(2)}) collective-permute-start(bf16[16,4608]{1,0:T(8,128)(2,1)S(1)} %get-tuple-element.34), channel_id=1, source_target_pairs={{0,1},{1,0},{2,3},{3,2},{4,5},{5,4},{6,7},{7,6},{8,9},{9,8},{10,11... | collective-permute-start | bytes 442376 | tf_op jit(solution)/shard_map/ppermute | solution.py:20
  38.3 0.9 %collective-permute-done.15.refs_1_ = bf16[16,4608]{1,0:T(8,128)(2,1)S(1)} collective-permute-done((bf16[16,4608]{1,0:T(8,128)(2,1)S(1)}, bf16[16,4608]{1,0:T(8,128)(2,1)S(1)}, u32[]{:S(2)}, u32[]{:S(2)}) %collective-permute-start.15) | collective-permute-done | bytes 147488 | tf_op jit(solution)/shard_map/ppermute | solution.py:20
  39.2 1.2 %collective-permute-start.16 = (bf16[16,4608]{1,0:T(8,128)(2,1)S(1)}, bf16[16,4608]{1,0:T(8,128)(2,1)S(1)}, u32[]{:S(2)}, u32[]{:S(2)}) collective-permute-start(bf16[16,4608]{1,0:T(8,128)(2,1)S(1)} %pair_sum.1), channel_id=1, source_target_pairs={{0,2},{2,0},{1,3},{3,1},{4,6},{6,4},{5,7},{7,5},{8,10},{10,8},{9,1... | collective-permute-start | bytes 442376 | tf_op jit(solution)/shard_map/ppermute | solution.py:20
  40.4 4.7 %collective-permute-done.16.refs_2_ = bf16[16,4608]{1,0:T(8,128)(2,1)S(1)} collective-permute-done((bf16[16,4608]{1,0:T(8,128)(2,1)S(1)}, bf16[16,4608]{1,0:T(8,128)(2,1)S(1)}, u32[]{:S(2)}, u32[]{:S(2)}) %collective-permute-start.16) | collective-permute-done | bytes 147488 | tf_op jit(solution)/shard_map/ppermute | solution.py:20
  45.1 0.7 %output_sum.1 = bf16[16,4608]{1,0:T(8,128)(2,1)} custom-call(bf16[16,4608]{1,0:T(8,128)(2,1)S(1)} %get-tuple-element.33.refs_0_, bf16[16,4608]{1,0:T(8,128)(2,1)S(1)} %collective-permute-done.14.refs_1_, bf16[16,4608]{1,0:T(8,128)(2,1)S(1)} %collective-permute-done.16.refs_2_), custom_call_target="tpu_custom_call" | custom-call | bytes 589824 | tf_op jit(solution)/shard_map/output_sum/pallas_call | solution.py:54
  (29 shorter events, 0.2 us)
Async XLA Ops:
  0.0 8.4 %copy-start = (bf16[4608,1536]{1,0:T(8,128)(2,1)S(1)}, bf16[4608,1536]{1,0:T(8,128)(2,1)}, u32[]{:S(2)}) copy-start(bf16[4608,1536]{1,0:T(8,128)(2,1)} %refs_4_.3) | copy-start | bytes 42467332
  0.0 7.0 %collective-permute-start.2 = (bf16[16,4608]{1,0:T(8,128)(2,1)}, bf16[16,4608]{1,0:T(8,128)(2,1)S(1)}, u32[]{:S(2)}, u32[]{:S(2)}) collective-permute-start(bf16[16,4608]{1,0:T(8,128)(2,1)} %tokens.1), channel_id=1, source_target_pairs={{0,2},{2,0},{1,3},{3,1},{4,6},{6,4},{5,7},{7,5},{8,10},{10,8},{9,1... | collective-permute-start | bytes 442376 | tf_op jit(solution)/shard_map/ppermute | solution.py:20
  2.9 5.2 %collective-permute-start.1 = (bf16[16,4608]{1,0:T(8,128)(2,1)}, bf16[16,4608]{1,0:T(8,128)(2,1)S(1)}, u32[]{:S(2)}, u32[]{:S(2)}) collective-permute-start(bf16[16,4608]{1,0:T(8,128)(2,1)} %tokens.1), channel_id=1, source_target_pairs={{0,1},{1,0},{2,3},{3,2},{4,5},{5,4},{6,7},{7,6},{8,9},{9,8},{10,11... | collective-permute-start | bytes 442376 | tf_op jit(solution)/shard_map/ppermute | solution.py:20
  7.0 1.4 %collective-permute-start.3 = (bf16[16,4608]{1,0:T(8,128)(2,1)S(1)}, bf16[16,4608]{1,0:T(8,128)(2,1)S(1)}, u32[]{:S(2)}, u32[]{:S(2)}) collective-permute-start(bf16[16,4608]{1,0:T(8,128)(2,1)S(1)} %collective-permute-done.2.refs_2_), channel_id=1, source_target_pairs={{0,1},{1,0},{2,3},{3,2},{4,5},{5,4},{6,7},{7,6},{8,9},{9,8},{10,11... | collective-permute-start | bytes 442376 | tf_op jit(solution)/shard_map/ppermute | solution.py:20
  7.0 0.9 %copy-start.4 = (bf16[16,4608]{1,0:T(8,128)(2,1)S(1)}, bf16[16,4608]{1,0:T(8,128)(2,1)}, u32[]{:S(2)}) copy-start(bf16[16,4608]{1,0:T(8,128)(2,1)} %tokens.1) | copy-start | bytes 442372
  8.1 8.1 %copy-start.1 = (bf16[4,512,256]{2,1,0:T(8,128)(2,1)S(1)}, bf16[4,512,256]{2,1,0:T(8,128)(2,1)}, u32[]{:S(2)}) copy-start(bf16[4,512,256]{2,1,0:T(8,128)(2,1)} %refs_4_.4) | copy-start | bytes 3145732
  8.1 8.1 %copy-start.2 = (bf16[4,512,256]{2,1,0:T(8,128)(2,1)S(1)}, bf16[4,512,256]{2,1,0:T(8,128)(2,1)}, u32[]{:S(2)}) copy-start(bf16[4,512,256]{2,1,0:T(8,128)(2,1)} %refs_6_.1) | copy-start | bytes 3145732
  8.4 27.3 %slice-start = ((s8[14155776]{0:T(1024)(128)(4,1)}), s8[1572864]{0:T(1024)(128)(4,1)S(1)}, s32[]{:S(2)}) async-start(s8[14155776]{0:T(1024)(128)(4,1)} %bitcast), calls=%async_computation | async-start | bytes 3145728
  8.4 27.3 %slice-start.1 = ((s8[14155776]{0:T(1024)(128)(4,1)}), s8[4194304]{0:T(1024)(128)(4,1)S(1)}, s32[]{:S(2)}) async-start(s8[14155776]{0:T(1024)(128)(4,1)} %bitcast), calls=%async_computation.1 | async-start | bytes 8388608
  10.4 6.3 %collective-permute-start.4 = (bf16[16,1536]{1,0:T(8,128)(2,1)S(1)}, bf16[16,1536]{1,0:T(8,128)(2,1)S(1)}, u32[]{:S(2)}, u32[]{:S(2)}) collective-permute-start(bf16[16,1536]{1,0:T(8,128)(2,1)S(1)} %get-tuple-element.22), channel_id=1, source_target_pairs={{0,4},{4,8},{8,12},{12,0},{1,5},{5,9},{9,13},{13,1},{2,6},{6,10},{... | collective-permute-start | bytes 147464 | tf_op jit(solution)/shard_map/ppermute | solution.py:20
  12.3 6.6 %collective-permute-start.5 = (bf16[16,1536]{1,0:T(8,128)(2,1)S(1)}, bf16[16,1536]{1,0:T(8,128)(2,1)S(1)}, u32[]{:S(2)}, u32[]{:S(2)}) collective-permute-start(bf16[16,1536]{1,0:T(8,128)(2,1)S(1)} %get-tuple-element.23), channel_id=1, source_target_pairs={{0,8},{4,12},{8,0},{12,4},{1,9},{5,13},{9,1},{13,5},{2,10},{6,14},... | collective-permute-start | bytes 147464 | tf_op jit(solution)/shard_map/ppermute | solution.py:20
  14.9 4.3 %collective-permute-start.6 = (bf16[16,1536]{1,0:T(8,128)(2,1)S(1)}, bf16[16,1536]{1,0:T(8,128)(2,1)S(1)}, u32[]{:S(2)}, u32[]{:S(2)}) collective-permute-start(bf16[16,1536]{1,0:T(8,128)(2,1)S(1)} %get-tuple-element.24), channel_id=1, source_target_pairs={{0,12},{4,0},{8,4},{12,8},{1,13},{5,1},{9,5},{13,9},{2,14},{6,2},{... | collective-permute-start | bytes 147464 | tf_op jit(solution)/shard_map/ppermute | solution.py:20
  16.2 6.5 %collective-permute-start.8 = (bf16[4,512,256]{2,1,0:T(8,128)(2,1)S(1)}, bf16[4,512,256]{2,1,0:T(8,128)(2,1)S(1)}, u32[]{:S(2)}, u32[]{:S(2)}) collective-permute-start(bf16[4,512,256]{2,1,0:T(8,128)(2,1)S(1)} %copy-done.1), channel_id=1, source_target_pairs={{0,1},{1,0},{2,3},{3,2},{4,5},{5,4},{6,7},{7,6},{8,9},{9,8},{10,11... | collective-permute-start | bytes 3145736 | tf_op jit(solution)/shard_map/ppermute | solution.py:20
  16.2 6.5 %collective-permute-start.9 = (bf16[4,512,256]{2,1,0:T(8,128)(2,1)S(1)}, bf16[4,512,256]{2,1,0:T(8,128)(2,1)S(1)}, u32[]{:S(2)}, u32[]{:S(2)}) collective-permute-start(bf16[4,512,256]{2,1,0:T(8,128)(2,1)S(1)} %copy-done.2), channel_id=1, source_target_pairs={{0,1},{1,0},{2,3},{3,2},{4,5},{5,4},{6,7},{7,6},{8,9},{9,8},{10,11... | collective-permute-start | bytes 3145736 | tf_op jit(solution)/shard_map/ppermute | solution.py:20
  19.2 0.7 %copy-start.3 = (s32[4]{0:T(128)S(1)}, s32[4]{0:T(128)}, u32[]{:S(2)}) copy-start(s32[4]{0:T(128)} %refs_0_.1) | copy-start | bytes 52
  19.2 16.5 %slice-start.2 = ((s8[14155776]{0:T(1024)(128)(4,1)}), s8[4194304]{0:T(1024)(128)(4,1)S(1)}, s32[]{:S(2)}) async-start(s8[14155776]{0:T(1024)(128)(4,1)} %bitcast), calls=%async_computation.2 | async-start | bytes 8388608
  19.2 16.5 %slice-start.3 = ((s8[14155776]{0:T(1024)(128)(4,1)}), s8[4194304]{0:T(1024)(128)(4,1)S(1)}, s32[]{:S(2)}) async-start(s8[14155776]{0:T(1024)(128)(4,1)} %bitcast), calls=%async_computation.3 | async-start | bytes 8388608
  19.2 3.5 %collective-permute-start.7 = (bf16[2,4,1536]{2,1,0:T(4,128)(2,1)S(1)}, bf16[2,4,1536]{2,1,0:T(4,128)(2,1)S(1)}, u32[]{:S(2)}, u32[]{:S(2)}) collective-permute-start(bf16[2,4,1536]{2,1,0:T(4,128)(2,1)S(1)} %get-tuple-element.26), channel_id=1, source_target_pairs={{0,3},{1,2},{2,1},{3,0},{4,7},{5,6},{6,5},{7,4},{8,11},{9,10},{10,... | collective-permute-start | bytes 73736 | tf_op jit(solution)/shard_map/ppermute | solution.py:32
  19.8 1.9 %collective-permute-start = (s32[4]{0:T(128)S(1)}, s32[4]{0:T(128)S(1)}, u32[]{:S(2)}, u32[]{:S(2)}) collective-permute-start(s32[4]{0:T(128)S(1)} %copy-done.3), channel_id=1, source_target_pairs={{0,1},{1,0},{2,3},{3,2},{4,5},{5,4},{6,7},{7,6},{8,9},{9,8},{10,11... | collective-permute-start | bytes 56 | tf_op jit(solution)/shard_map/ppermute | solution.py:20
  24.3 3.3 %collective-permute-start.10 = (bf16[2,4,1536]{2,1,0:T(4,128)(2,1)S(1)}, bf16[2,4,1536]{2,1,0:T(4,128)(2,1)S(1)}, u32[]{:S(2)}, u32[]{:S(2)}) collective-permute-start(bf16[2,4,1536]{2,1,0:T(4,128)(2,1)S(1)} %get-tuple-element.28), channel_id=1, source_target_pairs={{0,3},{1,2},{2,1},{3,0},{4,7},{5,6},{6,5},{7,4},{8,11},{9,10},{10,... | collective-permute-start | bytes 73736 | tf_op jit(solution)/shard_map/ppermute | solution.py:32
  27.6 6.6 %collective-permute-start.11 = (bf16[16,1536]{1,0:T(8,128)(2,1)S(1)}, bf16[16,1536]{1,0:T(8,128)(2,1)S(1)}, u32[]{:S(2)}, u32[]{:S(2)}) collective-permute-start(bf16[16,1536]{1,0:T(8,128)(2,1)S(1)} %get-tuple-element.30), channel_id=1, source_target_pairs={{0,4},{4,8},{8,12},{12,0},{1,5},{5,9},{9,13},{13,1},{2,6},{6,10},{... | collective-permute-start | bytes 147464 | tf_op jit(solution)/shard_map/ppermute | solution.py:20
  28.7 6.7 %collective-permute-start.12 = (bf16[16,1536]{1,0:T(8,128)(2,1)S(1)}, bf16[16,1536]{1,0:T(8,128)(2,1)S(1)}, u32[]{:S(2)}, u32[]{:S(2)}) collective-permute-start(bf16[16,1536]{1,0:T(8,128)(2,1)S(1)} %get-tuple-element.31), channel_id=1, source_target_pairs={{0,8},{4,12},{8,0},{12,4},{1,9},{5,13},{9,1},{13,5},{2,10},{6,14},... | collective-permute-start | bytes 147464 | tf_op jit(solution)/shard_map/ppermute | solution.py:20
  31.2 4.4 %collective-permute-start.13 = (bf16[16,1536]{1,0:T(8,128)(2,1)S(1)}, bf16[16,1536]{1,0:T(8,128)(2,1)S(1)}, u32[]{:S(2)}, u32[]{:S(2)}) collective-permute-start(bf16[16,1536]{1,0:T(8,128)(2,1)S(1)} %get-tuple-element.32), channel_id=1, source_target_pairs={{0,12},{4,0},{8,4},{12,8},{1,13},{5,1},{9,5},{13,9},{2,14},{6,2},{... | collective-permute-start | bytes 147464 | tf_op jit(solution)/shard_map/ppermute | solution.py:20
  37.7 1.4 %collective-permute-start.15 = (bf16[16,4608]{1,0:T(8,128)(2,1)S(1)}, bf16[16,4608]{1,0:T(8,128)(2,1)S(1)}, u32[]{:S(2)}, u32[]{:S(2)}) collective-permute-start(bf16[16,4608]{1,0:T(8,128)(2,1)S(1)} %get-tuple-element.36), channel_id=1, source_target_pairs={{0,1},{1,0},{2,3},{3,2},{4,5},{5,4},{6,7},{7,6},{8,9},{9,8},{10,11... | collective-permute-start | bytes 442376 | tf_op jit(solution)/shard_map/ppermute | solution.py:20
  37.8 2.6 %collective-permute-start.14 = (bf16[16,4608]{1,0:T(8,128)(2,1)S(1)}, bf16[16,4608]{1,0:T(8,128)(2,1)S(1)}, u32[]{:S(2)}, u32[]{:S(2)}) collective-permute-start(bf16[16,4608]{1,0:T(8,128)(2,1)S(1)} %get-tuple-element.34), channel_id=1, source_target_pairs={{0,1},{1,0},{2,3},{3,2},{4,5},{5,4},{6,7},{7,6},{8,9},{9,8},{10,11... | collective-permute-start | bytes 442376 | tf_op jit(solution)/shard_map/ppermute | solution.py:20
  39.2 6.0 %collective-permute-start.16 = (bf16[16,4608]{1,0:T(8,128)(2,1)S(1)}, bf16[16,4608]{1,0:T(8,128)(2,1)S(1)}, u32[]{:S(2)}, u32[]{:S(2)}) collective-permute-start(bf16[16,4608]{1,0:T(8,128)(2,1)S(1)} %pair_sum.1), channel_id=1, source_target_pairs={{0,2},{2,0},{1,3},{3,1},{4,6},{6,4},{5,7},{7,5},{8,10},{10,8},{9,1... | collective-permute-start | bytes 442376 | tf_op jit(solution)/shard_map/ppermute | solution.py:20

commit v7 on v6

--- a/solution.py
+++ b/solution.py
@@ -173,7 +173,7 @@
         out[...] = value
 
 
-def output_body(n_gx, n_gy, n_gz, chunk, *refs):
+def output_body(n_gx, n_gy, n_gz, chunk, first, *refs):
     where = position()
     pieces, weight = refs[:n_gx], refs[n_gx]
     count = n_gy * n_gz
@@ -186,14 +186,14 @@
     part = outs[0].shape[0]
     count = block * n_gx
     clear_below(rows, count)
-    for c in range(weight.shape[1] // chunk):
-        span = slice(c * chunk, (c + 1) * chunk)
+    for c in range(outs[0].shape[1] // chunk):
+        span = slice(first + c * chunk, first + (c + 1) * chunk)
         total[...] = product(rows, weight, span, 768)[:count]
         for k in range(n_gy):
             for j in range(n_gz):
                 at = lax.rem(where[1] + k, n_gy) * n_gz + lax.rem(where[2] + j, n_gz)
                 at = pl.multiple_of(at * part, part)
-                outs[k * n_gz + j][:, span] = total[pl.ds(at, part), :].astype(BF16)
+                outs[k * n_gz + j][:, c * chunk : (c + 1) * chunk] = total[pl.ds(at, part), :].astype(BF16)
 
 
 def sum_body(*refs):
@@ -201,6 +201,17 @@
     for ref in refs[1:-1]:
         value = value + ref[...].astype(F32)
     refs[-1][...] = value.astype(BF16)
+
+
+def sum_parts_body(*refs):
+    pieces, out = refs[:-1], refs[-1]
+    wide = pieces[0].shape[1]
+    each = len(pieces) // (out.shape[1] // wide)
+    for c in range(out.shape[1] // wide):
+        value = pieces[c * each][...].astype(F32)
+        for piece in pieces[c * each + 1 : (c + 1) * each]:
+            value = value + piece[...].astype(F32)
+        out[:, c * wide : (c + 1) * wide] = value.astype(BF16)
 
 
 def added(arrays, name):
@@ -240,6 +251,9 @@
     chip_keys, chip_values, chip_lengths = (
         [array] + [shift(array, "gz", j) for j in range(1, n_gz)] for array in (key_cache, value_cache, lengths)
     )
+    pieces, chip_keys, chip_values, chip_lengths = lax.optimization_barrier(
+        (pieces, chip_keys, chip_values, chip_lengths)
+    )
     chunk = largest_divisor(width, 256, 128)
     terms = call(
         functools.partial(query_body, n_gx, n_gy, n_gz, chunk),
@@ -287,28 +301,46 @@
     )
     blocks = [copies[0]] + [shift(copies[k], "gx", k) for k in range(1, n_gx)]
     columns = o_weight.shape[1]
-    chunk = largest_divisor(columns, 768, 128)
-    terms = call(
-        functools.partial(output_body, n_gx, n_gy, n_gz, chunk),
-        [struct((own_rows, columns), BF16)] * (n_gy * n_gz),
-        [*blocks, o_weight],
-        [VMEM] * n_gx + [VMEM],
-        scratch=[
-            pltpu.VMEM((tall, width), BF16),
-            pltpu.VMEM((row_count, chunk), F32),
-        ],
-        mib=mib_for(tall * width * 4, tall * (chunk * 4 + columns * 2), columns * width * 2),
-        flops=2 * row_count * columns * width,
-        name="output_terms",
-    )
-
-    arrived = []
-    for k in range(1, n_gy):
-        mine = [terms[k * n_gz + j] for j in range(n_gz)]
-        mine = [mine[0]] + [shift(mine[j], "gz", j) for j in range(1, n_gz)]
-        arrived.append(shift(added(mine, "pair_sum") if n_gz > 1 else mine[0], "gy", k))
-    mine = [terms[0]] + [shift(terms[j], "gz", j) for j in range(1, n_gz)]
-    return added(mine + arrived, "output_sum")
+    splits = 2 if columns % 512 == 0 else 1
+    wide = columns // splits
+    chunk = largest_divisor(wide, 768, 128)
+    terms = [
+        call(
+            functools.partial(output_body, n_gx, n_gy, n_gz, chunk, c * wide),
+            [struct((own_rows, wide), BF16)] * (n_gy * n_gz),
+            [*blocks, o_weight],
+            [VMEM] * (n_gx + 1),
+            scratch=[pltpu.VMEM((tall, width), BF16), pltpu.VMEM((row_count, chunk), F32)],
+            mib=mib_for(tall * width * 4, tall * (chunk * 4 + wide * 2), columns * width * 2),
+            flops=2 * tall * wide * width,
+            name="output_terms",
+        )
+        for c in range(splits)
+    ]
+
+    leaving, arrived = [], []
+    for term in terms:
+        for k in range(1, n_gy):
+            mine = term[k * n_gz : (k + 1) * n_gz]
+            mine = [mine[0]] + [shift(mine[j], "gz", j) for j in range(1, n_gz)]
+            leaving.append(added(mine, "pair_sum") if n_gz > 1 else mine[0])
+    for at, array in enumerate(leaving):
+        arrived.append(shift(array, "gy", at % (n_gy - 1) + 1))
+    staying = [term[j] for term in terms for j in range(1, n_gz)]
+    if leaving and staying:
+        leaving, staying = lax.optimization_barrier((leaving, staying))
+    operands = []
+    for c, term in enumerate(terms):
+        operands.append(term[0])
+        operands += [shift(staying[c * (n_gz - 1) + j - 1], "gz", j) for j in range(1, n_gz)]
+        operands += arrived[c * (n_gy - 1) : (c + 1) * (n_gy - 1)]
+    return call(
+        sum_parts_body,
+        [struct((own_rows, columns), BF16)],
+        operands,
+        [VMEM] * len(operands),
+        name="output_sum",
+    )[0]
 
 
 def solution(mesh):

time: 46 us -> 45.6 us (level)
  waiting for transfers between devices: 21.3 us -> 20 us
  starting transfers between devices: 16.8 us -> 17.7 us
    ppermute x15 -> x18, waiting for transfers between devices: 17.1 us -> 13.6 us  [shift(): lax.ppermute(array, axis, [(s, (s + by) % size) for s in range(size)])]
    ppermute x2, waiting for transfers between devices: 4.18 us -> 6.38 us  [hop(): return lax.ppermute(array, (axis, 'gz'), pairs)]
    ppermute x15 -> x18, starting transfers between devices: 16.2 us -> 17.2 us  [shift(): lax.ppermute(array, axis, [(s, (s + by) % size) for s in range(size)])]
    pallas_call x8 -> x10, Pallas kernels: 6.53 us -> 6.7 us  [call(): pl.pallas_call(body, out_shape=list(outs), in_specs=in_specs, out_specs=[...]
  transfers between devices with their start and end apart: 17 -> 20, of which waited for: 12 -> 12; matrix products, arithmetic and copies ran while one was open for 0% -> 0% of each run, Pallas kernels for 1% -> 3%
where the time goes in v7:
time: 45.6 us; the launch traced here: 45.5 us
  waiting for transfers between devices  20 us (44%)
  starting transfers between devices  17.7 us (39%)
  Pallas kernels  6.7 us (15%)
  local copies, waits for them, and re-layouts  0.95 us (2%)
    ppermute x18, starting transfers between devices, shift(): lax.ppermute(array, axis, [(s, (s + by) % size) for s in range(size)])  17.2 us
    ppermute x18, waiting for transfers between devices, shift(): lax.ppermute(array, axis, [(s, (s + by) % size) for s in range(size)])  13.6 us
    pallas_call x10, Pallas kernels, call(): pl.pallas_call(body, out_shape=list(outs), in_specs=in_specs, out_specs=[...  6.7 us
    ppermute x2, waiting for transfers between devices, hop(): return lax.ppermute(array, (axis, 'gz'), pairs)  6.38 us
    unnamed x18, local copies, waits for them, and re-layouts  0.95 us
  transfers between devices with their start and end apart: 20, of which 12 were waited for; matrix products, arithmetic and copies ran while one was open for 0% of the time, Pallas kernels for 3%

profile of v7, /device:TPU:0, one launch (start us, length us, event | category | flops | bytes accessed | tf_op | source)
XLA Modules:
  0.0 45.5 jit_solution(17158025213432841796)
XLA Ops:
  0.0 2.9 %collective-permute-start.1 = (bf16[16,4608]{1,0:T(8,128)(2,1)}, bf16[16,4608]{1,0:T(8,128)(2,1)S(1)}, u32[]{:S(2)}, u32[]{:S(2)}) collective-permute-start(bf16[16,4608]{1,0:T(8,128)(2,1)} %tokens.1), channel_id=1, source_target_pairs={{0,2},{2,0},{1,3},{3,1},{4,6},{6,4},{5,7},{7,5},{8,10},{10,8},{9,1... | collective-permute-start | bytes 442376 | tf_op jit(solution)/shard_map/ppermute | solution.py:20
  2.9 0.5 %collective-permute-start.5 = (s32[4]{0:T(128)}, s32[4]{0:T(128)S(1)}, u32[]{:S(2)}, u32[]{:S(2)}) collective-permute-start(s32[4]{0:T(128)} %refs_0_), channel_id=1, source_target_pairs={{0,1},{1,0},{2,3},{3,2},{4,5},{5,4},{6,7},{7,6},{8,9},{9,8},{10,11... | collective-permute-start | bytes 56 | tf_op jit(solution)/shard_map/ppermute | solution.py:20
  3.5 0.5 %collective-permute-start.4 = (bf16[4,512,256]{2,1,0:T(8,128)(2,1)}, bf16[4,512,256]{2,1,0:T(8,128)(2,1)S(1)}, u32[]{:S(2)}, u32[]{:S(2)}) collective-permute-start(bf16[4,512,256]{2,1,0:T(8,128)(2,1)} %refs_6_), channel_id=1, source_target_pairs={{0,1},{1,0},{2,3},{3,2},{4,5},{5,4},{6,7},{7,6},{8,9},{9,8},{10,11... | collective-permute-start | bytes 3145736 | tf_op jit(solution)/shard_map/ppermute | solution.py:20
  4.0 3.0 %collective-permute-done.1.refs_2_ = bf16[16,4608]{1,0:T(8,128)(2,1)S(1)} collective-permute-done((bf16[16,4608]{1,0:T(8,128)(2,1)}, bf16[16,4608]{1,0:T(8,128)(2,1)S(1)}, u32[]{:S(2)}, u32[]{:S(2)}) %collective-permute-start.1) | collective-permute-done | bytes 147488 | tf_op jit(solution)/shard_map/ppermute | solution.py:20
  7.0 0.9 %copy-done.4 = bf16[16,4608]{1,0:T(8,128)(2,1)S(1)} copy-done((bf16[16,4608]{1,0:T(8,128)(2,1)S(1)}, bf16[16,4608]{1,0:T(8,128)(2,1)}, u32[]{:S(2)}) %copy-start.4) | copy-done | bytes 147480
  8.1 0.3 collective-permute-done.2.refs_3_
  8.4 2.0 %query_terms.1 = (bf16[16,1536]{1,0:T(8,128)(2,1)S(1)}, bf16[16,1536]{1,0:T(8,128)(2,1)S(1)}, bf16[16,1536]{1,0:T(8,128)(2,1)S(1)}, bf16[16,1536]{1,0:T(8,128)(2,1)S(1)}) custom-call(bf16[16,4608]{1,0:T(8,128)(2,1)S(1)} %own_tokens.1.refs_0_, bf16[16,4608]{1,0:T(8,128)(2,1)S(1)} %collective-permute-done.refs_1_, ...), custom_call_target="tpu_custom_call" | custom-call | flops 905969664 | bytes 14942208 | tf_op jit(solution)/shard_map/query_terms/pallas_call | solution.py:54
  10.4 1.9 %collective-permute-start.6 = (bf16[16,1536]{1,0:T(8,128)(2,1)S(1)}, bf16[16,1536]{1,0:T(8,128)(2,1)S(1)}, u32[]{:S(2)}, u32[]{:S(2)}) collective-permute-start(bf16[16,1536]{1,0:T(8,128)(2,1)S(1)} %get-tuple-element.44), channel_id=1, source_target_pairs={{0,4},{4,8},{8,12},{12,0},{1,5},{5,9},{9,13},{13,1},{2,6},{6,10},{... | collective-permute-start | bytes 147464 | tf_op jit(solution)/shard_map/ppermute | solution.py:20
  12.3 2.6 %collective-permute-start.7 = (bf16[16,1536]{1,0:T(8,128)(2,1)S(1)}, bf16[16,1536]{1,0:T(8,128)(2,1)S(1)}, u32[]{:S(2)}, u32[]{:S(2)}) collective-permute-start(bf16[16,1536]{1,0:T(8,128)(2,1)S(1)} %get-tuple-element.45), channel_id=1, source_target_pairs={{0,8},{4,12},{8,0},{12,4},{1,9},{5,13},{9,1},{13,5},{2,10},{6,14},... | collective-permute-start | bytes 147464 | tf_op jit(solution)/shard_map/ppermute | solution.py:20
  14.9 1.3 %collective-permute-start.8 = (bf16[16,1536]{1,0:T(8,128)(2,1)S(1)}, bf16[16,1536]{1,0:T(8,128)(2,1)S(1)}, u32[]{:S(2)}, u32[]{:S(2)}) collective-permute-start(bf16[16,1536]{1,0:T(8,128)(2,1)S(1)} %get-tuple-element.46), channel_id=1, source_target_pairs={{0,12},{4,0},{8,4},{12,8},{1,13},{5,1},{9,5},{13,9},{2,14},{6,2},{... | collective-permute-start | bytes 147464 | tf_op jit(solution)/shard_map/ppermute | solution.py:20
  16.3 0.3 collective-permute-done.6.refs_1_
  16.6 2.3 %collective-permute-done.7.refs_2_ = bf16[16,1536]{1,0:T(8,128)(2,1)S(1)} collective-permute-done((bf16[16,1536]{1,0:T(8,128)(2,1)S(1)}, bf16[16,1536]{1,0:T(8,128)(2,1)S(1)}, u32[]{:S(2)}, u32[]{:S(2)}) %collective-permute-start.7) | collective-permute-done | bytes 49184 | tf_op jit(solution)/shard_map/ppermute | solution.py:20
  18.9 0.3 collective-permute-done.8.refs_3_
  19.3 0.3 collective-permute-start.9
  19.6 3.2 %collective-permute-done.9.refs_3_ = bf16[2,4,1536]{2,1,0:T(4,128)(2,1)S(1)} collective-permute-done((bf16[2,4,1536]{2,1,0:T(4,128)(2,1)S(1)}, bf16[2,4,1536]{2,1,0:T(4,128)(2,1)S(1)}, u32[]{:S(2)}, u32[]{:S(2)}) %collective-permute-start.9) | collective-permute-done | bytes 24608 | tf_op jit(solution)/shard_map/ppermute | solution.py:32
  22.8 1.5 %attention.1 = (bf16[2,4,1536]{2,1,0:T(4,128)(2,1)S(1)}, bf16[2,4,1536]{2,1,0:T(4,128)(2,1)S(1)}) custom-call(s32[4]{0:T(128)S(1)} %copy-done.3, s32[4]{0:T(128)S(1)} %collective-permute-done.5.refs_1_, bf16[2,4,1536]{2,1,0:T(4,128)(2,1)S(1)} %get-tuple-element.47.refs_2_, bf16[2,4,1536]{2,1,0:T(4,128)(2,1)S(1)} %collective-permute-done.9.refs_3_, ...), custom_call_target="tpu_custom_call" | custom-call | bytes 4292640 | tf_op jit(solution)/shard_map/attention/pallas_call | solution.py:54
  24.5 3.2 %collective-permute-done.10.refs_1_ = bf16[2,4,1536]{2,1,0:T(4,128)(2,1)S(1)} collective-permute-done((bf16[2,4,1536]{2,1,0:T(4,128)(2,1)S(1)}, bf16[2,4,1536]{2,1,0:T(4,128)(2,1)S(1)}, u32[]{:S(2)}, u32[]{:S(2)}) %collective-permute-start.10) | collective-permute-done | bytes 24608 | tf_op jit(solution)/shard_map/ppermute | solution.py:32
  27.7 1.1 %collective-permute-start.11 = (bf16[16,1536]{1,0:T(8,128)(2,1)S(1)}, bf16[16,1536]{1,0:T(8,128)(2,1)S(1)}, u32[]{:S(2)}, u32[]{:S(2)}) collective-permute-start(bf16[16,1536]{1,0:T(8,128)(2,1)S(1)} %get-tuple-element.56), channel_id=1, source_target_pairs={{0,4},{4,8},{8,12},{12,0},{1,5},{5,9},{9,13},{13,1},{2,6},{6,10},{... | collective-permute-start | bytes 147464 | tf_op jit(solution)/shard_map/ppermute | solution.py:20
  28.8 2.5 %collective-permute-start.12 = (bf16[16,1536]{1,0:T(8,128)(2,1)S(1)}, bf16[16,1536]{1,0:T(8,128)(2,1)S(1)}, u32[]{:S(2)}, u32[]{:S(2)}) collective-permute-start(bf16[16,1536]{1,0:T(8,128)(2,1)S(1)} %get-tuple-element.57), channel_id=1, source_target_pairs={{0,8},{4,12},{8,0},{12,4},{1,9},{5,13},{9,1},{13,5},{2,10},{6,14},... | collective-permute-start | bytes 147464 | tf_op jit(solution)/shard_map/ppermute | solution.py:20
  31.2 0.6 %collective-permute-start.13 = (bf16[16,1536]{1,0:T(8,128)(2,1)S(1)}, bf16[16,1536]{1,0:T(8,128)(2,1)S(1)}, u32[]{:S(2)}, u32[]{:S(2)}) collective-permute-start(bf16[16,1536]{1,0:T(8,128)(2,1)S(1)} %get-tuple-element.58), channel_id=1, source_target_pairs={{0,12},{4,0},{8,4},{12,8},{1,13},{5,1},{9,5},{13,9},{2,14},{6,2},{... | collective-permute-start | bytes 147464 | tf_op jit(solution)/shard_map/ppermute | solution.py:20
  31.8 2.4 %collective-permute-done.11.refs_1_ = bf16[16,1536]{1,0:T(8,128)(2,1)S(1)} collective-permute-done((bf16[16,1536]{1,0:T(8,128)(2,1)S(1)}, bf16[16,1536]{1,0:T(8,128)(2,1)S(1)}, u32[]{:S(2)}, u32[]{:S(2)}) %collective-permute-start.11) | collective-permute-done | bytes 49184 | tf_op jit(solution)/shard_map/ppermute | solution.py:20
  34.3 1.2 %collective-permute-done.12.refs_2_ = bf16[16,1536]{1,0:T(8,128)(2,1)S(1)} collective-permute-done((bf16[16,1536]{1,0:T(8,128)(2,1)S(1)}, bf16[16,1536]{1,0:T(8,128)(2,1)S(1)}, u32[]{:S(2)}, u32[]{:S(2)}) %collective-permute-start.12) | collective-permute-done | bytes 49184 | tf_op jit(solution)/shard_map/ppermute | solution.py:20
  35.5 0.2 collective-permute-done.13.refs_3_
  35.7 1.1 %output_terms.3 = (bf16[16,2304]{1,0:T(8,128)(2,1)S(1)}, bf16[16,2304]{1,0:T(8,128)(2,1)S(1)}, bf16[16,2304]{1,0:T(8,128)(2,1)S(1)}, bf16[16,2304]{1,0:T(8,128)(2,1)S(1)}) custom-call(bf16[16,1536]{1,0:T(8,128)(2,1)S(1)} %get-tuple-element.55.refs_0_, bf16[16,1536]{1,0:T(8,128)(2,1)S(1)} %collective-permute-done.11.refs_1_, ...), custom_call_target="tpu_custom_call" | custom-call | flops 905969664 | bytes 14647296 | tf_op jit(solution)/shard_map/output_terms/pallas_call | solution.py:54
  36.9 1.1 %output_terms.2 = (bf16[16,2304]{1,0:T(8,128)(2,1)S(1)}, bf16[16,2304]{1,0:T(8,128)(2,1)S(1)}, bf16[16,2304]{1,0:T(8,128)(2,1)S(1)}, bf16[16,2304]{1,0:T(8,128)(2,1)S(1)}) custom-call(bf16[16,1536]{1,0:T(8,128)(2,1)S(1)} %get-tuple-element.55.refs_0_, bf16[16,1536]{1,0:T(8,128)(2,1)S(1)} %collective-permute-done.11.refs_1_, ...), custom_call_target="tpu_custom_call" | custom-call | flops 905969664 | bytes 14647296 | tf_op jit(solution)/shard_map/output_terms/pallas_call | solution.py:54
  38.0 0.6 %collective-permute-start.14 = (bf16[16,2304]{1,0:T(8,128)(2,1)S(1)}, bf16[16,2304]{1,0:T(8,128)(2,1)S(1)}, u32[]{:S(2)}, u32[]{:S(2)}) collective-permute-start(bf16[16,2304]{1,0:T(8,128)(2,1)S(1)} %get-tuple-element.61), channel_id=1, source_target_pairs={{0,1},{1,0},{2,3},{3,2},{4,5},{5,4},{6,7},{7,6},{8,9},{9,8},{10,11... | collective-permute-start | bytes 221192 | tf_op jit(solution)/shard_map/ppermute | solution.py:20
  38.6 1.2 %collective-permute-start.19 = (bf16[16,2304]{1,0:T(8,128)(2,1)S(1)}, bf16[16,2304]{1,0:T(8,128)(2,1)S(1)}, u32[]{:S(2)}, u32[]{:S(2)}) collective-permute-start(bf16[16,2304]{1,0:T(8,128)(2,1)S(1)} %pair_sum.3), channel_id=1, source_target_pairs={{0,2},{2,0},{1,3},{3,1},{4,6},{6,4},{5,7},{7,5},{8,10},{10,8},{9,1... | collective-permute-start | bytes 221192 | tf_op jit(solution)/shard_map/ppermute | solution.py:20
  39.9 0.5 %collective-permute-start.18 = (bf16[16,2304]{1,0:T(8,128)(2,1)S(1)}, bf16[16,2304]{1,0:T(8,128)(2,1)S(1)}, u32[]{:S(2)}, u32[]{:S(2)}) collective-permute-start(bf16[16,2304]{1,0:T(8,128)(2,1)S(1)} %get-tuple-element.68), channel_id=1, source_target_pairs={{0,1},{1,0},{2,3},{3,2},{4,5},{5,4},{6,7},{7,6},{8,9},{9,8},{10,11... | collective-permute-start | bytes 221192 | tf_op jit(solution)/shard_map/ppermute | solution.py:20
  40.4 0.9 %collective-permute-start.17 = (bf16[16,2304]{1,0:T(8,128)(2,1)S(1)}, bf16[16,2304]{1,0:T(8,128)(2,1)S(1)}, u32[]{:S(2)}, u32[]{:S(2)}) collective-permute-start(bf16[16,2304]{1,0:T(8,128)(2,1)S(1)} %pair_sum.2), channel_id=1, source_target_pairs={{0,2},{2,0},{1,3},{3,1},{4,6},{6,4},{5,7},{7,5},{8,10},{10,8},{9,1... | collective-permute-start | bytes 221192 | tf_op jit(solution)/shard_map/ppermute | solution.py:20
  41.3 1.7 %collective-permute-done.19.refs_5_ = bf16[16,2304]{1,0:T(8,128)(2,1)S(1)} collective-permute-done((bf16[16,2304]{1,0:T(8,128)(2,1)S(1)}, bf16[16,2304]{1,0:T(8,128)(2,1)S(1)}, u32[]{:S(2)}, u32[]{:S(2)}) %collective-permute-start.19) | collective-permute-done | bytes 73760 | tf_op jit(solution)/shard_map/ppermute | solution.py:20
  43.0 1.7 %collective-permute-done.17.refs_2_ = bf16[16,2304]{1,0:T(8,128)(2,1)S(1)} collective-permute-done((bf16[16,2304]{1,0:T(8,128)(2,1)S(1)}, bf16[16,2304]{1,0:T(8,128)(2,1)S(1)}, u32[]{:S(2)}, u32[]{:S(2)}) %collective-permute-start.17) | collective-permute-done | bytes 73760 | tf_op jit(solution)/shard_map/ppermute | solution.py:20
  44.8 0.7 %output_sum.1 = bf16[16,4608]{1,0:T(8,128)(2,1)} custom-call(bf16[16,2304]{1,0:T(8,128)(2,1)S(1)} %get-tuple-element.59.refs_0_, bf16[16,2304]{1,0:T(8,128)(2,1)S(1)} %collective-permute-done.16.refs_1_, bf16[16,2304]{1,0:T(8,128)(2,1)S(1)} %collective-permute-done.17.refs_2_, bf16[16,2304]{1,0:T(8,128)(2,1)S(1)} %get-tuple-element.67.refs_3_, ...), custom_call_target="tpu_custom_call" | custom-call | bytes 589824 | tf_op jit(solution)/shard_map/output_sum/pallas_call | solution.py:54
  (37 shorter events, 0.6 us)
Async XLA Ops:
  0.0 8.4 %copy-start = (bf16[4608,1536]{1,0:T(8,128)(2,1)S(1)}, bf16[4608,1536]{1,0:T(8,128)(2,1)}, u32[]{:S(2)}) copy-start(bf16[4608,1536]{1,0:T(8,128)(2,1)} %refs_4_.3) | copy-start | bytes 42467332
  0.0 7.0 %collective-permute-start.1 = (bf16[16,4608]{1,0:T(8,128)(2,1)}, bf16[16,4608]{1,0:T(8,128)(2,1)S(1)}, u32[]{:S(2)}, u32[]{:S(2)}) collective-permute-start(bf16[16,4608]{1,0:T(8,128)(2,1)} %tokens.1), channel_id=1, source_target_pairs={{0,2},{2,0},{1,3},{3,1},{4,6},{6,4},{5,7},{7,5},{8,10},{10,8},{9,1... | collective-permute-start | bytes 442376 | tf_op jit(solution)/shard_map/ppermute | solution.py:20
  2.9 5.2 %collective-permute-start = (bf16[16,4608]{1,0:T(8,128)(2,1)}, bf16[16,4608]{1,0:T(8,128)(2,1)S(1)}, u32[]{:S(2)}, u32[]{:S(2)}) collective-permute-start(bf16[16,4608]{1,0:T(8,128)(2,1)} %tokens.1), channel_id=1, source_target_pairs={{0,1},{1,0},{2,3},{3,2},{4,5},{5,4},{6,7},{7,6},{8,9},{9,8},{10,11... | collective-permute-start | bytes 442376 | tf_op jit(solution)/shard_map/ppermute | solution.py:20
  2.9 5.1 %collective-permute-start.5 = (s32[4]{0:T(128)}, s32[4]{0:T(128)S(1)}, u32[]{:S(2)}, u32[]{:S(2)}) collective-permute-start(s32[4]{0:T(128)} %refs_0_), channel_id=1, source_target_pairs={{0,1},{1,0},{2,3},{3,2},{4,5},{5,4},{6,7},{7,6},{8,9},{9,8},{10,11... | collective-permute-start | bytes 56 | tf_op jit(solution)/shard_map/ppermute | solution.py:20
  3.5 4.9 %collective-permute-start.3 = (bf16[4,512,256]{2,1,0:T(8,128)(2,1)}, bf16[4,512,256]{2,1,0:T(8,128)(2,1)S(1)}, u32[]{:S(2)}, u32[]{:S(2)}) collective-permute-start(bf16[4,512,256]{2,1,0:T(8,128)(2,1)} %refs_4_.4), channel_id=1, source_target_pairs={{0,1},{1,0},{2,3},{3,2},{4,5},{5,4},{6,7},{7,6},{8,9},{9,8},{10,11... | collective-permute-start | bytes 3145736 | tf_op jit(solution)/shard_map/ppermute | solution.py:20
  3.5 4.9 %collective-permute-start.4 = (bf16[4,512,256]{2,1,0:T(8,128)(2,1)}, bf16[4,512,256]{2,1,0:T(8,128)(2,1)S(1)}, u32[]{:S(2)}, u32[]{:S(2)}) collective-permute-start(bf16[4,512,256]{2,1,0:T(8,128)(2,1)} %refs_6_), channel_id=1, source_target_pairs={{0,1},{1,0},{2,3},{3,2},{4,5},{5,4},{6,7},{7,6},{8,9},{9,8},{10,11... | collective-permute-start | bytes 3145736 | tf_op jit(solution)/shard_map/ppermute | solution.py:20
  7.0 1.4 %collective-permute-start.2 = (bf16[16,4608]{1,0:T(8,128)(2,1)S(1)}, bf16[16,4608]{1,0:T(8,128)(2,1)S(1)}, u32[]{:S(2)}, u32[]{:S(2)}) collective-permute-start(bf16[16,4608]{1,0:T(8,128)(2,1)S(1)} %collective-permute-done.1.refs_2_), channel_id=1, source_target_pairs={{0,1},{1,0},{2,3},{3,2},{4,5},{5,4},{6,7},{7,6},{8,9},{9,8},{10,11... | collective-permute-start | bytes 442376 | tf_op jit(solution)/shard_map/ppermute | solution.py:20
  7.0 0.9 %copy-start.4 = (bf16[16,4608]{1,0:T(8,128)(2,1)S(1)}, bf16[16,4608]{1,0:T(8,128)(2,1)}, u32[]{:S(2)}) copy-start(bf16[16,4608]{1,0:T(8,128)(2,1)} %tokens.1) | copy-start | bytes 442372
  8.4 27.3 %slice-start = ((s8[14155776]{0:T(1024)(128)(4,1)}), s8[1572864]{0:T(1024)(128)(4,1)S(1)}, s32[]{:S(2)}) async-start(s8[14155776]{0:T(1024)(128)(4,1)} %bitcast), calls=%async_computation | async-start | bytes 3145728
  8.4 27.3 %slice-start.1 = ((s8[14155776]{0:T(1024)(128)(4,1)}), s8[4194304]{0:T(1024)(128)(4,1)S(1)}, s32[]{:S(2)}) async-start(s8[14155776]{0:T(1024)(128)(4,1)} %bitcast), calls=%async_computation.1 | async-start | bytes 8388608
  10.4 6.2 %collective-permute-start.6 = (bf16[16,1536]{1,0:T(8,128)(2,1)S(1)}, bf16[16,1536]{1,0:T(8,128)(2,1)S(1)}, u32[]{:S(2)}, u32[]{:S(2)}) collective-permute-start(bf16[16,1536]{1,0:T(8,128)(2,1)S(1)} %get-tuple-element.44), channel_id=1, source_target_pairs={{0,4},{4,8},{8,12},{12,0},{1,5},{5,9},{9,13},{13,1},{2,6},{6,10},{... | collective-permute-start | bytes 147464 | tf_op jit(solution)/shard_map/ppermute | solution.py:20
  12.3 6.6 %collective-permute-start.7 = (bf16[16,1536]{1,0:T(8,128)(2,1)S(1)}, bf16[16,1536]{1,0:T(8,128)(2,1)S(1)}, u32[]{:S(2)}, u32[]{:S(2)}) collective-permute-start(bf16[16,1536]{1,0:T(8,128)(2,1)S(1)} %get-tuple-element.45), channel_id=1, source_target_pairs={{0,8},{4,12},{8,0},{12,4},{1,9},{5,13},{9,1},{13,5},{2,10},{6,14},... | collective-permute-start | bytes 147464 | tf_op jit(solution)/shard_map/ppermute | solution.py:20
  14.9 4.3 %collective-permute-start.8 = (bf16[16,1536]{1,0:T(8,128)(2,1)S(1)}, bf16[16,1536]{1,0:T(8,128)(2,1)S(1)}, u32[]{:S(2)}, u32[]{:S(2)}) collective-permute-start(bf16[16,1536]{1,0:T(8,128)(2,1)S(1)} %get-tuple-element.46), channel_id=1, source_target_pairs={{0,12},{4,0},{8,4},{12,8},{1,13},{5,1},{9,5},{13,9},{2,14},{6,2},{... | collective-permute-start | bytes 147464 | tf_op jit(solution)/shard_map/ppermute | solution.py:20
  19.2 3.6 %copy-start.1 = (bf16[4,512,256]{2,1,0:T(8,128)(2,1)S(1)}, bf16[4,512,256]{2,1,0:T(8,128)(2,1)}, u32[]{:S(2)}) copy-start(bf16[4,512,256]{2,1,0:T(8,128)(2,1)} %refs_4_.4) | copy-start | bytes 3145732
  19.2 3.6 %copy-start.2 = (bf16[4,512,256]{2,1,0:T(8,128)(2,1)S(1)}, bf16[4,512,256]{2,1,0:T(8,128)(2,1)}, u32[]{:S(2)}) copy-start(bf16[4,512,256]{2,1,0:T(8,128)(2,1)} %refs_6_) | copy-start | bytes 3145732
  19.2 3.6 %copy-start.3 = (s32[4]{0:T(128)S(1)}, s32[4]{0:T(128)}, u32[]{:S(2)}) copy-start(s32[4]{0:T(128)} %refs_0_) | copy-start | bytes 52
  19.2 16.5 %slice-start.2 = ((s8[14155776]{0:T(1024)(128)(4,1)}), s8[4194304]{0:T(1024)(128)(4,1)S(1)}, s32[]{:S(2)}) async-start(s8[14155776]{0:T(1024)(128)(4,1)} %bitcast), calls=%async_computation.2 | async-start | bytes 8388608
  19.2 16.5 %slice-start.3 = ((s8[14155776]{0:T(1024)(128)(4,1)}), s8[4194304]{0:T(1024)(128)(4,1)S(1)}, s32[]{:S(2)}) async-start(s8[14155776]{0:T(1024)(128)(4,1)} %bitcast), calls=%async_computation.3 | async-start | bytes 8388608
  19.3 3.5 %collective-permute-start.9 = (bf16[2,4,1536]{2,1,0:T(4,128)(2,1)S(1)}, bf16[2,4,1536]{2,1,0:T(4,128)(2,1)S(1)}, u32[]{:S(2)}, u32[]{:S(2)}) collective-permute-start(bf16[2,4,1536]{2,1,0:T(4,128)(2,1)S(1)} %get-tuple-element.48), channel_id=1, source_target_pairs={{0,3},{1,2},{2,1},{3,0},{4,7},{5,6},{6,5},{7,4},{8,11},{9,10},{10,... | collective-permute-start | bytes 73736 | tf_op jit(solution)/shard_map/ppermute | solution.py:32
  24.3 3.3 %collective-permute-start.10 = (bf16[2,4,1536]{2,1,0:T(4,128)(2,1)S(1)}, bf16[2,4,1536]{2,1,0:T(4,128)(2,1)S(1)}, u32[]{:S(2)}, u32[]{:S(2)}) collective-permute-start(bf16[2,4,1536]{2,1,0:T(4,128)(2,1)S(1)} %get-tuple-element.54), channel_id=1, source_target_pairs={{0,3},{1,2},{2,1},{3,0},{4,7},{5,6},{6,5},{7,4},{8,11},{9,10},{10,... | collective-permute-start | bytes 73736 | tf_op jit(solution)/shard_map/ppermute | solution.py:32
  27.7 6.6 %collective-permute-start.11 = (bf16[16,1536]{1,0:T(8,128)(2,1)S(1)}, bf16[16,1536]{1,0:T(8,128)(2,1)S(1)}, u32[]{:S(2)}, u32[]{:S(2)}) collective-permute-start(bf16[16,1536]{1,0:T(8,128)(2,1)S(1)} %get-tuple-element.56), channel_id=1, source_target_pairs={{0,4},{4,8},{8,12},{12,0},{1,5},{5,9},{9,13},{13,1},{2,6},{6,10},{... | collective-permute-start | bytes 147464 | tf_op jit(solution)/shard_map/ppermute | solution.py:20
  28.8 6.7 %collective-permute-start.12 = (bf16[16,1536]{1,0:T(8,128)(2,1)S(1)}, bf16[16,1536]{1,0:T(8,128)(2,1)S(1)}, u32[]{:S(2)}, u32[]{:S(2)}) collective-permute-start(bf16[16,1536]{1,0:T(8,128)(2,1)S(1)} %get-tuple-element.57), channel_id=1, source_target_pairs={{0,8},{4,12},{8,0},{12,4},{1,9},{5,13},{9,1},{13,5},{2,10},{6,14},... | collective-permute-start | bytes 147464 | tf_op jit(solution)/shard_map/ppermute | solution.py:20
  31.2 4.4 %collective-permute-start.13 = (bf16[16,1536]{1,0:T(8,128)(2,1)S(1)}, bf16[16,1536]{1,0:T(8,128)(2,1)S(1)}, u32[]{:S(2)}, u32[]{:S(2)}) collective-permute-start(bf16[16,1536]{1,0:T(8,128)(2,1)S(1)} %get-tuple-element.58), channel_id=1, source_target_pairs={{0,12},{4,0},{8,4},{12,8},{1,13},{5,1},{9,5},{13,9},{2,14},{6,2},{... | collective-permute-start | bytes 147464 | tf_op jit(solution)/shard_map/ppermute | solution.py:20
  36.8 1.7 %collective-permute-start.15 = (bf16[16,2304]{1,0:T(8,128)(2,1)S(1)}, bf16[16,2304]{1,0:T(8,128)(2,1)S(1)}, u32[]{:S(2)}, u32[]{:S(2)}) collective-permute-start(bf16[16,2304]{1,0:T(8,128)(2,1)S(1)} %get-tuple-element.63), channel_id=1, source_target_pairs={{0,1},{1,0},{2,3},{3,2},{4,5},{5,4},{6,7},{7,6},{8,9},{9,8},{10,11... | collective-permute-start | bytes 221192 | tf_op jit(solution)/shard_map/ppermute | solution.py:20
  38.0 1.8 %collective-permute-start.14 = (bf16[16,2304]{1,0:T(8,128)(2,1)S(1)}, bf16[16,2304]{1,0:T(8,128)(2,1)S(1)}, u32[]{:S(2)}, u32[]{:S(2)}) collective-permute-start(bf16[16,2304]{1,0:T(8,128)(2,1)S(1)} %get-tuple-element.61), channel_id=1, source_target_pairs={{0,1},{1,0},{2,3},{3,2},{4,5},{5,4},{6,7},{7,6},{8,9},{9,8},{10,11... | collective-permute-start | bytes 221192 | tf_op jit(solution)/shard_map/ppermute | solution.py:20
  38.6 4.4 %collective-permute-start.19 = (bf16[16,2304]{1,0:T(8,128)(2,1)S(1)}, bf16[16,2304]{1,0:T(8,128)(2,1)S(1)}, u32[]{:S(2)}, u32[]{:S(2)}) collective-permute-start(bf16[16,2304]{1,0:T(8,128)(2,1)S(1)} %pair_sum.3), channel_id=1, source_target_pairs={{0,2},{2,0},{1,3},{3,1},{4,6},{6,4},{5,7},{7,5},{8,10},{10,8},{9,1... | collective-permute-start | bytes 221192 | tf_op jit(solution)/shard_map/ppermute | solution.py:20
  39.8 3.2 %collective-permute-start.16 = (bf16[16,2304]{1,0:T(8,128)(2,1)S(1)}, bf16[16,2304]{1,0:T(8,128)(2,1)S(1)}, u32[]{:S(2)}, u32[]{:S(2)}) collective-permute-start(bf16[16,2304]{1,0:T(8,128)(2,1)S(1)} %get-tuple-element.66), channel_id=1, source_target_pairs={{0,1},{1,0},{2,3},{3,2},{4,5},{5,4},{6,7},{7,6},{8,9},{9,8},{10,11... | collective-permute-start | bytes 221192 | tf_op jit(solution)/shard_map/ppermute | solution.py:20
  39.9 3.1 %collective-permute-start.18 = (bf16[16,2304]{1,0:T(8,128)(2,1)S(1)}, bf16[16,2304]{1,0:T(8,128)(2,1)S(1)}, u32[]{:S(2)}, u32[]{:S(2)}) collective-permute-start(bf16[16,2304]{1,0:T(8,128)(2,1)S(1)} %get-tuple-element.68), channel_id=1, source_target_pairs={{0,1},{1,0},{2,3},{3,2},{4,5},{5,4},{6,7},{7,6},{8,9},{9,8},{10,11... | collective-permute-start | bytes 221192 | tf_op jit(solution)/shard_map/ppermute | solution.py:20
  40.4 4.4 %collective-permute-start.17 = (bf16[16,2304]{1,0:T(8,128)(2,1)S(1)}, bf16[16,2304]{1,0:T(8,128)(2,1)S(1)}, u32[]{:S(2)}, u32[]{:S(2)}) collective-permute-start(bf16[16,2304]{1,0:T(8,128)(2,1)S(1)} %pair_sum.2), channel_id=1, source_target_pairs={{0,2},{2,0},{1,3},{3,1},{4,6},{6,4},{5,7},{7,5},{8,10},{10,8},{9,1... | collective-permute-start | bytes 221192 | tf_op jit(solution)/shard_map/ppermute | solution.py:20

commit v8 on v7

--- a/solution.py
+++ b/solution.py
@@ -321,11 +321,11 @@
     leaving, arrived = [], []
     for term in terms:
         for k in range(1, n_gy):
-            mine = term[k * n_gz : (k + 1) * n_gz]
+            mine = [term[k * n_gz + (j + across()) % n_gz] for j in range(n_gz)]
             mine = [mine[0]] + [shift(mine[j], "gz", j) for j in range(1, n_gz)]
             leaving.append(added(mine, "pair_sum") if n_gz > 1 else mine[0])
     for at, array in enumerate(leaving):
-        arrived.append(shift(array, "gy", at % (n_gy - 1) + 1))
+        arrived.append(hop(array, "gy", at % (n_gy - 1) + 1))
     staying = [term[j] for term in terms for j in range(1, n_gz)]
     if leaving and staying:
         leaving, staying = lax.optimization_barrier((leaving, staying))

time: 45.6 us -> 45.2 us (level)
    ppermute x18 -> x16, waiting for transfers between devices: 13.6 us -> 10.2 us  [shift(): lax.ppermute(array, axis, [(s, (s + by) % size) for s in range(size)])]
    ppermute x2 -> x4, waiting for transfers between devices: 6.38 us -> 9.57 us  [hop(): return lax.ppermute(array, (axis, 'gz'), pairs)]
    ppermute x18 -> x16, starting transfers between devices: 17.2 us -> 15.1 us  [shift(): lax.ppermute(array, axis, [(s, (s + by) % size) for s in range(size)])]
    ppermute x2 -> x4, starting transfers between devices: 0.47 us -> 2.4 us  [hop(): return lax.ppermute(array, (axis, 'gz'), pairs)]
where the time goes in v8:
time: 45.2 us; the launch traced here: 45.1 us
  waiting for transfers between devices  19.7 us (44%)
  starting transfers between devices  17.6 us (39%)
  Pallas kernels  6.7 us (15%)
  local copies, waits for them, and re-layouts  0.95 us (2%)
    ppermute x16, starting transfers between devices, shift(): lax.ppermute(array, axis, [(s, (s + by) % size) for s in range(size)])  15.1 us
    ppermute x16, waiting for transfers between devices, shift(): lax.ppermute(array, axis, [(s, (s + by) % size) for s in range(size)])  10.2 us
    ppermute x4, waiting for transfers between devices, hop(): return lax.ppermute(array, (axis, 'gz'), pairs)  9.57 us
    pallas_call x10, Pallas kernels, call(): pl.pallas_call(body, out_shape=list(outs), in_specs=in_specs, out_specs=[...  6.7 us
    ppermute x4, starting transfers between devices, hop(): return lax.ppermute(array, (axis, 'gz'), pairs)  2.4 us
    unnamed x18, local copies, waits for them, and re-layouts  0.95 us
  transfers between devices with their start and end apart: 20, of which 12 were waited for; matrix products, arithmetic and copies ran while one was open for 0% of the time, Pallas kernels for 3%

profile of v8, /device:TPU:0, one launch (start us, length us, event | category | flops | bytes accessed | tf_op | source)
XLA Modules:
  0.0 45.1 jit_solution(17275116817802305046)
XLA Ops:
  0.0 2.9 %collective-permute-start.1 = (bf16[16,4608]{1,0:T(8,128)(2,1)}, bf16[16,4608]{1,0:T(8,128)(2,1)S(1)}, u32[]{:S(2)}, u32[]{:S(2)}) collective-permute-start(bf16[16,4608]{1,0:T(8,128)(2,1)} %tokens.1), channel_id=1, source_target_pairs={{0,2},{2,0},{1,3},{3,1},{4,6},{6,4},{5,7},{7,5},{8,10},{10,8},{9,1... | collective-permute-start | bytes 442376 | tf_op jit(solution)/shard_map/ppermute | solution.py:20
  2.9 0.5 %collective-permute-start.5 = (s32[4]{0:T(128)}, s32[4]{0:T(128)S(1)}, u32[]{:S(2)}, u32[]{:S(2)}) collective-permute-start(s32[4]{0:T(128)} %refs_0_), channel_id=1, source_target_pairs={{0,1},{1,0},{2,3},{3,2},{4,5},{5,4},{6,7},{7,6},{8,9},{9,8},{10,11... | collective-permute-start | bytes 56 | tf_op jit(solution)/shard_map/ppermute | solution.py:20
  3.5 0.5 %collective-permute-start.4 = (bf16[4,512,256]{2,1,0:T(8,128)(2,1)}, bf16[4,512,256]{2,1,0:T(8,128)(2,1)S(1)}, u32[]{:S(2)}, u32[]{:S(2)}) collective-permute-start(bf16[4,512,256]{2,1,0:T(8,128)(2,1)} %refs_6_), channel_id=1, source_target_pairs={{0,1},{1,0},{2,3},{3,2},{4,5},{5,4},{6,7},{7,6},{8,9},{9,8},{10,11... | collective-permute-start | bytes 3145736 | tf_op jit(solution)/shard_map/ppermute | solution.py:20
  4.0 3.0 %collective-permute-done.1.refs_2_ = bf16[16,4608]{1,0:T(8,128)(2,1)S(1)} collective-permute-done((bf16[16,4608]{1,0:T(8,128)(2,1)}, bf16[16,4608]{1,0:T(8,128)(2,1)S(1)}, u32[]{:S(2)}, u32[]{:S(2)}) %collective-permute-start.1) | collective-permute-done | bytes 147488 | tf_op jit(solution)/shard_map/ppermute | solution.py:20
  7.0 0.9 %copy-done.4 = bf16[16,4608]{1,0:T(8,128)(2,1)S(1)} copy-done((bf16[16,4608]{1,0:T(8,128)(2,1)S(1)}, bf16[16,4608]{1,0:T(8,128)(2,1)}, u32[]{:S(2)}) %copy-start.4) | copy-done | bytes 147480
  8.1 0.3 collective-permute-done.2.refs_3_
  8.4 2.0 %query_terms.1 = (bf16[16,1536]{1,0:T(8,128)(2,1)S(1)}, bf16[16,1536]{1,0:T(8,128)(2,1)S(1)}, bf16[16,1536]{1,0:T(8,128)(2,1)S(1)}, bf16[16,1536]{1,0:T(8,128)(2,1)S(1)}) custom-call(bf16[16,4608]{1,0:T(8,128)(2,1)S(1)} %own_tokens.1.refs_0_, bf16[16,4608]{1,0:T(8,128)(2,1)S(1)} %collective-permute-done.refs_1_, ...), custom_call_target="tpu_custom_call" | custom-call | flops 905969664 | bytes 14942208 | tf_op jit(solution)/shard_map/query_terms/pallas_call | solution.py:54
  10.4 1.9 %collective-permute-start.6 = (bf16[16,1536]{1,0:T(8,128)(2,1)S(1)}, bf16[16,1536]{1,0:T(8,128)(2,1)S(1)}, u32[]{:S(2)}, u32[]{:S(2)}) collective-permute-start(bf16[16,1536]{1,0:T(8,128)(2,1)S(1)} %get-tuple-element.44), channel_id=1, source_target_pairs={{0,4},{4,8},{8,12},{12,0},{1,5},{5,9},{9,13},{13,1},{2,6},{6,10},{... | collective-permute-start | bytes 147464 | tf_op jit(solution)/shard_map/ppermute | solution.py:20
  12.3 2.6 %collective-permute-start.7 = (bf16[16,1536]{1,0:T(8,128)(2,1)S(1)}, bf16[16,1536]{1,0:T(8,128)(2,1)S(1)}, u32[]{:S(2)}, u32[]{:S(2)}) collective-permute-start(bf16[16,1536]{1,0:T(8,128)(2,1)S(1)} %get-tuple-element.45), channel_id=1, source_target_pairs={{0,8},{4,12},{8,0},{12,4},{1,9},{5,13},{9,1},{13,5},{2,10},{6,14},... | collective-permute-start | bytes 147464 | tf_op jit(solution)/shard_map/ppermute | solution.py:20
  14.9 1.3 %collective-permute-start.8 = (bf16[16,1536]{1,0:T(8,128)(2,1)S(1)}, bf16[16,1536]{1,0:T(8,128)(2,1)S(1)}, u32[]{:S(2)}, u32[]{:S(2)}) collective-permute-start(bf16[16,1536]{1,0:T(8,128)(2,1)S(1)} %get-tuple-element.46), channel_id=1, source_target_pairs={{0,12},{4,0},{8,4},{12,8},{1,13},{5,1},{9,5},{13,9},{2,14},{6,2},{... | collective-permute-start | bytes 147464 | tf_op jit(solution)/shard_map/ppermute | solution.py:20
  16.3 0.3 collective-permute-done.6.refs_1_
  16.6 2.3 %collective-permute-done.7.refs_2_ = bf16[16,1536]{1,0:T(8,128)(2,1)S(1)} collective-permute-done((bf16[16,1536]{1,0:T(8,128)(2,1)S(1)}, bf16[16,1536]{1,0:T(8,128)(2,1)S(1)}, u32[]{:S(2)}, u32[]{:S(2)}) %collective-permute-start.7) | collective-permute-done | bytes 49184 | tf_op jit(solution)/shard_map/ppermute | solution.py:20
  18.9 0.3 collective-permute-done.8.refs_3_
  19.3 0.3 collective-permute-start.9
  19.6 3.2 %collective-permute-done.9.refs_3_ = bf16[2,4,1536]{2,1,0:T(4,128)(2,1)S(1)} collective-permute-done((bf16[2,4,1536]{2,1,0:T(4,128)(2,1)S(1)}, bf16[2,4,1536]{2,1,0:T(4,128)(2,1)S(1)}, u32[]{:S(2)}, u32[]{:S(2)}) %collective-permute-start.9) | collective-permute-done | bytes 24608 | tf_op jit(solution)/shard_map/ppermute | solution.py:32
  22.8 1.5 %attention.1 = (bf16[2,4,1536]{2,1,0:T(4,128)(2,1)S(1)}, bf16[2,4,1536]{2,1,0:T(4,128)(2,1)S(1)}) custom-call(s32[4]{0:T(128)S(1)} %copy-done.3, s32[4]{0:T(128)S(1)} %collective-permute-done.5.refs_1_, bf16[2,4,1536]{2,1,0:T(4,128)(2,1)S(1)} %get-tuple-element.47.refs_2_, bf16[2,4,1536]{2,1,0:T(4,128)(2,1)S(1)} %collective-permute-done.9.refs_3_, ...), custom_call_target="tpu_custom_call" | custom-call | bytes 4292640 | tf_op jit(solution)/shard_map/attention/pallas_call | solution.py:54
  24.5 3.2 %collective-permute-done.10.refs_1_ = bf16[2,4,1536]{2,1,0:T(4,128)(2,1)S(1)} collective-permute-done((bf16[2,4,1536]{2,1,0:T(4,128)(2,1)S(1)}, bf16[2,4,1536]{2,1,0:T(4,128)(2,1)S(1)}, u32[]{:S(2)}, u32[]{:S(2)}) %collective-permute-start.10) | collective-permute-done | bytes 24608 | tf_op jit(solution)/shard_map/ppermute | solution.py:32
  27.7 1.1 %collective-permute-start.11 = (bf16[16,1536]{1,0:T(8,128)(2,1)S(1)}, bf16[16,1536]{1,0:T(8,128)(2,1)S(1)}, u32[]{:S(2)}, u32[]{:S(2)}) collective-permute-start(bf16[16,1536]{1,0:T(8,128)(2,1)S(1)} %get-tuple-element.56), channel_id=1, source_target_pairs={{0,4},{4,8},{8,12},{12,0},{1,5},{5,9},{9,13},{13,1},{2,6},{6,10},{... | collective-permute-start | bytes 147464 | tf_op jit(solution)/shard_map/ppermute | solution.py:20
  28.8 2.5 %collective-permute-start.12 = (bf16[16,1536]{1,0:T(8,128)(2,1)S(1)}, bf16[16,1536]{1,0:T(8,128)(2,1)S(1)}, u32[]{:S(2)}, u32[]{:S(2)}) collective-permute-start(bf16[16,1536]{1,0:T(8,128)(2,1)S(1)} %get-tuple-element.57), channel_id=1, source_target_pairs={{0,8},{4,12},{8,0},{12,4},{1,9},{5,13},{9,1},{13,5},{2,10},{6,14},... | collective-permute-start | bytes 147464 | tf_op jit(solution)/shard_map/ppermute | solution.py:20
  31.2 0.6 %collective-permute-start.13 = (bf16[16,1536]{1,0:T(8,128)(2,1)S(1)}, bf16[16,1536]{1,0:T(8,128)(2,1)S(1)}, u32[]{:S(2)}, u32[]{:S(2)}) collective-permute-start(bf16[16,1536]{1,0:T(8,128)(2,1)S(1)} %get-tuple-element.58), channel_id=1, source_target_pairs={{0,12},{4,0},{8,4},{12,8},{1,13},{5,1},{9,5},{13,9},{2,14},{6,2},{... | collective-permute-start | bytes 147464 | tf_op jit(solution)/shard_map/ppermute | solution.py:20
  31.8 2.4 %collective-permute-done.11.refs_1_ = bf16[16,1536]{1,0:T(8,128)(2,1)S(1)} collective-permute-done((bf16[16,1536]{1,0:T(8,128)(2,1)S(1)}, bf16[16,1536]{1,0:T(8,128)(2,1)S(1)}, u32[]{:S(2)}, u32[]{:S(2)}) %collective-permute-start.11) | collective-permute-done | bytes 49184 | tf_op jit(solution)/shard_map/ppermute | solution.py:20
  34.3 1.2 %collective-permute-done.12.refs_2_ = bf16[16,1536]{1,0:T(8,128)(2,1)S(1)} collective-permute-done((bf16[16,1536]{1,0:T(8,128)(2,1)S(1)}, bf16[16,1536]{1,0:T(8,128)(2,1)S(1)}, u32[]{:S(2)}, u32[]{:S(2)}) %collective-permute-start.12) | collective-permute-done | bytes 49184 | tf_op jit(solution)/shard_map/ppermute | solution.py:20
  35.5 0.2 collective-permute-done.13.refs_3_
  35.7 1.1 %output_terms.3 = (bf16[16,2304]{1,0:T(8,128)(2,1)S(1)}, bf16[16,2304]{1,0:T(8,128)(2,1)S(1)}, bf16[16,2304]{1,0:T(8,128)(2,1)S(1)}, bf16[16,2304]{1,0:T(8,128)(2,1)S(1)}) custom-call(bf16[16,1536]{1,0:T(8,128)(2,1)S(1)} %get-tuple-element.55.refs_0_, bf16[16,1536]{1,0:T(8,128)(2,1)S(1)} %collective-permute-done.11.refs_1_, ...), custom_call_target="tpu_custom_call" | custom-call | flops 905969664 | bytes 14647296 | tf_op jit(solution)/shard_map/output_terms/pallas_call | solution.py:54
  36.9 1.1 %output_terms.2 = (bf16[16,2304]{1,0:T(8,128)(2,1)S(1)}, bf16[16,2304]{1,0:T(8,128)(2,1)S(1)}, bf16[16,2304]{1,0:T(8,128)(2,1)S(1)}, bf16[16,2304]{1,0:T(8,128)(2,1)S(1)}) custom-call(bf16[16,1536]{1,0:T(8,128)(2,1)S(1)} %get-tuple-element.55.refs_0_, bf16[16,1536]{1,0:T(8,128)(2,1)S(1)} %collective-permute-done.11.refs_1_, ...), custom_call_target="tpu_custom_call" | custom-call | flops 905969664 | bytes 14647296 | tf_op jit(solution)/shard_map/output_terms/pallas_call | solution.py:54
  38.0 0.6 %collective-permute-start.14 = (bf16[16,2304]{1,0:T(8,128)(2,1)S(1)}, bf16[16,2304]{1,0:T(8,128)(2,1)S(1)}, u32[]{:S(2)}, u32[]{:S(2)}) collective-permute-start(bf16[16,2304]{1,0:T(8,128)(2,1)S(1)} %get-tuple-element.61), channel_id=1, source_target_pairs={{0,1},{1,0},{2,3},{3,2},{4,5},{5,4},{6,7},{7,6},{8,9},{9,8},{10,11... | collective-permute-start | bytes 221192 | tf_op jit(solution)/shard_map/ppermute | solution.py:20
  38.6 0.8 %collective-permute-start.19 = (bf16[16,2304]{1,0:T(8,128)(2,1)S(1)}, bf16[16,2304]{1,0:T(8,128)(2,1)S(1)}, u32[]{:S(2)}, u32[]{:S(2)}) collective-permute-start(bf16[16,2304]{1,0:T(8,128)(2,1)S(1)} %pair_sum.3), channel_id=1, source_target_pairs={{0,3},{1,2},{2,1},{3,0},{4,7},{5,6},{6,5},{7,4},{8,11},{9,10},{10,... | collective-permute-start | bytes 221192 | tf_op jit(solution)/shard_map/ppermute | solution.py:32
  39.5 0.5 %collective-permute-start.16 = (bf16[16,2304]{1,0:T(8,128)(2,1)S(1)}, bf16[16,2304]{1,0:T(8,128)(2,1)S(1)}, u32[]{:S(2)}, u32[]{:S(2)}) collective-permute-start(bf16[16,2304]{1,0:T(8,128)(2,1)S(1)} %get-tuple-element.66), channel_id=1, source_target_pairs={{0,1},{1,0},{2,3},{3,2},{4,5},{5,4},{6,7},{7,6},{8,9},{9,8},{10,11... | collective-permute-start | bytes 221192 | tf_op jit(solution)/shard_map/ppermute | solution.py:20
  40.1 1.1 %collective-permute-start.17 = (bf16[16,2304]{1,0:T(8,128)(2,1)S(1)}, bf16[16,2304]{1,0:T(8,128)(2,1)S(1)}, u32[]{:S(2)}, u32[]{:S(2)}) collective-permute-start(bf16[16,2304]{1,0:T(8,128)(2,1)S(1)} %pair_sum.2), channel_id=1, source_target_pairs={{0,3},{1,2},{2,1},{3,0},{4,7},{5,6},{6,5},{7,4},{8,11},{9,10},{10,... | collective-permute-start | bytes 221192 | tf_op jit(solution)/shard_map/ppermute | solution.py:32
  41.2 1.8 %collective-permute-done.19.refs_5_ = bf16[16,2304]{1,0:T(8,128)(2,1)S(1)} collective-permute-done((bf16[16,2304]{1,0:T(8,128)(2,1)S(1)}, bf16[16,2304]{1,0:T(8,128)(2,1)S(1)}, u32[]{:S(2)}, u32[]{:S(2)}) %collective-permute-start.19) | collective-permute-done | bytes 73760 | tf_op jit(solution)/shard_map/ppermute | solution.py:32
  43.0 1.4 %collective-permute-done.17.refs_2_ = bf16[16,2304]{1,0:T(8,128)(2,1)S(1)} collective-permute-done((bf16[16,2304]{1,0:T(8,128)(2,1)S(1)}, bf16[16,2304]{1,0:T(8,128)(2,1)S(1)}, u32[]{:S(2)}, u32[]{:S(2)}) %collective-permute-start.17) | collective-permute-done | bytes 73760 | tf_op jit(solution)/shard_map/ppermute | solution.py:32
  44.4 0.7 %output_sum.1 = bf16[16,4608]{1,0:T(8,128)(2,1)} custom-call(bf16[16,2304]{1,0:T(8,128)(2,1)S(1)} %get-tuple-element.59.refs_0_, bf16[16,2304]{1,0:T(8,128)(2,1)S(1)} %collective-permute-done.16.refs_1_, bf16[16,2304]{1,0:T(8,128)(2,1)S(1)} %collective-permute-done.17.refs_2_, bf16[16,2304]{1,0:T(8,128)(2,1)S(1)} %get-tuple-element.67.refs_3_, ...), custom_call_target="tpu_custom_call" | custom-call | bytes 589824 | tf_op jit(solution)/shard_map/output_sum/pallas_call | solution.py:54
  (37 shorter events, 0.7 us)
Async XLA Ops:
  0.0 8.4 %copy-start = (bf16[4608,1536]{1,0:T(8,128)(2,1)S(1)}, bf16[4608,1536]{1,0:T(8,128)(2,1)}, u32[]{:S(2)}) copy-start(bf16[4608,1536]{1,0:T(8,128)(2,1)} %refs_4_.3) | copy-start | bytes 42467332
  0.0 7.0 %collective-permute-start.1 = (bf16[16,4608]{1,0:T(8,128)(2,1)}, bf16[16,4608]{1,0:T(8,128)(2,1)S(1)}, u32[]{:S(2)}, u32[]{:S(2)}) collective-permute-start(bf16[16,4608]{1,0:T(8,128)(2,1)} %tokens.1), channel_id=1, source_target_pairs={{0,2},{2,0},{1,3},{3,1},{4,6},{6,4},{5,7},{7,5},{8,10},{10,8},{9,1... | collective-permute-start | bytes 442376 | tf_op jit(solution)/shard_map/ppermute | solution.py:20
  2.9 5.2 %collective-permute-start = (bf16[16,4608]{1,0:T(8,128)(2,1)}, bf16[16,4608]{1,0:T(8,128)(2,1)S(1)}, u32[]{:S(2)}, u32[]{:S(2)}) collective-permute-start(bf16[16,4608]{1,0:T(8,128)(2,1)} %tokens.1), channel_id=1, source_target_pairs={{0,1},{1,0},{2,3},{3,2},{4,5},{5,4},{6,7},{7,6},{8,9},{9,8},{10,11... | collective-permute-start | bytes 442376 | tf_op jit(solution)/shard_map/ppermute | solution.py:20
  2.9 5.1 %collective-permute-start.5 = (s32[4]{0:T(128)}, s32[4]{0:T(128)S(1)}, u32[]{:S(2)}, u32[]{:S(2)}) collective-permute-start(s32[4]{0:T(128)} %refs_0_), channel_id=1, source_target_pairs={{0,1},{1,0},{2,3},{3,2},{4,5},{5,4},{6,7},{7,6},{8,9},{9,8},{10,11... | collective-permute-start | bytes 56 | tf_op jit(solution)/shard_map/ppermute | solution.py:20
  3.5 4.9 %collective-permute-start.3 = (bf16[4,512,256]{2,1,0:T(8,128)(2,1)}, bf16[4,512,256]{2,1,0:T(8,128)(2,1)S(1)}, u32[]{:S(2)}, u32[]{:S(2)}) collective-permute-start(bf16[4,512,256]{2,1,0:T(8,128)(2,1)} %refs_4_.4), channel_id=1, source_target_pairs={{0,1},{1,0},{2,3},{3,2},{4,5},{5,4},{6,7},{7,6},{8,9},{9,8},{10,11... | collective-permute-start | bytes 3145736 | tf_op jit(solution)/shard_map/ppermute | solution.py:20
  3.5 4.9 %collective-permute-start.4 = (bf16[4,512,256]{2,1,0:T(8,128)(2,1)}, bf16[4,512,256]{2,1,0:T(8,128)(2,1)S(1)}, u32[]{:S(2)}, u32[]{:S(2)}) collective-permute-start(bf16[4,512,256]{2,1,0:T(8,128)(2,1)} %refs_6_), channel_id=1, source_target_pairs={{0,1},{1,0},{2,3},{3,2},{4,5},{5,4},{6,7},{7,6},{8,9},{9,8},{10,11... | collective-permute-start | bytes 3145736 | tf_op jit(solution)/shard_map/ppermute | solution.py:20
  7.0 1.4 %collective-permute-start.2 = (bf16[16,4608]{1,0:T(8,128)(2,1)S(1)}, bf16[16,4608]{1,0:T(8,128)(2,1)S(1)}, u32[]{:S(2)}, u32[]{:S(2)}) collective-permute-start(bf16[16,4608]{1,0:T(8,128)(2,1)S(1)} %collective-permute-done.1.refs_2_), channel_id=1, source_target_pairs={{0,1},{1,0},{2,3},{3,2},{4,5},{5,4},{6,7},{7,6},{8,9},{9,8},{10,11... | collective-permute-start | bytes 442376 | tf_op jit(solution)/shard_map/ppermute | solution.py:20
  7.0 0.9 %copy-start.4 = (bf16[16,4608]{1,0:T(8,128)(2,1)S(1)}, bf16[16,4608]{1,0:T(8,128)(2,1)}, u32[]{:S(2)}) copy-start(bf16[16,4608]{1,0:T(8,128)(2,1)} %tokens.1) | copy-start | bytes 442372
  8.4 27.3 %slice-start = ((s8[14155776]{0:T(1024)(128)(4,1)}), s8[1572864]{0:T(1024)(128)(4,1)S(1)}, s32[]{:S(2)}) async-start(s8[14155776]{0:T(1024)(128)(4,1)} %bitcast), calls=%async_computation | async-start | bytes 3145728
  8.4 27.3 %slice-start.1 = ((s8[14155776]{0:T(1024)(128)(4,1)}), s8[4194304]{0:T(1024)(128)(4,1)S(1)}, s32[]{:S(2)}) async-start(s8[14155776]{0:T(1024)(128)(4,1)} %bitcast), calls=%async_computation.1 | async-start | bytes 8388608
  10.4 6.2 %collective-permute-start.6 = (bf16[16,1536]{1,0:T(8,128)(2,1)S(1)}, bf16[16,1536]{1,0:T(8,128)(2,1)S(1)}, u32[]{:S(2)}, u32[]{:S(2)}) collective-permute-start(bf16[16,1536]{1,0:T(8,128)(2,1)S(1)} %get-tuple-element.44), channel_id=1, source_target_pairs={{0,4},{4,8},{8,12},{12,0},{1,5},{5,9},{9,13},{13,1},{2,6},{6,10},{... | collective-permute-start | bytes 147464 | tf_op jit(solution)/shard_map/ppermute | solution.py:20
  12.3 6.6 %collective-permute-start.7 = (bf16[16,1536]{1,0:T(8,128)(2,1)S(1)}, bf16[16,1536]{1,0:T(8,128)(2,1)S(1)}, u32[]{:S(2)}, u32[]{:S(2)}) collective-permute-start(bf16[16,1536]{1,0:T(8,128)(2,1)S(1)} %get-tuple-element.45), channel_id=1, source_target_pairs={{0,8},{4,12},{8,0},{12,4},{1,9},{5,13},{9,1},{13,5},{2,10},{6,14},... | collective-permute-start | bytes 147464 | tf_op jit(solution)/shard_map/ppermute | solution.py:20
  14.9 4.3 %collective-permute-start.8 = (bf16[16,1536]{1,0:T(8,128)(2,1)S(1)}, bf16[16,1536]{1,0:T(8,128)(2,1)S(1)}, u32[]{:S(2)}, u32[]{:S(2)}) collective-permute-start(bf16[16,1536]{1,0:T(8,128)(2,1)S(1)} %get-tuple-element.46), channel_id=1, source_target_pairs={{0,12},{4,0},{8,4},{12,8},{1,13},{5,1},{9,5},{13,9},{2,14},{6,2},{... | collective-permute-start | bytes 147464 | tf_op jit(solution)/shard_map/ppermute | solution.py:20
  19.2 3.6 %copy-start.1 = (bf16[4,512,256]{2,1,0:T(8,128)(2,1)S(1)}, bf16[4,512,256]{2,1,0:T(8,128)(2,1)}, u32[]{:S(2)}) copy-start(bf16[4,512,256]{2,1,0:T(8,128)(2,1)} %refs_4_.4) | copy-start | bytes 3145732
  19.2 3.6 %copy-start.2 = (bf16[4,512,256]{2,1,0:T(8,128)(2,1)S(1)}, bf16[4,512,256]{2,1,0:T(8,128)(2,1)}, u32[]{:S(2)}) copy-start(bf16[4,512,256]{2,1,0:T(8,128)(2,1)} %refs_6_) | copy-start | bytes 3145732
  19.2 3.6 %copy-start.3 = (s32[4]{0:T(128)S(1)}, s32[4]{0:T(128)}, u32[]{:S(2)}) copy-start(s32[4]{0:T(128)} %refs_0_) | copy-start | bytes 52
  19.2 16.5 %slice-start.2 = ((s8[14155776]{0:T(1024)(128)(4,1)}), s8[4194304]{0:T(1024)(128)(4,1)S(1)}, s32[]{:S(2)}) async-start(s8[14155776]{0:T(1024)(128)(4,1)} %bitcast), calls=%async_computation.2 | async-start | bytes 8388608
  19.2 16.5 %slice-start.3 = ((s8[14155776]{0:T(1024)(128)(4,1)}), s8[4194304]{0:T(1024)(128)(4,1)S(1)}, s32[]{:S(2)}) async-start(s8[14155776]{0:T(1024)(128)(4,1)} %bitcast), calls=%async_computation.3 | async-start | bytes 8388608
  19.3 3.5 %collective-permute-start.9 = (bf16[2,4,1536]{2,1,0:T(4,128)(2,1)S(1)}, bf16[2,4,1536]{2,1,0:T(4,128)(2,1)S(1)}, u32[]{:S(2)}, u32[]{:S(2)}) collective-permute-start(bf16[2,4,1536]{2,1,0:T(4,128)(2,1)S(1)} %get-tuple-element.48), channel_id=1, source_target_pairs={{0,3},{1,2},{2,1},{3,0},{4,7},{5,6},{6,5},{7,4},{8,11},{9,10},{10,... | collective-permute-start | bytes 73736 | tf_op jit(solution)/shard_map/ppermute | solution.py:32
  24.3 3.3 %collective-permute-start.10 = (bf16[2,4,1536]{2,1,0:T(4,128)(2,1)S(1)}, bf16[2,4,1536]{2,1,0:T(4,128)(2,1)S(1)}, u32[]{:S(2)}, u32[]{:S(2)}) collective-permute-start(bf16[2,4,1536]{2,1,0:T(4,128)(2,1)S(1)} %get-tuple-element.54), channel_id=1, source_target_pairs={{0,3},{1,2},{2,1},{3,0},{4,7},{5,6},{6,5},{7,4},{8,11},{9,10},{10,... | collective-permute-start | bytes 73736 | tf_op jit(solution)/shard_map/ppermute | solution.py:32
  27.7 6.6 %collective-permute-start.11 = (bf16[16,1536]{1,0:T(8,128)(2,1)S(1)}, bf16[16,1536]{1,0:T(8,128)(2,1)S(1)}, u32[]{:S(2)}, u32[]{:S(2)}) collective-permute-start(bf16[16,1536]{1,0:T(8,128)(2,1)S(1)} %get-tuple-element.56), channel_id=1, source_target_pairs={{0,4},{4,8},{8,12},{12,0},{1,5},{5,9},{9,13},{13,1},{2,6},{6,10},{... | collective-permute-start | bytes 147464 | tf_op jit(solution)/shard_map/ppermute | solution.py:20
  28.8 6.7 %collective-permute-start.12 = (bf16[16,1536]{1,0:T(8,128)(2,1)S(1)}, bf16[16,1536]{1,0:T(8,128)(2,1)S(1)}, u32[]{:S(2)}, u32[]{:S(2)}) collective-permute-start(bf16[16,1536]{1,0:T(8,128)(2,1)S(1)} %get-tuple-element.57), channel_id=1, source_target_pairs={{0,8},{4,12},{8,0},{12,4},{1,9},{5,13},{9,1},{13,5},{2,10},{6,14},... | collective-permute-start | bytes 147464 | tf_op jit(solution)/shard_map/ppermute | solution.py:20
  31.2 4.4 %collective-permute-start.13 = (bf16[16,1536]{1,0:T(8,128)(2,1)S(1)}, bf16[16,1536]{1,0:T(8,128)(2,1)S(1)}, u32[]{:S(2)}, u32[]{:S(2)}) collective-permute-start(bf16[16,1536]{1,0:T(8,128)(2,1)S(1)} %get-tuple-element.58), channel_id=1, source_target_pairs={{0,12},{4,0},{8,4},{12,8},{1,13},{5,1},{9,5},{13,9},{2,14},{6,2},{... | collective-permute-start | bytes 147464 | tf_op jit(solution)/shard_map/ppermute | solution.py:20
  36.8 1.7 %collective-permute-start.15 = (bf16[16,2304]{1,0:T(8,128)(2,1)S(1)}, bf16[16,2304]{1,0:T(8,128)(2,1)S(1)}, u32[]{:S(2)}, u32[]{:S(2)}) collective-permute-start(bf16[16,2304]{1,0:T(8,128)(2,1)S(1)} %get-tuple-element.63), channel_id=1, source_target_pairs={{0,1},{1,0},{2,3},{3,2},{4,5},{5,4},{6,7},{7,6},{8,9},{9,8},{10,11... | collective-permute-start | bytes 221192 | tf_op jit(solution)/shard_map/ppermute | solution.py:20
  38.0 1.5 %collective-permute-start.14 = (bf16[16,2304]{1,0:T(8,128)(2,1)S(1)}, bf16[16,2304]{1,0:T(8,128)(2,1)S(1)}, u32[]{:S(2)}, u32[]{:S(2)}) collective-permute-start(bf16[16,2304]{1,0:T(8,128)(2,1)S(1)} %get-tuple-element.61), channel_id=1, source_target_pairs={{0,1},{1,0},{2,3},{3,2},{4,5},{5,4},{6,7},{7,6},{8,9},{9,8},{10,11... | collective-permute-start | bytes 221192 | tf_op jit(solution)/shard_map/ppermute | solution.py:20
  38.6 4.4 %collective-permute-start.19 = (bf16[16,2304]{1,0:T(8,128)(2,1)S(1)}, bf16[16,2304]{1,0:T(8,128)(2,1)S(1)}, u32[]{:S(2)}, u32[]{:S(2)}) collective-permute-start(bf16[16,2304]{1,0:T(8,128)(2,1)S(1)} %pair_sum.3), channel_id=1, source_target_pairs={{0,3},{1,2},{2,1},{3,0},{4,7},{5,6},{6,5},{7,4},{8,11},{9,10},{10,... | collective-permute-start | bytes 221192 | tf_op jit(solution)/shard_map/ppermute | solution.py:32
  39.5 3.5 %collective-permute-start.16 = (bf16[16,2304]{1,0:T(8,128)(2,1)S(1)}, bf16[16,2304]{1,0:T(8,128)(2,1)S(1)}, u32[]{:S(2)}, u32[]{:S(2)}) collective-permute-start(bf16[16,2304]{1,0:T(8,128)(2,1)S(1)} %get-tuple-element.66), channel_id=1, source_target_pairs={{0,1},{1,0},{2,3},{3,2},{4,5},{5,4},{6,7},{7,6},{8,9},{9,8},{10,11... | collective-permute-start | bytes 221192 | tf_op jit(solution)/shard_map/ppermute | solution.py:20
  40.0 3.0 %collective-permute-start.18 = (bf16[16,2304]{1,0:T(8,128)(2,1)S(1)}, bf16[16,2304]{1,0:T(8,128)(2,1)S(1)}, u32[]{:S(2)}, u32[]{:S(2)}) collective-permute-start(bf16[16,2304]{1,0:T(8,128)(2,1)S(1)} %get-tuple-element.68), channel_id=1, source_target_pairs={{0,1},{1,0},{2,3},{3,2},{4,5},{5,4},{6,7},{7,6},{8,9},{9,8},{10,11... | collective-permute-start | bytes 221192 | tf_op jit(solution)/shard_map/ppermute | solution.py:20
  40.1 4.3 %collective-permute-start.17 = (bf16[16,2304]{1,0:T(8,128)(2,1)S(1)}, bf16[16,2304]{1,0:T(8,128)(2,1)S(1)}, u32[]{:S(2)}, u32[]{:S(2)}) collective-permute-start(bf16[16,2304]{1,0:T(8,128)(2,1)S(1)} %pair_sum.2), channel_id=1, source_target_pairs={{0,3},{1,2},{2,1},{3,0},{4,7},{5,6},{6,5},{7,4},{8,11},{9,10},{10,... | collective-permute-start | bytes 221192 | tf_op jit(solution)/shard_map/ppermute | solution.py:32
